TPU v7x, 128 devices: a whole 4x4x4 slice. The times are simulated.
128 devices in a mesh: dp: 16 (over x, y), row: 2 (over z_hi), col: 4 (over z_lo, core).
Axes of the slice: x: 4, y: 4, z: 4 (z_hi: 2, z_lo: 2; z = z_hi * 2 + z_lo), core: 2. Of those that a mesh axis runs over, the one named last changes fastest.
Arguments:
- act_in: bfloat16 [16384, 768], P(('dp', 'col'), 'row'), may hold values from -6 to 6
- cotangent: bfloat16 [16384, 768], P(('dp', 'col'), 'row'), may hold values from -6 to 6
- lengths: int32 [16], P('dp'), may hold values from 769 to 1024, as said below
- w_qkv: bfloat16 [2, 768, 3, 768], P(None, 'row', None, 'col'), may hold values from -0.21875 to 0.21875
- bias_qv: bfloat16 [2, 2, 768], P(None, None, 'col'), may hold values from -0.75 to 0.75
- w_out: bfloat16 [2, 768, 768], P(None, 'col', 'row'), may hold values from -4 to 4
- bias_out: bfloat16 [2, 768], P(None, 'row'), may hold values from -4 to 4
- w_up: bfloat16 [2, 768, 3072], P(None, 'row', 'col'), may hold values from -0.21875 to 0.21875
- bias_up: bfloat16 [2, 3072], P(None, 'col'), may hold values from -4 to 4
- w_down: bfloat16 [2, 3072, 768], P(None, 'col', 'row'), may hold values from -0.109375 to 0.109375
- bias_down: bfloat16 [2, 768], P(None, 'row'), may hold values from -4 to 4
- ln_gain: bfloat16 [2, 2, 768], P(None, None, 'row'), may hold values from 0.3 to 2
- ln_shift: bfloat16 [2, 2, 768], P(None, None, 'row'), may hold values from -4 to 4
Outputs:
- out_act: bfloat16 [16384, 768], P(('dp', 'col'), 'row')
- grad_in: float32 [16384, 768], P(('dp', 'col'), 'row')
- grad_qkv: float32 [2, 768, 3, 768], P(None, 'row', None, 'col')
- grad_bias_qv: float32 [2, 2, 768], P(None, None, 'col')
- grad_out_proj: float32 [2, 768, 768], P(None, 'col', 'row')
- grad_out_bias: float32 [2, 768], P(None, 'row')
- grad_up: float32 [2, 768, 3072], P(None, 'row', 'col')
- grad_up_bias: float32 [2, 3072], P(None, 'col')
- grad_down: float32 [2, 3072, 768], P(None, 'col', 'row')
- grad_down_bias: float32 [2, 768], P(None, 'row')
- grad_gain: float32 [2, 2, 768], P(None, None, 'row')
- grad_shift: float32 [2, 2, 768], P(None, None, 'row')
Inputs may be any that keep to these rules, and one draw needn't show every extreme that they name: `lengths`: each group's valid tokens form one sequence at the start of its buffer; at least one group in every draw is completely filled.
All inputs are finite; a program needn't handle non-finite values.
Results may differ from a plain program's by a relative error of at most 0.013.
Values may be sent and summed in bfloat16 or wider, within the bound.
No kernel may reach another device: no remote copies, remote signals or barrier semaphores. Data moves between devices by JAX's collectives and lax.ppermute only.
A program may use at most 128 MiB of HBM per device.

v0:
```python
import jax
import jax.numpy as jnp
from jax import lax
from jax.sharding import PartitionSpec as P

HDIM = 64
LAYERS = 2


EPSILON = 1e-05
MASKED = -1000000000.0


def gather_cols(value):
    return lax.all_gather(value, "col", axis=0, tiled=True)


def gather_rows(value):
    return lax.all_gather(value, "row", axis=0, tiled=True)


def gather_keys(value):
    return lax.all_gather(value, "row", axis=0, tiled=True)


def back_gather_cols(value):
    return lax.all_gather(value, "col", axis=0, tiled=True)


def back_gather_rows(value):
    return lax.all_gather(value, "row", axis=0, tiled=True)


def sum_rows(left, right, form, local_rows):

    def term(start, count):
        return jnp.einsum(form, left, right, preferred_element_type=jnp.float32)

    return lax.psum_scatter(
        term(jnp.int32(0), lax.axis_size("row") * local_rows),
        "row",
        scatter_dimension=0,
        tiled=True,
    )


def sum_cols(left, right, form, local_rows):

    def term(start, count):
        return jnp.einsum(form, left, right, preferred_element_type=jnp.float32)

    return lax.psum_scatter(
        term(jnp.int32(0), lax.axis_size("col") * local_rows),
        "col",
        scatter_dimension=0,
        tiled=True,
    )


def back_sum_rows(left, right, form, local_rows):

    def term(start, count):
        return jnp.einsum(form, left, right, preferred_element_type=jnp.float32)

    return lax.psum_scatter(
        term(jnp.int32(0), lax.axis_size("row") * local_rows),
        "row",
        scatter_dimension=0,
        tiled=True,
    )


def back_sum_cols(left, right, form, local_rows):

    def term(start, count):
        return jnp.einsum(form, left, right, preferred_element_type=jnp.float32)

    return lax.psum_scatter(
        term(jnp.int32(0), lax.axis_size("col") * local_rows),
        "col",
        scatter_dimension=0,
        tiled=True,
    )


def norm_forward(resid, gain, shift, width):
    totals, squares = lax.psum((jnp.sum(resid, 1), jnp.sum(resid * resid, 1)), "row")
    mean = totals / width
    inverse = lax.rsqrt(squares / width - mean * mean + EPSILON)
    unit = (resid - mean[:, None]) * inverse[:, None]
    return (unit * gain + shift, unit, inverse)


def norm_backward(grad, unit, inverse, gain, width):
    scaled = grad * gain
    first, second = lax.psum((jnp.sum(scaled, 1), jnp.sum(scaled * unit, 1)), "row")
    resid_grad = inverse[:, None] * (
        scaled - first[:, None] / width - unit * (second[:, None] / width)
    )
    return (resid_grad, jnp.sum(grad * unit, 0), jnp.sum(grad, 0))


def attend_forward(query, keys, values, key_ok):
    query_rows, head_count, head_depth = query.shape
    block_rows = min(512, query_rows)

    def single_block(query_block):
        scores = (
            jnp.einsum("qhd,khd->hqk", query_block, keys, preferred_element_type=jnp.float32)
            * 0.125
        )
        scores = jnp.where(key_ok[None, None, :], scores, MASKED)
        peak = jnp.max(scores, axis=2, keepdims=True)
        raised = jnp.exp(scores - peak)
        denominator = jnp.sum(raised, axis=2, keepdims=True)
        probs_low = (raised / denominator).astype(jnp.bfloat16)
        mixture = jnp.einsum("hqk,khd->qhd", probs_low, values, preferred_element_type=jnp.float32)
        return (mixture, peak[..., 0] + jnp.log(denominator[..., 0]))

    blocks = query.reshape(query_rows // block_rows, block_rows, head_count, head_depth)
    mixture, logsum = lax.map(single_block, blocks)
    return (mixture.reshape(query_rows, head_count * head_depth), logsum)


def attend_backward(query, keys, values, key_ok, logsum, grad_low):
    query_rows, head_count, head_depth = query.shape
    block_rows = min(512, query_rows)
    block_count = query_rows // block_rows

    def single_block(carry, item):
        query_block, grad_block, logsum_block = item
        scores = (
            jnp.einsum("qhd,khd->hqk", query_block, keys, preferred_element_type=jnp.float32)
            * 0.125
        )
        scores = jnp.where(key_ok[None, None, :], scores, MASKED)
        probs = jnp.exp(scores - logsum_block[..., None])
        grad_probs = jnp.einsum(
            "qhd,khd->hqk", grad_block, values, preferred_element_type=jnp.float32
        )
        inner = jnp.sum(probs * grad_probs, axis=2, keepdims=True)
        grad_scores = (probs * (grad_probs - inner)).astype(jnp.bfloat16)
        query_grad = (
            jnp.einsum("hqk,khd->qhd", grad_scores, keys, preferred_element_type=jnp.float32)
            * 0.125
        )
        key_grad = (
            carry[0]
            + jnp.einsum(
                "hqk,qhd->khd", grad_scores, query_block, preferred_element_type=jnp.float32
            )
            * 0.125
        )
        value_grad = carry[1] + jnp.einsum(
            "hqk,qhd->khd",
            probs.astype(jnp.bfloat16),
            grad_block,
            preferred_element_type=jnp.float32,
        )
        return ((key_grad, value_grad), query_grad)

    zeros = jnp.zeros(keys.shape, jnp.float32)
    items = (
        query.reshape(block_count, block_rows, head_count, head_depth),
        grad_low.reshape(block_count, block_rows, head_count, head_depth),
        logsum,
    )
    (key_grad, value_grad), query_grad = lax.scan(single_block, (zeros, zeros), items)
    return (query_grad.reshape(query_rows, head_count * head_depth), key_grad, value_grad)


def gelu_exact(value):
    return jax.nn.gelu(value, approximate=False)


def sum_weights(qkv_part, qv_part, out_part, out_bias, up_part, up_bias, down_part, down_bias):
    return lax.psum(
        (qkv_part, qv_part, out_part, out_bias, up_part, up_bias, down_part, down_bias), "dp"
    )


def on_device(
    act_in,
    cotangent,
    lengths,
    w_qkv,
    bias_qv,
    w_out,
    bias_out,
    w_up,
    bias_up,
    w_down,
    bias_down,
    ln_gain,
    ln_shift,
):
    col_count = lax.axis_size("col")
    row_count = lax.axis_size("row")
    quarter = act_in.shape[0]
    group = quarter * col_count
    half = group // row_count
    width = act_in.shape[1] * row_count
    head_depth = HDIM
    positions = jnp.arange(group, dtype=jnp.int32)
    key_ok = positions < lengths[0]
    own_ok = lax.dynamic_slice_in_dim(key_ok, lax.axis_index("col") * quarter, quarter, 0)
    kept = []
    state = act_in.astype(jnp.float32)
    for layer in range(LAYERS):
        gains = ln_gain[layer].astype(jnp.float32)
        shifts = ln_shift[layer].astype(jnp.float32)
        state_all = gather_cols(state.astype(jnp.bfloat16))
        qkv = sum_rows(state_all, w_qkv[layer], "ta,asc->tsc", half)
        bias_rows = bias_qv[layer].astype(jnp.float32)
        qkv = qkv + jnp.stack([bias_rows[0], jnp.zeros_like(bias_rows[0]), bias_rows[1]])[None]
        qkv_low = qkv.astype(jnp.bfloat16)
        key_value = gather_keys(qkv_low[:, 1:])
        head_local = qkv_low.shape[2] // head_depth
        query = qkv_low[:, 0].reshape(half, head_local, head_depth)
        keys = key_value[:, 0].reshape(group, head_local, head_depth)
        values = key_value[:, 1].reshape(group, head_local, head_depth)
        mixture, logsum = attend_forward(query, keys, values, key_ok)
        mixture_all = gather_rows(mixture.astype(jnp.bfloat16))
        branch = sum_cols(mixture_all, w_out[layer], "tc,ca->ta", quarter) + bias_out[layer].astype(
            jnp.float32
        )
        normed, unit_one, inverse_one = norm_forward(state + branch, gains[0], shifts[0], width)
        normed_all = gather_cols(normed.astype(jnp.bfloat16))
        hidden_pre = sum_rows(normed_all, w_up[layer], "ta,af->tf", half)
        hidden_pre = hidden_pre + bias_up[layer].astype(jnp.float32)
        hidden_all = gather_rows(gelu_exact(hidden_pre).astype(jnp.bfloat16))
        branch_two = sum_cols(hidden_all, w_down[layer], "tf,fa->ta", quarter) + bias_down[
            layer
        ].astype(jnp.float32)
        state_next, unit_two, inverse_two = norm_forward(
            normed + branch_two, gains[1], shifts[1], width
        )
        kept.append(
            (
                state_all,
                query,
                keys,
                values,
                logsum,
                mixture_all,
                unit_one,
                inverse_one,
                normed_all,
                hidden_pre,
                hidden_all,
                unit_two,
                inverse_two,
            )
        )
        state = state_next
    output = jnp.where(own_ok[:, None], state, 0.0).astype(jnp.bfloat16)
    grad_state = jnp.where(own_ok[:, None], cotangent.astype(jnp.float32), 0.0)
    layer_grads = [None] * LAYERS
    gain_parts = [None] * LAYERS
    shift_parts = [None] * LAYERS
    for layer in range(LAYERS - 1, -1, -1):
        (
            state_all,
            query,
            keys,
            values,
            logsum,
            mixture_all,
            unit_one,
            inverse_one,
            normed_all,
            hidden_pre,
            hidden_all,
            unit_two,
            inverse_two,
        ) = kept[layer]
        gains = ln_gain[layer].astype(jnp.float32)
        head_local = query.shape[1]
        resid_two, gain_two, shift_two = norm_backward(
            grad_state, unit_two, inverse_two, gains[1], width
        )
        branch_grad = back_gather_cols(resid_two.astype(jnp.bfloat16))
        down_grad = jnp.einsum(
            "tf,ta->fa", hidden_all, branch_grad, preferred_element_type=jnp.float32
        )
        down_bias_grad = jnp.sum(branch_grad, 0, dtype=jnp.float32)
        hidden_grad = back_sum_rows(branch_grad, w_down[layer], "ta,fa->tf", half)
        hidden_pre_grad = jax.vjp(gelu_exact, hidden_pre)[1](hidden_grad)[0]
        pre_all = back_gather_rows(hidden_pre_grad.astype(jnp.bfloat16))
        up_grad = jnp.einsum("ta,tf->af", normed_all, pre_all, preferred_element_type=jnp.float32)
        up_bias_grad = jnp.sum(pre_all, 0, dtype=jnp.float32)
        normed_grad = resid_two + back_sum_cols(pre_all, w_up[layer], "tf,af->ta", quarter)
        resid_one, gain_one, shift_one = norm_backward(
            normed_grad, unit_one, inverse_one, gains[0], width
        )
        attn_grad = back_gather_cols(resid_one.astype(jnp.bfloat16))
        out_grad = jnp.einsum(
            "tc,ta->ca", mixture_all, attn_grad, preferred_element_type=jnp.float32
        )
        out_bias_grad = jnp.sum(attn_grad, 0, dtype=jnp.float32)
        mixture_grad = back_sum_rows(attn_grad, w_out[layer], "ta,ca->tc", half)
        grad_low = mixture_grad.astype(jnp.bfloat16).reshape(half, head_local, head_depth)
        query_grad, key_grad, value_grad = attend_backward(
            query, keys, values, key_ok, logsum, grad_low
        )
        key_half, value_half = (
            lax.psum_scatter(key_grad.reshape(group, -1), "row", scatter_dimension=0, tiled=True),
            lax.psum_scatter(value_grad.reshape(group, -1), "row", scatter_dimension=0, tiled=True),
        )
        qkv_grad = jnp.stack([query_grad, key_half, value_half], 1).astype(jnp.bfloat16)
        qkv_all = back_gather_rows(qkv_grad)
        qkv_weight_grad = jnp.einsum(
            "ta,tsc->asc", state_all, qkv_all, preferred_element_type=jnp.float32
        )
        qv_bias_grad = jnp.sum(qkv_all[:, ::2], 0, dtype=jnp.float32)
        grad_state = resid_one + back_sum_cols(qkv_all, w_qkv[layer], "tsc,asc->ta", quarter)
        gain_parts[layer] = jnp.stack([gain_one, gain_two])
        shift_parts[layer] = jnp.stack([shift_one, shift_two])
        layer_grads[layer] = (
            qkv_weight_grad,
            qv_bias_grad,
            out_grad,
            out_bias_grad,
            up_grad,
            up_bias_grad,
            down_grad,
            down_bias_grad,
        )
    stacked = sum_weights(
        *[jnp.stack([layer_grads[layer][slot] for layer in range(LAYERS)]) for slot in range(8)]
    )
    gain_grad, shift_grad = lax.psum((jnp.stack(gain_parts), jnp.stack(shift_parts)), ("dp", "col"))
    return (
        output,
        grad_state,
        stacked[0],
        stacked[1],
        stacked[2],
        stacked[3],
        stacked[4],
        stacked[5],
        stacked[6],
        stacked[7],
        gain_grad,
        shift_grad,
    )


def solution(mesh):
    return jax.shard_map(
        on_device,
        mesh=mesh,
        in_specs=(
            P(("dp", "col"), "row"),
            P(("dp", "col"), "row"),
            P("dp"),
            P(None, "row", None, "col"),
            P(None, None, "col"),
            P(None, "col", "row"),
            P(None, "row"),
            P(None, "row", "col"),
            P(None, "col"),
            P(None, "col", "row"),
            P(None, "row"),
            P(None, None, "row"),
            P(None, None, "row"),
        ),
        out_specs=(
            P(("dp", "col"), "row"),
            P(("dp", "col"), "row"),
            P(None, "row", None, "col"),
            P(None, None, "col"),
            P(None, "col", "row"),
            P(None, "row"),
            P(None, "row", "col"),
            P(None, "col"),
            P(None, "col", "row"),
            P(None, "row"),
            P(None, None, "row"),
            P(None, None, "row"),
        ),
        check_vma=False,
    )
```

profile of v0, /device:TPU:0, one launch (start us, length us, event | category | flops | bytes accessed | tf_op | source)
XLA Modules:
  0.0 1422.1 jit_solution(13531446442578852716)
XLA Ops:
  7.2 9.5 all_gather.54
  21.4 39.6 %reduce-scatter.21.cloned.1.call-done = f32[512,3,192]{0,2,1:T(8,128)} async-done(((f32[1024,3,192]{0,2,1:T(8,128)}), f32[512,3,192]{0,2,1:T(8,128)}) %reduce-scatter.21.cloned.1.call-update) | async-done | bytes 1179664 | tf_op jit(solution)/shard_map/reduce_scatter | solution.py:39
  62.4 13.0 all_gather.55
  81.0 8.0 all_gather.56
  93.3 21.4 %reduce-scatter.23.cloned.1.call-done = f32[256,384]{1,0:T(8,128)} async-done(((f32[1024,384]{1,0:T(8,128)}), f32[256,384]{1,0:T(8,128)}) %reduce-scatter.23.cloned.1.call-update) | async-done | bytes 393232 | tf_op jit(solution)/shard_map/reduce_scatter | solution.py:52
  115.9 6.4 all-reduce.10
  122.5 7.6 all_gather.57
  135.0 47.7 %reduce-scatter.25.cloned.1.call-done = f32[512,768]{1,0:T(8,128)} async-done(((f32[1024,768]{1,0:T(8,128)}), f32[512,768]{1,0:T(8,128)}) %reduce-scatter.25.cloned.1.call-update) | async-done | bytes 1572880 | tf_op jit(solution)/shard_map/reduce_scatter | solution.py:39
  188.5 30.7 %all-gather.7.cloned.1.call-done = bf16[1024,768]{1,0:T(8,128)(2,1)} async-done(((bf16[512,768]{1,0:T(8,128)(2,1)}), bf16[1024,768]{1,0:T(8,128)(2,1)}) %all-gather.7.cloned.1.call-update) | async-done | bytes 1572880 | tf_op jit(solution)/shard_map/all_gather | solution.py:19
  224.0 22.1 %reduce-scatter.27.cloned.1.call-done = f32[256,384]{1,0:T(8,128)} async-done(((f32[1024,384]{1,0:T(8,128)}), f32[256,384]{1,0:T(8,128)}) %reduce-scatter.27.cloned.1.call-update) | async-done | bytes 393232 | tf_op jit(solution)/shard_map/reduce_scatter | solution.py:52
  247.3 6.4 all-reduce.9
  254.0 7.5 all_gather.59
  265.1 40.4 %reduce-scatter.29.cloned.1.call-done = f32[512,3,192]{0,2,1:T(8,128)} async-done(((f32[1024,3,192]{0,2,1:T(8,128)}), f32[512,3,192]{0,2,1:T(8,128)}) %reduce-scatter.29.cloned.1.call-update) | async-done | bytes 1179664 | tf_op jit(solution)/shard_map/reduce_scatter | solution.py:39
  307.0 13.3 all_gather.60
  325.9 7.9 all_gather.61
  335.6 23.2 %reduce-scatter.31.cloned.1.call-done = f32[256,384]{1,0:T(8,128)} async-done(((f32[1024,384]{1,0:T(8,128)}), f32[256,384]{1,0:T(8,128)}) %reduce-scatter.31.cloned.1.call-update) | async-done | bytes 393232 | tf_op jit(solution)/shard_map/reduce_scatter | solution.py:52
  360.2 6.4 all-reduce.8
  366.8 7.4 all_gather.62
  377.0 49.1 %reduce-scatter.33.cloned.1.call-done = f32[512,768]{1,0:T(8,128)} async-done(((f32[1024,768]{1,0:T(8,128)}), f32[512,768]{1,0:T(8,128)}) %reduce-scatter.33.cloned.1.call-update) | async-done | bytes 1572880 | tf_op jit(solution)/shard_map/reduce_scatter | solution.py:39
  426.1 5.7 multiply_convert_fusion.2
  431.8 30.7 %all-gather.9.cloned.1.call-done = bf16[1024,768]{1,0:T(8,128)(2,1)} async-done(((bf16[512,768]{1,0:T(8,128)(2,1)}), bf16[1024,768]{1,0:T(8,128)(2,1)}) %all-gather.9.cloned.1.call-update) | async-done | bytes 1572880 | tf_op jit(solution)/shard_map/all_gather | solution.py:19
  466.8 22.6 %reduce-scatter.35.cloned.1.call-done = f32[256,384]{1,0:T(8,128)} async-done(((f32[1024,384]{1,0:T(8,128)}), f32[256,384]{1,0:T(8,128)}) %reduce-scatter.35.cloned.1.call-update) | async-done | bytes 393232 | tf_op jit(solution)/shard_map/reduce_scatter | solution.py:52
  490.7 6.4 all-reduce.7
  497.9 6.4 all-reduce.6
  504.6 7.5 all_gather.64
  516.2 49.0 %reduce-scatter.37.cloned.1.call-done = f32[512,768]{1,0:T(8,128)} async-done(((f32[1024,768]{1,0:T(8,128)}), f32[512,768]{1,0:T(8,128)}) %reduce-scatter.37.cloned.1.call-update) | async-done | bytes 1572880 | tf_op jit(solution)/shard_map/reduce_scatter | solution.py:65
  568.8 30.7 %all-gather.11.cloned.1.call-done = bf16[1024,768]{1,0:T(8,128)(2,1)} async-done(((bf16[512,768]{1,0:T(8,128)(2,1)}), bf16[1024,768]{1,0:T(8,128)(2,1)}) %all-gather.11.cloned.1.call-update) | async-done | bytes 1572880 | tf_op jit(solution)/shard_map/all_gather | solution.py:31
  603.2 23.3 %reduce-scatter.39.cloned.1.call-done = f32[256,384]{1,0:T(8,128)} async-done(((f32[1024,384]{1,0:T(8,128)}), f32[256,384]{1,0:T(8,128)}) %reduce-scatter.39.cloned.1.call-update) | async-done | bytes 393232 | tf_op jit(solution)/shard_map/reduce_scatter | solution.py:78
  629.1 6.8 all-reduce.5
  637.6 7.7 all_gather.66
  647.6 23.0 %reduce-scatter.41.cloned.1.call-done = f32[512,192]{0,1:T(8,128)} async-done(((f32[1024,192]{0,1:T(8,128)}), f32[512,192]{0,1:T(8,128)}) %reduce-scatter.41.cloned.1.call-update) | async-done | bytes 393232 | tf_op jit(solution)/shard_map/reduce_scatter | solution.py:65
  688.4 9.1 reduce-scatter.45.cloned.1.call-done
  698.5 22.7 %reduce-scatter.43.cloned.1.call-done = f32[512,192]{0,1:T(8,128)} async-done(((f32[1024,192]{0,1:T(8,128)}), f32[512,192]{0,1:T(8,128)}) %reduce-scatter.43.cloned.1.call-update) | async-done | bytes 393232 | tf_op jit(solution)/shard_map/reduce_scatter | solution.py:307
  724.1 26.3 %all-gather.13.cloned.1.call-done = bf16[1024,3,192]{0,2,1:T(8,128)(2,1)} async-done(((bf16[512,3,192]{0,2,1:T(8,128)(2,1)}), bf16[1024,3,192]{0,2,1:T(8,128)(2,1)}) %all-gather.13.cloned.1.call-update) | async-done | bytes 1179664 | tf_op jit(solution)/shard_map/all_gather | solution.py:31
  753.8 23.3 %reduce-scatter.47.cloned.1.call-done = f32[256,384]{1,0:T(8,128)} async-done(((f32[1024,384]{1,0:T(8,128)}), f32[256,384]{1,0:T(8,128)}) %reduce-scatter.47.cloned.1.call-update) | async-done | bytes 393232 | tf_op jit(solution)/shard_map/reduce_scatter | solution.py:78
  779.0 6.6 all-reduce.4
  786.5 7.6 all_gather.68
  797.8 48.9 %reduce-scatter.49.cloned.1.call-done = f32[512,768]{1,0:T(8,128)} async-done(((f32[1024,768]{1,0:T(8,128)}), f32[512,768]{1,0:T(8,128)}) %reduce-scatter.49.cloned.1.call-update) | async-done | bytes 1572880 | tf_op jit(solution)/shard_map/reduce_scatter | solution.py:65
  849.7 30.7 %all-gather.15.cloned.1.call-done = bf16[1024,768]{1,0:T(8,128)(2,1)} async-done(((bf16[512,768]{1,0:T(8,128)(2,1)}), bf16[1024,768]{1,0:T(8,128)(2,1)}) %all-gather.15.cloned.1.call-update) | async-done | bytes 1572880 | tf_op jit(solution)/shard_map/all_gather | solution.py:31
  884.2 23.3 %reduce-scatter.51.cloned.1.call-done = f32[256,384]{1,0:T(8,128)} async-done(((f32[1024,384]{1,0:T(8,128)}), f32[256,384]{1,0:T(8,128)}) %reduce-scatter.51.cloned.1.call-update) | async-done | bytes 393232 | tf_op jit(solution)/shard_map/reduce_scatter | solution.py:78
  909.4 6.6 all-reduce.3
  916.9 7.7 all_gather.70
  926.9 23.0 %reduce-scatter.53.cloned.1.call-done = f32[512,192]{0,1:T(8,128)} async-done(((f32[1024,192]{0,1:T(8,128)}), f32[512,192]{0,1:T(8,128)}) %reduce-scatter.53.cloned.1.call-update) | async-done | bytes 393232 | tf_op jit(solution)/shard_map/reduce_scatter | solution.py:65
  967.0 9.8 reduce-scatter.57.cloned.1.call-done
  977.8 22.7 %reduce-scatter.55.cloned.1.call-done = f32[512,192]{0,1:T(8,128)} async-done(((f32[1024,192]{0,1:T(8,128)}), f32[512,192]{0,1:T(8,128)}) %reduce-scatter.55.cloned.1.call-update) | async-done | bytes 393232 | tf_op jit(solution)/shard_map/reduce_scatter | solution.py:307
  1003.4 26.2 %all-gather.17.cloned.1.call-done = bf16[1024,3,192]{0,2,1:T(8,128)(2,1)} async-done(((bf16[512,3,192]{0,2,1:T(8,128)(2,1)}), bf16[1024,3,192]{0,2,1:T(8,128)(2,1)}) %all-gather.17.cloned.1.call-update) | async-done | bytes 1179664 | tf_op jit(solution)/shard_map/all_gather | solution.py:31
  1054.0 281.6 %all-reduce = (f32[2,2,384]{2,1,0:T(2,128)}, f32[2,2,384]{2,1,0:T(2,128)}) all-reduce(f32[2,2,384]{2,1,0:T(2,128)S(1)} %pad_maximum_fusion.7, f32[2,2,384]{2,1,0:T(2,128)S(1)} %pad_maximum_fusion.8), channel_id=1, replica_groups=mesh['dp'=16,'row'=2,'col'=4] {'dp','col'}, use_global_device_ids=true, to_apply=%region_78.79 | all-reduce | flops 3072 | bytes 24576 | tf_op jit(solution)/shard_map/psum | solution.py:332
  1335.8 69.6 %all-reduce.1 = (f32[2,2,192]{2,1,0:T(2,128)}, f32[2,384]{1,0:T(2,128)}, f32[2,768]{1,0:T(2,128)}, f32[2,384]{1,0:T(2,128)}) all-reduce(f32[2,2,192]{2,1,0:T(2,128)S(1)} %pad_maximum_fusion.11, f32[2,384]{1,0:T(2,128)S(1)} %pad_maximum_fusion.12, ...), channel_id=1, replica_groups=mesh['dp'=16,'row'=2,'col'=4] {'dp'}, use_global_device_ids=true, to_apply=%region_61.62 | all-reduce | flops 3840 | bytes 30720 | tf_op jit(solution)/shard_map/psum | solution.py:177
  (433 shorter events, 172.1 us)
Async XLA Ops:
  7.2 53.7 %reduce-scatter.21.cloned.1.call-start = ((), (), s32[]{:S(2)}) async-start(), calls=%async_computation.20 | async-start | bytes 3538944 | tf_op jit(solution)/shard_map/reduce_scatter | solution.py:39
  19.9 94.8 %reduce-scatter.23.cloned.1.call-start = ((), (), s32[]{:S(2)}) async-start(), calls=%async_computation.21 | async-start | bytes 1966080 | tf_op jit(solution)/shard_map/reduce_scatter | solution.py:52
  20.7 54.9 %copy-start.110 = (pred[1024]{0:T(1024)(128)(4,1)}, pred[1024]{0:T(1024)(128)(4,1)S(1)}, u32[]{:S(2)}) copy-start(pred[1024]{0:T(1024)(128)(4,1)S(1)} %iota_compare_fusion) | copy-start | bytes 3076
  91.4 39.6 %copy-start.24 = (bf16[2,384,768]{2,1,0:T(8,128)(2,1)S(1)}, bf16[2,384,768]{2,1,0:T(8,128)(2,1)}, u32[]{:S(2)}) copy-start(bf16[2,384,768]{2,1,0:T(8,128)(2,1)} %param.20) | copy-start | bytes 3538948
  91.4 91.3 %reduce-scatter.25.cloned.1.call-start = ((), (), s32[]{:S(2)}) async-start(), calls=%async_computation.22 | async-start | bytes 4718592 | tf_op jit(solution)/shard_map/reduce_scatter | solution.py:39
  93.3 152.8 %copy-start.68 = (f32[384]{0:T(512)}, f32[384]{0:T(512)S(1)}, u32[]{:S(2)}) copy-start(f32[384]{0:T(512)S(1)} %get-tuple-element.232) | copy-start | bytes 4612
  93.3 160.5 %copy-start.70 = (f32[384]{0:T(512)}, f32[384]{0:T(512)S(1)}, u32[]{:S(2)}) copy-start(f32[384]{0:T(512)S(1)} %get-tuple-element.233) | copy-start | bytes 4612
  93.3 160.5 %copy-start.92 = (f32[384]{0:T(512)}, f32[384]{0:T(512)S(1)}, u32[]{:S(2)}) copy-start(f32[384]{0:T(512)S(1)} %get-tuple-element.146) | copy-start | bytes 4612
  122.4 123.7 %copy-start.82 = (f32[256]{0:T(256)}, f32[256]{0:T(256)S(1)}, u32[]{:S(2)}) copy-start(f32[256]{0:T(256)S(1)} %get-tuple-element.218) | copy-start | bytes 3076
  122.4 123.7 %copy-start.84 = (f32[256]{0:T(256)}, f32[256]{0:T(256)S(1)}, u32[]{:S(2)}) copy-start(f32[256]{0:T(256)S(1)} %get-tuple-element.219) | copy-start | bytes 3076
  133.7 85.4 %all-gather.7.cloned.1.call-start = ((), (), s32[]{:S(2)}) async-start(), calls=%async_computation.23 | async-start | bytes 2359296 | tf_op jit(solution)/shard_map/all_gather | solution.py:19
  135.0 53.4 %copy-start.73 = (f32[768]{0:T(1024)}, f32[768]{0:T(1024)S(1)}, u32[]{:S(2)}) copy-start(f32[768]{0:T(1024)S(1)} %get-tuple-element.143) | copy-start | bytes 9220
  188.4 57.6 %reduce-scatter.27.cloned.1.call-start = ((), (), s32[]{:S(2)}) async-start(), calls=%async_computation.24 | async-start | bytes 1966080 | tf_op jit(solution)/shard_map/reduce_scatter | solution.py:52
  222.7 82.8 %reduce-scatter.29.cloned.1.call-start = ((), (), s32[]{:S(2)}) async-start(), calls=%async_computation.25 | async-start | bytes 3538944 | tf_op jit(solution)/shard_map/reduce_scatter | solution.py:39
  247.3 111.5 %copy-start.10 = (f32[256,384]{1,0:T(8,128)}, f32[256,384]{1,0:T(8,128)S(1)}, u32[]{:S(2)}) copy-start(f32[256,384]{1,0:T(8,128)S(1)} %get-tuple-element.191) | copy-start | bytes 1179652
  265.0 40.5 %copy-start.94 = (f32[3,192]{1,0:T(4,128)S(1)}, f32[3,192]{1,0:T(4,128)}, u32[]{:S(2)}) copy-start(f32[3,192]{1,0:T(4,128)} %get-tuple-element.220) | copy-start | bytes 6916
  265.0 93.8 %reduce-scatter.31.cloned.1.call-start = ((), (), s32[]{:S(2)}) async-start(), calls=%async_computation.26 | async-start | bytes 1966080 | tf_op jit(solution)/shard_map/reduce_scatter | solution.py:52
  335.5 90.5 %reduce-scatter.33.cloned.1.call-start = ((), (), s32[]{:S(2)}) async-start(), calls=%async_computation.27 | async-start | bytes 4718592 | tf_op jit(solution)/shard_map/reduce_scatter | solution.py:39
  366.6 259.9 %copy-start.80 = (f32[256]{0:T(256)}, f32[256]{0:T(256)S(1)}, u32[]{:S(2)}) copy-start(f32[256]{0:T(256)S(1)} %get-tuple-element.214) | copy-start | bytes 3076
  366.6 259.9 %copy-start.81 = (f32[256]{0:T(256)}, f32[256]{0:T(256)S(1)}, u32[]{:S(2)}) copy-start(f32[256]{0:T(256)S(1)} %get-tuple-element.215) | copy-start | bytes 3076
  376.9 49.2 %copy-start.75 = (f32[768]{0:T(1024)S(1)}, f32[768]{0:T(1024)}, u32[]{:S(2)}) copy-start(f32[768]{0:T(1024)} %get-tuple-element.142) | copy-start | bytes 9220
  376.9 85.6 %all-gather.9.cloned.1.call-start = ((), (), s32[]{:S(2)}) async-start(), calls=%async_computation.28 | async-start | bytes 2359296 | tf_op jit(solution)/shard_map/all_gather | solution.py:19
  431.8 57.6 %reduce-scatter.35.cloned.1.call-start = ((), (), s32[]{:S(2)}) async-start(), calls=%async_computation.29 | async-start | bytes 1966080 | tf_op jit(solution)/shard_map/reduce_scatter | solution.py:52
  466.1 99.2 %reduce-scatter.37.cloned.1.call-start = ((), (), s32[]{:S(2)}) async-start(), calls=%async_computation.30 | async-start | bytes 4718592 | tf_op jit(solution)/shard_map/reduce_scatter | solution.py:65
  516.1 49.1 %copy-start.23 = (f32[512,768]{1,0:T(8,128)S(1)}, f32[512,768]{1,0:T(8,128)}, u32[]{:S(2)}) copy-start(f32[512,768]{1,0:T(8,128)} %reduce-scatter.33.cloned.1.call-done) | copy-start | bytes 4718596
  516.2 83.3 %all-gather.11.cloned.1.call-start = ((), (), s32[]{:S(2)}) async-start(), calls=%async_computation.31 | async-start | bytes 2359296 | tf_op jit(solution)/shard_map/all_gather | solution.py:31
  568.7 57.8 %reduce-scatter.39.cloned.1.call-start = ((), (), s32[]{:S(2)}) async-start(), calls=%async_computation.32 | async-start | bytes 1966080 | tf_op jit(solution)/shard_map/reduce_scatter | solution.py:78
  603.2 67.4 %reduce-scatter.41.cloned.1.call-start = ((), (), s32[]{:S(2)}) async-start(), calls=%async_computation.33 | async-start | bytes 1179648 | tf_op jit(solution)/shard_map/reduce_scatter | solution.py:65
  647.5 50.0 %reduce-scatter.45.cloned.1.call-start = ((), (), s32[]{:S(2)}) async-start(), calls=%async_computation.35 | async-start | bytes 1179648 | tf_op jit(solution)/shard_map/reduce_scatter | solution.py:308
  676.5 44.7 %reduce-scatter.43.cloned.1.call-start = ((), (), s32[]{:S(2)}) async-start(), calls=%async_computation.34 | async-start | bytes 1179648 | tf_op jit(solution)/shard_map/reduce_scatter | solution.py:307
  685.6 64.8 %all-gather.13.cloned.1.call-start = ((), (), s32[]{:S(2)}) async-start(), calls=%async_computation.36 | async-start | bytes 1769472 | tf_op jit(solution)/shard_map/all_gather | solution.py:31
  688.4 62.0 %copy-start.58 = (bf16[2,384,3,192]{1,3,2,0:T(8,128)(2,1)S(1)}, bf16[2,384,3,192]{1,3,2,0:T(8,128)(2,1)}, u32[]{:S(2)}) copy-start(bf16[2,384,3,192]{1,3,2,0:T(8,128)(2,1)} %param.16) | copy-start | bytes 2654212
  724.1 53.1 %reduce-scatter.47.cloned.1.call-start = ((), (), s32[]{:S(2)}) async-start(), calls=%async_computation.37 | async-start | bytes 1966080 | tf_op jit(solution)/shard_map/reduce_scatter | solution.py:78
  753.8 92.9 %reduce-scatter.49.cloned.1.call-start = ((), (), s32[]{:S(2)}) async-start(), calls=%async_computation.38 | async-start | bytes 4718592 | tf_op jit(solution)/shard_map/reduce_scatter | solution.py:65
  795.0 51.7 %copy-start.74 = (f32[768]{0:T(1024)S(1)}, f32[768]{0:T(1024)}, u32[]{:S(2)}) copy-start(f32[768]{0:T(1024)} %copy-done.73) | copy-start | bytes 9220
  797.7 49.0 %copy-start.21 = (f32[512,768]{1,0:T(8,128)S(1)}, f32[512,768]{1,0:T(8,128)}, u32[]{:S(2)}) copy-start(f32[512,768]{1,0:T(8,128)} %reduce-scatter.25.cloned.1.call-done) | copy-start | bytes 4718596
  797.7 49.0 %copy-start.22 = (f32[512,768]{1,0:T(8,128)S(1)}, f32[512,768]{1,0:T(8,128)}, u32[]{:S(2)}) copy-start(f32[512,768]{1,0:T(8,128)} %get-tuple-element.193) | copy-start | bytes 4718596
  797.7 82.7 %all-gather.15.cloned.1.call-start = ((), (), s32[]{:S(2)}) async-start(), calls=%async_computation.39 | async-start | bytes 2359296 | tf_op jit(solution)/shard_map/all_gather | solution.py:31
  849.7 57.8 %reduce-scatter.51.cloned.1.call-start = ((), (), s32[]{:S(2)}) async-start(), calls=%async_computation.40 | async-start | bytes 1966080 | tf_op jit(solution)/shard_map/reduce_scatter | solution.py:78
  884.2 65.7 %reduce-scatter.53.cloned.1.call-start = ((), (), s32[]{:S(2)}) async-start(), calls=%async_computation.41 | async-start | bytes 1179648 | tf_op jit(solution)/shard_map/reduce_scatter | solution.py:65
  926.8 50.0 %reduce-scatter.57.cloned.1.call-start = ((), (), s32[]{:S(2)}) async-start(), calls=%async_computation.43 | async-start | bytes 1179648 | tf_op jit(solution)/shard_map/reduce_scatter | solution.py:308
  955.8 44.7 %reduce-scatter.55.cloned.1.call-start = ((), (), s32[]{:S(2)}) async-start(), calls=%async_computation.42 | async-start | bytes 1179648 | tf_op jit(solution)/shard_map/reduce_scatter | solution.py:307
  965.1 64.6 %all-gather.17.cloned.1.call-start = ((), (), s32[]{:S(2)}) async-start(), calls=%async_computation.44 | async-start | bytes 1769472 | tf_op jit(solution)/shard_map/all_gather | solution.py:31
  967.0 62.7 %copy-start.59 = (bf16[2,384,3,192]{1,3,2,0:T(8,128)(2,1)S(1)}, bf16[2,384,3,192]{1,3,2,0:T(8,128)(2,1)}, u32[]{:S(2)}) copy-start(bf16[2,384,3,192]{1,3,2,0:T(8,128)(2,1)} %param.16) | copy-start | bytes 2654212
  1003.4 401.9 %reduce-scatter.59.cloned.1.call-start = ((), (), s32[]{:S(2)}) async-start(), calls=%async_computation.45 | async-start | bytes 1966080 | tf_op jit(solution)/shard_map/reduce_scatter | solution.py:78
  1033.1 374.0 %all-reduce.13.cloned.1.call-start = ((), (), s32[]{:S(2)}) async-start(), calls=%async_computation.46 | async-start | bytes 14155776 | tf_op jit(solution)/shard_map/psum | solution.py:177
  1053.1 282.4 %copy-start.65 = (bf16[1024,3,192]{0,2,1:T(8,128)(2,1)S(1)}, bf16[1024,3,192]{0,2,1:T(8,128)(2,1)}, u32[]{:S(2)}) copy-start(bf16[1024,3,192]{0,2,1:T(8,128)(2,1)} %all-gather.17.cloned.1.call-done) | copy-start | bytes 3538948
  1053.3 352.0 %copy-start.47 = (f32[256,384]{1,0:T(8,128)S(1)}, f32[256,384]{1,0:T(8,128)}, u32[]{:S(2)}) copy-start(f32[256,384]{1,0:T(8,128)} %get-tuple-element.179) | copy-start | bytes 1179652
  (96 other events, 786.1 us)
Sparse Core Ops, SparseCore 0:
  20.0 40.8 reduce-scatter.20
  91.5 23.1 reduce-scatter.22
  133.9 48.7 reduce-scatter.24
  188.5 30.5 all-gather.6
  222.8 23.1 reduce-scatter.26
  265.1 40.2 reduce-scatter.28
  335.6 23.1 reduce-scatter.30
  377.0 48.9 reduce-scatter.32
  431.9 30.5 all-gather.8
  466.2 23.1 reduce-scatter.34
  516.3 48.9 reduce-scatter.36
  568.8 30.6 all-gather.10
  603.3 23.1 reduce-scatter.38
  647.6 22.8 reduce-scatter.40
  676.6 20.8 reduce-scatter.44
  700.4 20.7 reduce-scatter.42
  724.2 26.1 all-gather.12
  753.9 23.1 reduce-scatter.46
  797.9 48.7 reduce-scatter.48
  849.8 30.5 all-gather.14
  884.3 23.1 reduce-scatter.50
  926.9 22.9 reduce-scatter.52
  955.9 20.8 reduce-scatter.56
  979.7 20.8 reduce-scatter.54
  1003.5 26.1 all-gather.16
  1033.2 23.1 reduce-scatter.58
  1061.2 130.8 all-reduce.12
where the time goes:
time: 1430 us; the launch traced here: 1420 us
  waiting for transfers between devices  720 us (50%)
  blocking collectives  508 us (36%)
  matrix products  82.7 us (6%)
  other arithmetic  70.6 us (5%)
  local copies, waits for them, and re-layouts  22.7 us (2%)
  between operations  16.7 us (1%)
    psum x1, blocking collectives, on_device(): lax.psum((jnp.stack(gain_parts), jnp.stack(shift_parts)), ('dp', 'col'))  282 us
    reduce_scatter x4, waiting for transfers between devices, sum_rows(): lax.psum_scatter(term(jnp.int32(0), lax.axis_size('row') * local_rows), '...  177 us
    reduce_scatter x4, waiting for transfers between devices, back_sum_rows(): lax.psum_scatter(term(jnp.int32(0), lax.axis_size('row') * local_rows), '...  144 us
    all_gather x4, waiting for transfers between devices, back_gather_rows(): return lax.all_gather(value, 'row', axis=0, tiled=True)  114 us
    reduce_scatter x4, waiting for transfers between devices, sum_cols(): lax.psum_scatter(term(jnp.int32(0), lax.axis_size('col') * local_rows), '...  89.4 us
    reduce_scatter x4, waiting for transfers between devices, back_sum_cols(): lax.psum_scatter(term(jnp.int32(0), lax.axis_size('col') * local_rows), '...  69.9 us
    psum x1, blocking collectives, sum_weights(): lax.psum((qkv_part, qv_part, out_part, out_bias, up_part, up_bias, down_p...  69.6 us
    all_gather x2, waiting for transfers between devices, gather_rows(): return lax.all_gather(value, 'row', axis=0, tiled=True)  61.4 us
  transfers between devices with their start and end apart: 27, of which 25 were waited for; matrix products, arithmetic and copies ran while one was open for 3% of the time, Pallas kernels for 0%

commit v1 on v0

v1 whole, which is shorter than its diff:
```python
import jax
import jax.numpy as jnp
from jax import lax
from jax.sharding import Mesh
from jax.sharding import PartitionSpec as P

LAYERS = 2
HDIM = 64
HEADS = 6
GROUP = 1024
QUARTER = 256
WIDTH = 768
HALF = 384
BLOCK = 192
HID = 768
PACK_A = 768
PACK_B = 1536
SMALL = 456

EPSILON = 1e-05
MASKED = -1000000000.0

LINE = ("row", "zl")
PLANE = ("x", "y")
bf16 = jnp.bfloat16
f32 = jnp.float32


def swapped(value, axes, count, bits):
    return lax.ppermute(value, axes, [(i, i ^ bits) for i in range(count)])


def in_order(parts, place):
    flip = (place % 2) == 1
    parts = [jnp.where(flip, parts[s ^ 1], parts[s]) for s in range(4)]
    flip = (place // 2) == 1
    return [jnp.where(flip, parts[s ^ 2], parts[s]) for s in range(4)]


def gather(value, axes):
    return [value] + [swapped(value, axes, 4, bits) for bits in (1, 3, 2)]


def near_first(parts):
    return [parts[0], parts[1], parts[3], parts[2]]


def piece_of(value, index, dim):
    return lax.dynamic_index_in_dim(value, index, dim, keepdims=False)


def split3(value):
    high = lax.reduce_precision(value, 8, 7)
    rest = value - high
    middle = lax.reduce_precision(rest, 8, 7)
    return jnp.stack([high, middle, rest - middle]).astype(bf16)


def dot(left, right, dims):
    return lax.dot_general(left, right, ((dims[0], dims[1]), ((), ())), preferred_element_type=f32)


def mm(left, right):
    return dot(left, right, ((1,), (0,)))


def mt(left, right):
    return dot(left, right, ((1,), (1,)))


def tm(left, right):
    return dot(left, right, ((0,), (0,)))


def core_sum(value):
    return value + swapped(value, "core", 2, 1)


def norm_forward(resid, gain, shift):
    mean = jnp.mean(resid, 1, keepdims=True)
    square = jnp.mean(resid * resid, 1, keepdims=True)
    inverse = lax.rsqrt(square - mean * mean + EPSILON)
    unit = (resid - mean) * inverse
    return unit * gain + shift, unit, inverse


def norm_backward(grad, unit, inverse, gain):
    scaled = grad * gain
    first = jnp.mean(scaled, 1, keepdims=True)
    second = jnp.mean(scaled * unit, 1, keepdims=True)
    resid_grad = inverse * (scaled - first - unit * second)
    return resid_grad, jnp.sum(grad * unit, 0), jnp.sum(grad, 0)


def heads_of(value):
    return value.reshape(value.shape[0], HEADS, HDIM)


def attend_forward(query, keys, values, key_ok):
    scores = jnp.einsum("qhd,khd->hqk", heads_of(query), heads_of(keys), preferred_element_type=f32) * 0.125
    scores = jnp.where(key_ok[None, None, :], scores, MASKED)
    peak = jnp.max(scores, axis=2, keepdims=True)
    raised = jnp.exp(scores - peak)
    probs = raised / jnp.sum(raised, axis=2, keepdims=True)
    mixture = jnp.einsum("hqk,khd->qhd", probs.astype(bf16), heads_of(values), preferred_element_type=f32)
    return mixture.reshape(QUARTER, HEADS * HDIM), probs


def attend_backward(query, keys, values, probs, grad):
    grad = heads_of(grad)
    grad_probs = jnp.einsum("qhd,khd->hqk", grad, heads_of(values), preferred_element_type=f32)
    inner = jnp.sum(probs * grad_probs, axis=2, keepdims=True)
    grad_scores = (probs * (grad_probs - inner)).astype(bf16)
    query_grad = jnp.einsum("hqk,khd->qhd", grad_scores, heads_of(keys), preferred_element_type=f32) * 0.125
    key_grad = jnp.einsum("hqk,qhd->khd", grad_scores, heads_of(query), preferred_element_type=f32) * 0.125
    value_grad = jnp.einsum("hqk,qhd->khd", probs.astype(bf16), grad, preferred_element_type=f32)
    return (
        query_grad.reshape(QUARTER, HEADS * HDIM),
        key_grad.reshape(GROUP, HEADS * HDIM),
        value_grad.reshape(GROUP, HEADS * HDIM),
    )


def gelu_exact(value):
    return jax.nn.gelu(value, approximate=False)


def weight_grad(pairs):
    blocks = []
    for row in range(2):
        for z in range(2):
            blocks += [tm(right[z], left[:, row * HALF : (row + 1) * HALF]).astype(bf16) for left, right in pairs]
    return jnp.concatenate(blocks, 0).reshape(64, -1, HALF)


def plane_pieces(pieces):
    return pieces.reshape(4, 16, -1, HALF).transpose(1, 0, 2, 3).reshape(16, -1, HALF)


def plane_exchange(pieces):
    return lax.all_to_all(pieces, PLANE, 0, 0, tiled=True)


def plane_sum(received):
    return jnp.sum(received, 0, dtype=f32)


def line_sum(pieces, place):
    total = piece_of(pieces, place, 0).astype(f32)
    for bits in (1, 3, 2):
        total = total + swapped(piece_of(pieces, place ^ bits, 0), LINE, 4, bits).astype(f32)
    return total


def exchange(pieces):
    return lax.all_to_all(pieces, LINE + PLANE, 0, 0, tiled=True)


def when(value):
    return lax.slice(value, (0,) * value.ndim, (1,) * value.ndim).reshape(()).astype(f32) * 0.0


def on_device(
    act_in, cotangent, lengths, w_qkv, bias_qv, w_out, bias_out, w_up, bias_up, w_down, bias_down, ln_gain, ln_shift
):
    at_x, at_y = lax.axis_index("x"), lax.axis_index("y")
    row, zl, core = lax.axis_index("row"), lax.axis_index("zl"), lax.axis_index("core")
    place = 2 * row + zl

    first = in_order(near_first(gather(jnp.concatenate([w_qkv[0].reshape(HALF, 3 * BLOCK), w_out[0].T], 1), LINE)), place)
    first = [jnp.concatenate([first[z], first[2 + z]], 0) for z in range(2)]
    rank = 4 * at_x + at_y
    late = [lax.dynamic_slice_in_dim(part, 24 * rank, 24, dim) for part, dim in ((w_qkv, 1), (w_out, 2), (w_up, 1), (w_down, 2))]
    late = [late[0].reshape(LAYERS, 24, 3 * BLOCK), late[1].transpose(0, 2, 1), late[2], late[3].transpose(0, 2, 1)]
    sooner = jnp.concatenate([late[2][0], late[3][0], late[0][1], late[1][1]], 1)
    later = jnp.concatenate([late[2][1], late[3][1]], 1)
    sooner = lax.all_gather(sooner, LINE + PLANE, axis=0, tiled=True).reshape(2, 2, HALF, -1)
    later = lax.all_gather(later, LINE + PLANE, axis=0, tiled=True).reshape(2, 2, HALF, -1)

    def part(late, z, start, count):
        return jnp.concatenate([late[0, z, :, start : start + count], late[1, z, :, start : start + count]], 0)

    weights_a = [first, [part(sooner, z, PACK_B, PACK_A) for z in range(2)]]
    weights_b = [[part(late, z, 0, PACK_B) for z in range(2)] for late in (sooner, later)]

    def both_blocks(value):
        other = swapped(value, "zl", 2, 1)
        pair = jnp.where(zl == 0, jnp.stack([value, other]), jnp.stack([other, value]))
        return jnp.concatenate([pair[0], pair[1]], -1)

    def both_halves(value):
        other = swapped(value, "row", 2, 1)
        pair = jnp.where(row == 0, jnp.stack([value, other]), jnp.stack([other, value]))
        return jnp.concatenate([pair[0], pair[1]], -1)

    column_small = both_blocks(jnp.concatenate([bias_qv.reshape(2, 2 * BLOCK), bias_up], 1)).astype(f32)
    column_small = column_small.reshape(LAYERS, 2, 2 * BLOCK + HID)
    feature_small = jnp.concatenate([bias_out[:, None], bias_down[:, None], ln_gain, ln_shift], 1)
    feature_small = both_halves(feature_small).astype(f32)

    mates = [(2 * z + 1, 4 + 2 * z) for z in range(2)] + [(4 + 2 * z, 2 * z + 1) for z in range(2)]
    everywhere = ("row", "zl", "core")
    at_home = core == row
    entered = jnp.concatenate([act_in, cotangent], 0)
    mine = jnp.where(at_home, entered, lax.ppermute(entered, everywhere, mates))
    other = swapped(mine, "core", 2, 1)
    entered = jnp.where(core == 0, jnp.concatenate([mine, other], 1), jnp.concatenate([other, mine], 1))
    length = lengths[0]
    ones = jnp.arange(QUARTER, dtype=jnp.int32)
    key_at = jnp.concatenate([(2 * (zl ^ (s & 1)) + (row ^ (s >> 1))) * QUARTER + ones for s in (0, 1, 3, 2)])
    key_ok = key_at < length
    own_ok = ((2 * zl + row) * QUARTER + ones < length)[:, None]

    kept = []
    state = entered[:QUARTER].astype(f32)
    for l in range(LAYERS):
        wa, wb = weights_a[l], weights_b[l]
        gain = feature_small[l, 2:4]
        shift = feature_small[l, 4:6]
        low = state.astype(bf16)
        qkv = []
        for z in range(2):
            value = mm(low, wa[z][:, : 3 * BLOCK])
            bias = column_small[l, z]
            bias = jnp.concatenate([bias[:BLOCK], jnp.zeros((BLOCK,), f32), bias[BLOCK : 2 * BLOCK]])
            qkv.append((value + bias).astype(bf16))
        query = jnp.concatenate([qkv[0][:, :BLOCK], qkv[1][:, :BLOCK]], 1)
        key_value = jnp.concatenate(
            [qkv[z][:, s * BLOCK : (s + 1) * BLOCK] for s in (1, 2) for z in range(2)], 1
        )
        key_value = jnp.concatenate(gather(key_value, LINE), 0)
        keys, values = key_value[:, : 2 * BLOCK], key_value[:, 2 * BLOCK :]
        mixture, probs = attend_forward(query, keys, values, key_ok)
        mixture = mixture.astype(bf16)
        branch = sum(mt(mixture[:, z * BLOCK : (z + 1) * BLOCK], wa[z][:, 3 * BLOCK :]) for z in range(2))
        branch = core_sum(branch) + feature_small[l, 0]
        normed, unit_one, inverse_one = norm_forward(state + branch, gain[0], shift[0])
        mix_parts = [mixture[:, z * BLOCK : (z + 1) * BLOCK] for z in range(2)]
        normed_low = normed.astype(bf16)
        pre = [mm(normed_low, wb[z][:, :HID]) + column_small[l, z, 2 * BLOCK :] for z in range(2)]
        hidden = [gelu_exact(pre[z]).astype(bf16) for z in range(2)]
        branch = sum(mt(hidden[z], wb[z][:, HID:]) for z in range(2))
        branch = core_sum(branch) + feature_small[l, 1]
        state, unit_two, inverse_two = norm_forward(normed + branch, gain[1], shift[1])
        kept.append(
            (low, mix_parts, query, keys, values, probs, unit_one, inverse_one, normed_low, pre, hidden, unit_two, inverse_two)
        )

    def to_output(value):
        halves = (value[:, :HALF], value[:, HALF:])
        sent = jnp.where(row == 0, halves[1], halves[0])
        here = jnp.where(row == 0, halves[0], halves[1])
        return jnp.where(at_home, here, lax.ppermute(sent, everywhere, mates))

    output = to_output(jnp.where(own_ok, state, 0.0).astype(bf16))
    grad_state = jnp.where(own_ok, entered[QUARTER:].astype(f32), 0.0)
    wide = []
    narrow = [[], []]
    for l in range(LAYERS - 1, -1, -1):
        low, mix_parts, query, keys, values, probs, unit_one, inverse_one, normed_low, pre, hidden, unit_two, inverse_two = kept[l]
        wa, wb = weights_a[l], weights_b[l]
        gain = feature_small[l, 2:4]
        resid_two, gain_two, shift_two = norm_backward(grad_state, unit_two, inverse_two, gain[1])
        grad_low = resid_two.astype(bf16)
        down_bias = jnp.sum(grad_low, 0, dtype=f32)
        pre_grad = []
        for z in range(2):
            hidden_grad = mm(grad_low, wb[z][:, HID:])
            pre_grad.append(jax.vjp(gelu_exact, pre[z])[1](hidden_grad)[0].astype(bf16))
        up_bias = [jnp.sum(pre_grad[z], 0, dtype=f32) for z in range(2)]
        normed_grad = resid_two + core_sum(sum(mt(pre_grad[z], wb[z][:, :HID]) for z in range(2)))
        pieces = plane_pieces(weight_grad([(normed_low, pre_grad), (grad_low, hidden)]))
        if l == 1:
            one = plane_exchange(pieces)
        else:
            one = line_sum(one.reshape(4, 96, HALF).astype(bf16), place).astype(bf16)
            zero = plane_exchange(jnp.concatenate([pieces, one_a.astype(bf16).reshape(16, 48, HALF)], 1))
        resid_one, gain_one, shift_one = norm_backward(normed_grad, unit_one, inverse_one, gain[0])
        attn_low = resid_one.astype(bf16)
        out_bias = jnp.sum(attn_low, 0, dtype=f32)
        mixture_grad = jnp.concatenate([mm(attn_low, wa[z][:, 3 * BLOCK :]) for z in range(2)], 1).astype(bf16)
        query_grad, key_grad, value_grad = attend_backward(query, keys, values, probs, mixture_grad)
        key_value_grad = jnp.concatenate([key_grad, value_grad], 1).reshape(4, QUARTER, 4 * BLOCK)
        parts = [swapped(key_value_grad[i].astype(bf16), LINE, 4, bits) for i, bits in ((1, 1), (2, 3), (3, 2))]
        key_value_grad = key_value_grad[0] + sum(part.astype(f32) for part in parts)
        if l == 0:
            key_value_grad = key_value_grad + when(one)
            one = lax.all_gather(one, PLANE, axis=0, tiled=True)
        qkv_grad = []
        for z in range(2):
            cut = slice(z * BLOCK, (z + 1) * BLOCK)
            later = slice((z + 2) * BLOCK, (z + 3) * BLOCK)
            qkv_grad.append(
                jnp.concatenate([query_grad[:, cut], key_value_grad[:, cut], key_value_grad[:, later]], 1).astype(bf16)
            )
        qkv_bias = [jnp.sum(qkv_grad[z], 0, dtype=f32) for z in range(2)]
        grad_state = resid_one + core_sum(sum(mt(qkv_grad[z], wa[z][:, : 3 * BLOCK]) for z in range(2)))
        full_a = weight_grad([(low, qkv_grad), (attn_low, mix_parts)])
        if l == 1:
            one = plane_sum(one)
            grad_state = grad_state + when(one)
            one_a = line_sum(full_a.reshape(4, PACK_A, HALF), place)
        else:
            zero = plane_sum(zero) + when(one)
        wide += [out_bias, down_bias, gain_one, gain_two, shift_one, shift_two]
        narrow = [narrow[z] + [qkv_bias[z], up_bias[z]] for z in range(2)]

    grad_in = to_output(grad_state)

    wide = jnp.stack(wide) + when(zero)
    narrow = [jnp.concatenate(part) for part in narrow]
    small = jnp.stack(
        [jnp.concatenate([wide[:, (j // 2) * HALF : (j // 2 + 1) * HALF].reshape(-1), narrow[j % 2]]) for j in range(4)]
    )
    small = split3(small.reshape(4, 16, SMALL)).transpose(1, 2, 0, 3).reshape(4, 16, 3 * SMALL)
    small = jnp.pad(small, ((0, 0), (0, 0), (0, 8 * HALF - 3 * SMALL))).reshape(64, 8, HALF)
    moved = exchange(jnp.concatenate([full_a, small], 1))
    zero_b = line_sum(zero[:HALF].reshape(4, 96, HALF).astype(bf16), place).astype(bf16)
    own = jnp.sum(moved[:, 48:].reshape(64, 8 * HALF)[:, : 3 * SMALL].reshape(64 * 3, SMALL), 0, dtype=f32)
    own = jnp.pad(split3(own).reshape(-1), (0, 8 * HALF - 3 * SMALL)).reshape(8, HALF)
    zero = jnp.concatenate([zero_b, zero[HALF:].astype(bf16), jnp.sum(moved[:, :48], 0, dtype=f32).astype(bf16), own], 0)
    zero = jnp.stack(in_order(near_first(gather(zero, "y")), at_y))
    zero = jnp.stack(in_order(near_first(gather(zero, "x")), at_x)).reshape(16, 200, HALF)
    own = zero[:, 192:].reshape(16, 8 * HALF)[:, : 3 * SMALL].reshape(16, 3, SMALL).astype(f32)
    own = jnp.sum(own, 1).reshape(-1)
    wide = own[: 12 * HALF].reshape(LAYERS, 6, HALF)[::-1]
    own = own[12 * HALF :].reshape(LAYERS, 3 * BLOCK + HID)[::-1]
    grad_a = [zero[:, 144:192].reshape(PACK_A, HALF), zero[:, 96:144].reshape(PACK_A, HALF)]
    grad_b = [zero[:, :96].reshape(PACK_B, HALF), one.reshape(PACK_B, HALF)]

    def both(parts, turn):
        return jnp.stack([part.T if turn else part for part in parts]).astype(f32)

    return (
        output,
        grad_in,
        both([part[: 3 * BLOCK] for part in grad_a], True).reshape(LAYERS, HALF, 3, BLOCK),
        jnp.stack([own[:, :BLOCK], own[:, 2 * BLOCK : 3 * BLOCK]], 1),
        both([part[3 * BLOCK :] for part in grad_a], False),
        wide[:, 0],
        both([part[:HID] for part in grad_b], True),
        own[:, 3 * BLOCK :],
        both([part[HID:] for part in grad_b], False),
        wide[:, 1],
        wide[:, 2:4],
        wide[:, 4:6],
    )


def solution(mesh):
    fine = Mesh(mesh.devices.reshape(4, 4, 2, 2, 2), ("x", "y", "row", "zl", "core"))
    tokens = P(("x", "y", "zl", "core"), "row")
    col = ("zl", "core")
    in_specs = (
        tokens,
        tokens,
        P(("x", "y")),
        P(None, "row", None, col),
        P(None, None, col),
        P(None, col, "row"),
        P(None, "row"),
        P(None, "row", col),
        P(None, col),
        P(None, col, "row"),
        P(None, "row"),
        P(None, None, "row"),
        P(None, None, "row"),
    )
    out_specs = (tokens, tokens) + in_specs[3:8] + (in_specs[8],) + in_specs[9:11] + (in_specs[11], in_specs[12])
    return jax.shard_map(on_device, mesh=fine, in_specs=in_specs, out_specs=out_specs, check_vma=False)
```

time: 1430 us -> 555 us (0.39)
  blocking collectives: 508 us -> 0 us
  waiting for transfers between devices: 720 us -> 224 us
  starting transfers between devices: 1.38 us -> 85 us
  local copies, waits for them, and re-layouts: 22.7 us -> 59.2 us
    reduce_scatter x20 -> x0, waiting for transfers between devices: 544 us -> none  [the longest x4 177 us: sum_rows(): lax.psum_scatter(term(jnp.int32(0), lax.axis_size('row') * local_rows), '...]
    psum x10 -> x0, blocking collectives: 403 us -> none  [the longest x1 282 us: on_device(): lax.psum((jnp.stack(gain_parts), jnp.stack(shift_parts)), ('dp', 'col'))]
    ppermute x0 -> x44, waiting for transfers between devices: none -> 161 us  [the longest x41 161 us: swapped(): return lax.ppermute(value, axes, [(i, i ^ bits) for i in range(count)])]
    all_gather x6 -> x3, waiting for transfers between devices: 175 us -> 62.8 us  [the longest x1 43.1 us: on_device(): one = lax.all_gather(one, PLANE, axis=0, tiled=True)]
    all_gather x12 -> x0, blocking collectives: 105 us -> none  [the longest x4 32 us: gather_cols(): return lax.all_gather(value, 'col', axis=0, tiled=True)]
    ppermute x0 -> x44, starting transfers between devices: none -> 57.5 us  [the longest x41 54.7 us: swapped(): return lax.ppermute(value, axes, [(i, i ^ bits) for i in range(count)])]
    all_to_all x0 -> x3, starting transfers between devices: none -> 27.1 us  [the longest x2 14.3 us: plane_exchange(): return lax.all_to_all(pieces, PLANE, 0, 0, tiled=True)]
    convert_element_type x20 -> x16, other arithmetic: 35.2 us -> 13.3 us  [the longest x4 6.31 us: both(): return jnp.stack([part.T if turn else part for part in parts]).astype(f32)]
  transfers between devices with their start and end apart: 27 -> 50, of which waited for: 25 -> 28; matrix products, arithmetic and copies ran while one was open for 3% -> 25% of each run, Pallas kernels for 0% -> 0%
where the time goes in v1:
time: 555 us; the launch traced here: 545 us
  waiting for transfers between devices  224 us (40%)
  matrix products  89.7 us (16%)
  starting transfers between devices  85 us (15%)
  other arithmetic  66.9 us (12%)
  local copies, waits for them, and re-layouts  59.2 us (11%)
  between operations  20.3 us (4%)
    ppermute x41, waiting for transfers between devices, swapped(): return lax.ppermute(value, axes, [(i, i ^ bits) for i in range(count)])  161 us
    dot_general x64, matrix products, dot(): lax.dot_general(left, right, ((dims[0], dims[1]), ((), ())), preferred_el...  55.6 us
    ppermute x41, starting transfers between devices, swapped(): return lax.ppermute(value, axes, [(i, i ^ bits) for i in range(count)])  54.7 us
    all_gather x1, waiting for transfers between devices, on_device(): one = lax.all_gather(one, PLANE, axis=0, tiled=True)  43.1 us
    all_gather x1, waiting for transfers between devices, on_device(): lax.all_gather(later, LINE + PLANE, axis=0, tiled=True)  19.5 us
    unnamed x320, local copies, waits for them, and re-layouts  14.3 us
    all_to_all x2, starting transfers between devices, plane_exchange(): return lax.all_to_all(pieces, PLANE, 0, 0, tiled=True)  14.3 us
    all_to_all x1, starting transfers between devices, exchange(): return lax.all_to_all(pieces, LINE + PLANE, 0, 0, tiled=True)  12.8 us
  transfers between devices with their start and end apart: 50, of which 28 were waited for; matrix products, arithmetic and copies ran while one was open for 25% of the time, Pallas kernels for 0%

profile of v1, /device:TPU:0, one launch (start us, length us, event | category | flops | bytes accessed | tf_op | source)
XLA Modules:
  0.0 545.2 jit_solution(14613198119944877691)
XLA Ops:
  13.5 4.2 collective-permute-start.2
  25.2 21.6 %collective-permute-done.5 = bf16[2,1152]{1,0:T(2,128)(2,1)S(1)} collective-permute-done((bf16[2,1152]{1,0:T(2,128)(2,1)S(1)}, bf16[2,1152]{1,0:T(2,128)(2,1)S(1)}, u32[]{:S(2)}, u32[]{:S(2)}) %collective-permute-start.5) | collective-permute-done | bytes 4640 | tf_op jit(solution)/shard_map/ppermute | solution.py:30
  48.6 4.8 collective-permute-start.1
  57.3 2.8 collective-permute-start.8
  60.3 9.0 %collective-permute-done.6 = bf16[256,768]{0,1:T(8,128)(2,1)S(1)} collective-permute-done((bf16[256,768]{0,1:T(8,128)(2,1)S(1)}, bf16[256,768]{0,1:T(8,128)(2,1)S(1)}, u32[]{:S(2)}, u32[]{:S(2)}) %collective-permute-start.6) | collective-permute-done | bytes 393248 | tf_op jit(solution)/shard_map/ppermute | solution.py:30
  69.3 7.7 %collective-permute-done.7 = bf16[256,768]{0,1:T(8,128)(2,1)S(1)} collective-permute-done((bf16[256,768]{0,1:T(8,128)(2,1)S(1)}, bf16[256,768]{0,1:T(8,128)(2,1)S(1)}, u32[]{:S(2)}, u32[]{:S(2)}) %collective-permute-start.7) | collective-permute-done | bytes 393248 | tf_op jit(solution)/shard_map/ppermute | solution.py:30
  77.0 4.4 collective-permute-done.8
  85.0 4.8 fusion.249
  89.8 4.4 fusion.57
  100.8 3.1 multiply_convert_fusion.5
  104.7 3.1 multiply_convert_fusion.4
  117.3 8.0 %collective-permute-done.12 = bf16[256,768]{0,1:T(8,128)(2,1)S(1)} collective-permute-done((bf16[256,768]{0,1:T(8,128)(2,1)S(1)}, bf16[256,768]{0,1:T(8,128)(2,1)S(1)}, u32[]{:S(2)}, u32[]{:S(2)}) %collective-permute-start.12) | collective-permute-done | bytes 393248 | tf_op jit(solution)/shard_map/ppermute | solution.py:30
  125.2 9.3 %collective-permute-done.13 = bf16[256,768]{0,1:T(8,128)(2,1)S(1)} collective-permute-done((bf16[256,768]{0,1:T(8,128)(2,1)S(1)}, bf16[256,768]{0,1:T(8,128)(2,1)S(1)}, u32[]{:S(2)}, u32[]{:S(2)}) %collective-permute-start.13) | collective-permute-done | bytes 393248 | tf_op jit(solution)/shard_map/ppermute | solution.py:30
  139.1 6.5 %fusion.250 = (f32[6,256]{1,0:T(8,128)}, f32[6,256,1024]{2,1,0:T(8,128)}) fusion(pred[1024]{0:T(1024)(128)(4,1)} %copy-done.144, bf16[256,6,64]{0,2,1:T(8,128)(2,1)S(1)} %bitcast.315, bf16[1024,6,64]{0,2,1:T(8,128)(2,1)} %bitcast.296), kind=kOutput, calls=%fused_computation.589 | convolution fusion | flops 207619072 | bytes 7281664 | tf_op jit(solution)/shard_map/sub | solution.py:103
  145.6 4.1 fusion.60
  151.5 19.5 %all-gather.6.cloned.1.call-done = bf16[1536,1536]{1,0:T(8,128)(2,1)} async-done(((bf16[24,1536]{1,0:T(8,128)(2,1)}), bf16[1536,1536]{1,0:T(8,128)(2,1)}) %all-gather.6.cloned.1.call-update) | async-done | bytes 4718608 | tf_op jit(solution)/shard_map/all_gather | solution.py:178
  170.9 2.6 slice_bitcast_fusion
  177.0 3.1 multiply_convert_fusion.3
  180.8 3.1 multiply_convert_fusion.2
  193.4 3.0 convert_reduce_fusion.5
  198.4 3.0 convert_reduce_fusion.3
  206.2 2.9 copy.66
  209.1 5.0 all-to-all-start
  214.1 3.0 multiply_reduce_fusion.5
  219.6 3.9 multiply_reduce_fusion.1
  232.0 6.7 %collective-permute-done.19 = bf16[256,768]{0,1:T(8,128)(2,1)S(1)} collective-permute-done((bf16[256,768]{0,1:T(8,128)(2,1)S(1)}, bf16[256,768]{0,1:T(8,128)(2,1)S(1)}, u32[]{:S(2)}, u32[]{:S(2)}) %collective-permute-start.19) | collective-permute-done | bytes 393248 | tf_op jit(solution)/shard_map/ppermute | solution.py:30
  238.7 9.2 %collective-permute-done.20 = bf16[256,768]{0,1:T(8,128)(2,1)S(1)} collective-permute-done((bf16[256,768]{0,1:T(8,128)(2,1)S(1)}, bf16[256,768]{0,1:T(8,128)(2,1)S(1)}, u32[]{:S(2)}, u32[]{:S(2)}) %collective-permute-start.20) | collective-permute-done | bytes 393248 | tf_op jit(solution)/shard_map/ppermute | solution.py:30
  263.8 5.2 collective-permute-done.32
  269.0 10.3 %collective-permute-done.33 = bf16[768,384]{1,0:T(8,128)(2,1)} collective-permute-done((bf16[768,384]{1,0:T(8,128)(2,1)}, bf16[768,384]{1,0:T(8,128)(2,1)}, u32[]{:S(2)}, u32[]{:S(2)}) %collective-permute-start.33) | collective-permute-done | bytes 589856 | tf_op jit(solution)/shard_map/ppermute | solution.py:30
  283.8 3.1 convert_reduce_fusion.1
  292.3 3.0 convert_reduce_fusion.4
  297.6 3.0 convert_reduce_fusion.2
  309.6 2.8 pad_maximum_fusion
  312.4 9.3 %all-to-all-start.1 = ((bf16[16,432,384]{2,1,0:T(8,128)(2,1)}), bf16[16,432,384]{2,1,0:T(8,128)(2,1)}, u32[]{:S(2)}, u32[]{:S(2)}) async-start(bf16[16,432,384]{2,1,0:T(8,128)(2,1)} %pad_maximum_fusion), calls=%async_computation.1 | async-start | bytes 10616832 | tf_op jit(solution)/shard_map/all_to_all | solution.py:141
  331.4 4.1 multiply_reduce_fusion
  347.9 2.7 stack.191
  352.6 9.2 %collective-permute-done.25 = bf16[256,768]{0,1:T(8,128)(2,1)} collective-permute-done((bf16[256,768]{0,1:T(8,128)(2,1)}, bf16[256,768]{0,1:T(8,128)(2,1)}, u32[]{:S(2)}, u32[]{:S(2)}) %collective-permute-start.25) | collective-permute-done | bytes 393248 | tf_op jit(solution)/shard_map/ppermute | solution.py:30
  371.5 43.1 %all-gather.8.cloned.1.call-done = bf16[1536,384]{1,0:T(8,128)(2,1)} async-done(((bf16[96,384]{1,0:T(8,128)(2,1)}), bf16[1536,384]{1,0:T(8,128)(2,1)}) %all-gather.8.cloned.1.call-update) | async-done | bytes 1179664 | tf_op jit(solution)/shard_map/all_gather | solution.py:288
  416.5 3.4 convert_reduce_fusion
  422.6 3.5 pad_maximum_fusion.3
  426.1 12.8 %all-to-all-start.2 = ((bf16[64,56,384]{2,1,0:T(8,128)(2,1)}), bf16[64,56,384]{2,1,0:T(8,128)(2,1)}, u32[]{:S(2)}, u32[]{:S(2)}) async-start(bf16[64,56,384]{2,1,0:T(8,128)(2,1)} %pad_maximum_fusion.3), calls=%async_computation.2 | async-start | bytes 5505024 | tf_op jit(solution)/shard_map/all_to_all | solution.py:156
  445.0 4.1 collective-permute-start.36
  452.8 18.1 %collective-permute-done.35 = bf16[96,384]{1,0:T(8,128)(2,1)S(1)} collective-permute-done((bf16[96,384]{1,0:T(8,128)(2,1)S(1)}, bf16[96,384]{1,0:T(8,128)(2,1)S(1)}, u32[]{:S(2)}, u32[]{:S(2)}) %collective-permute-start.35) | collective-permute-done | bytes 73760 | tf_op jit(solution)/shard_map/ppermute | solution.py:30
  470.9 5.6 %collective-permute-done.36 = bf16[96,384]{1,0:T(8,128)(2,1)S(1)} collective-permute-done((bf16[96,384]{1,0:T(8,128)(2,1)S(1)}, bf16[96,384]{1,0:T(8,128)(2,1)S(1)}, u32[]{:S(2)}, u32[]{:S(2)}) %collective-permute-start.36) | collective-permute-done | bytes 73760 | tf_op jit(solution)/shard_map/ppermute | solution.py:30
  485.8 4.9 collective-permute-done.38
  491.6 2.9 collective-permute-start.41
  497.5 23.2 %collective-permute-done.41 = bf16[4,200,384]{2,1,0:T(8,128)(2,1)S(1)} collective-permute-done((bf16[4,200,384]{2,1,0:T(8,128)(2,1)S(1)}, bf16[4,200,384]{2,1,0:T(8,128)(2,1)S(1)}, u32[]{:S(2)}, u32[]{:S(2)}) %collective-permute-start.41) | collective-permute-done | bytes 614432 | tf_op jit(solution)/shard_map/ppermute | solution.py:30
  525.6 3.0 copy.70
  (650 shorter events, 184.9 us)
Async XLA Ops:
  7.2 90.9 %all-gather.4.cloned.1.call-start = ((), (), s32[]{:S(2)}) async-start(), calls=%async_computation.3 | async-start | bytes 7188480 | tf_op jit(solution)/shard_map/all_gather | solution.py:177
  13.3 157.6 %all-gather.6.cloned.1.call-start = ((), (), s32[]{:S(2)}) async-start(), calls=%async_computation.4 | async-start | bytes 4792320 | tf_op jit(solution)/shard_map/all_gather | solution.py:178
  13.5 39.9 %collective-permute-start.2 = (bf16[384,768]{0,1:T(8,128)(2,1)S(1)}, bf16[384,768]{0,1:T(8,128)(2,1)S(1)}, u32[]{:S(2)}, u32[]{:S(2)}) collective-permute-start(bf16[384,768]{0,1:T(8,128)(2,1)S(1)} %pad_maximum_fusion.12), channel_id=1, source_target_pairs={{0,6},{2,4},{4,2},{6,0},{1,7},{3,5},{5,3},{7,1},{8,14},{10,12},{12... | collective-permute-start | bytes 1769480 | tf_op jit(solution)/shard_map/ppermute | solution.py:30
  17.7 35.7 %collective-permute-start.3 = (bf16[384,768]{0,1:T(8,128)(2,1)S(1)}, bf16[384,768]{0,1:T(8,128)(2,1)S(1)}, u32[]{:S(2)}, u32[]{:S(2)}) collective-permute-start(bf16[384,768]{0,1:T(8,128)(2,1)S(1)} %pad_maximum_fusion.12), channel_id=1, source_target_pairs={{0,4},{2,6},{4,0},{6,2},{1,5},{3,7},{5,1},{7,3},{8,12},{10,14},{12... | collective-permute-start | bytes 1769480 | tf_op jit(solution)/shard_map/ppermute | solution.py:30
  17.7 35.7 %collective-permute-start.4 = (bf16[384,768]{0,1:T(8,128)(2,1)S(1)}, bf16[384,768]{0,1:T(8,128)(2,1)S(1)}, u32[]{:S(2)}, u32[]{:S(2)}) collective-permute-start(bf16[384,768]{0,1:T(8,128)(2,1)S(1)} %pad_maximum_fusion.12), channel_id=1, source_target_pairs={{0,2},{2,0},{4,6},{6,4},{1,3},{3,1},{5,7},{7,5},{8,10},{10,8},{12,... | collective-permute-start | bytes 1769480 | tf_op jit(solution)/shard_map/ppermute | solution.py:30
  18.8 28.0 %collective-permute-start.5 = (bf16[2,1152]{1,0:T(2,128)(2,1)S(1)}, bf16[2,1152]{1,0:T(2,128)(2,1)S(1)}, u32[]{:S(2)}, u32[]{:S(2)}) collective-permute-start(bf16[2,1152]{1,0:T(2,128)(2,1)S(1)} %constant_dynamic-update-slice_fusion.2), channel_id=1, source_target_pairs={{0,2},{2,0},{1,3},{3,1},{4,6},{6,4},{5,7},{7,5},{8,10},{10,8},{9,1... | collective-permute-start | bytes 13832 | tf_op jit(solution)/shard_map/ppermute | solution.py:30
  20.9 27.6 %collective-permute-start = (bf16[512,384]{1,0:T(8,128)(2,1)S(1)}, bf16[512,384]{1,0:T(8,128)(2,1)}, u32[]{:S(2)}, u32[]{:S(2)}) collective-permute-start(bf16[512,384]{1,0:T(8,128)(2,1)S(1)} %constant_dynamic-update-slice_fusion), channel_id=1, source_target_pairs={{1,4},{3,6},{4,1},{6,3},{9,12},{11,14},{12,9},{14,11},{17,20},{19,... | collective-permute-start | bytes 1179656 | tf_op jit(solution)/shard_map/ppermute | solution.py:205
  46.8 49.1 %collective-permute-start.10 = (bf16[2,6,384]{2,1,0:T(8,128)(2,1)S(1)}, bf16[2,6,384]{2,1,0:T(8,128)(2,1)S(1)}, u32[]{:S(2)}, u32[]{:S(2)}) collective-permute-start(bf16[2,6,384]{2,1,0:T(8,128)(2,1)S(1)} %get-tuple-element.222), channel_id=1, source_target_pairs={{0,4},{4,0},{1,5},{5,1},{2,6},{6,2},{3,7},{7,3},{8,12},{12,8},{9,1... | collective-permute-start | bytes 27656 | tf_op jit(solution)/shard_map/ppermute | solution.py:30
  48.6 6.1 %collective-permute-start.1 = (bf16[512,384]{1,0:T(8,128)(2,1)S(1)}, bf16[512,384]{1,0:T(8,128)(2,1)S(1)}, u32[]{:S(2)}, u32[]{:S(2)}) collective-permute-start(bf16[512,384]{1,0:T(8,128)(2,1)S(1)} %broadcast_select_fusion.12), channel_id=1, source_target_pairs={{0,1},{1,0},{2,3},{3,2},{4,5},{5,4},{6,7},{7,6},{8,9},{9,8},{10,11... | collective-permute-start | bytes 1179656 | tf_op jit(solution)/shard_map/ppermute | solution.py:30
  55.9 13.4 %collective-permute-start.6 = (bf16[256,768]{0,1:T(8,128)(2,1)S(1)}, bf16[256,768]{0,1:T(8,128)(2,1)S(1)}, u32[]{:S(2)}, u32[]{:S(2)}) collective-permute-start(bf16[256,768]{0,1:T(8,128)(2,1)S(1)} %pad_maximum_fusion.15), channel_id=1, source_target_pairs={{0,2},{2,0},{4,6},{6,4},{1,3},{3,1},{5,7},{7,5},{8,10},{10,8},{12,... | collective-permute-start | bytes 1179656 | tf_op jit(solution)/shard_map/ppermute | solution.py:30
  56.0 21.0 %collective-permute-start.7 = (bf16[256,768]{0,1:T(8,128)(2,1)S(1)}, bf16[256,768]{0,1:T(8,128)(2,1)S(1)}, u32[]{:S(2)}, u32[]{:S(2)}) collective-permute-start(bf16[256,768]{0,1:T(8,128)(2,1)S(1)} %pad_maximum_fusion.15), channel_id=1, source_target_pairs={{0,6},{2,4},{4,2},{6,0},{1,7},{3,5},{5,3},{7,1},{8,14},{10,12},{12... | collective-permute-start | bytes 1179656 | tf_op jit(solution)/shard_map/ppermute | solution.py:30
  57.3 24.1 %collective-permute-start.8 = (bf16[256,768]{0,1:T(8,128)(2,1)S(1)}, bf16[256,768]{0,1:T(8,128)(2,1)S(1)}, u32[]{:S(2)}, u32[]{:S(2)}) collective-permute-start(bf16[256,768]{0,1:T(8,128)(2,1)S(1)} %pad_maximum_fusion.15), channel_id=1, source_target_pairs={{0,4},{2,6},{4,0},{6,2},{1,5},{3,7},{5,1},{7,3},{8,12},{10,14},{12... | collective-permute-start | bytes 1179656 | tf_op jit(solution)/shard_map/ppermute | solution.py:30
  112.7 12.5 %collective-permute-start.12 = (bf16[256,768]{0,1:T(8,128)(2,1)S(1)}, bf16[256,768]{0,1:T(8,128)(2,1)S(1)}, u32[]{:S(2)}, u32[]{:S(2)}) collective-permute-start(bf16[256,768]{0,1:T(8,128)(2,1)S(1)} %pad_maximum_fusion.16), channel_id=1, source_target_pairs={{0,2},{2,0},{4,6},{6,4},{1,3},{3,1},{5,7},{7,5},{8,10},{10,8},{12,... | collective-permute-start | bytes 1179656 | tf_op jit(solution)/shard_map/ppermute | solution.py:30
  113.2 21.3 %collective-permute-start.13 = (bf16[256,768]{0,1:T(8,128)(2,1)S(1)}, bf16[256,768]{0,1:T(8,128)(2,1)S(1)}, u32[]{:S(2)}, u32[]{:S(2)}) collective-permute-start(bf16[256,768]{0,1:T(8,128)(2,1)S(1)} %pad_maximum_fusion.16), channel_id=1, source_target_pairs={{0,6},{2,4},{4,2},{6,0},{1,7},{3,5},{5,3},{7,1},{8,14},{10,12},{12... | collective-permute-start | bytes 1179656 | tf_op jit(solution)/shard_map/ppermute | solution.py:30
  115.7 19.6 %collective-permute-start.14 = (bf16[256,768]{0,1:T(8,128)(2,1)S(1)}, bf16[256,768]{0,1:T(8,128)(2,1)S(1)}, u32[]{:S(2)}, u32[]{:S(2)}) collective-permute-start(bf16[256,768]{0,1:T(8,128)(2,1)S(1)} %pad_maximum_fusion.16), channel_id=1, source_target_pairs={{0,4},{2,6},{4,0},{6,2},{1,5},{3,7},{5,1},{7,3},{8,12},{10,14},{12... | collective-permute-start | bytes 1179656 | tf_op jit(solution)/shard_map/ppermute | solution.py:30
  150.7 22.9 %collective-permute-start.15 = (f32[256,768]{1,0:T(8,128)S(1)}, f32[256,768]{1,0:T(8,128)S(1)}, u32[]{:S(2)}, u32[]{:S(2)}) collective-permute-start(f32[256,768]{1,0:T(8,128)S(1)} %convolution_add_fusion.7), channel_id=1, source_target_pairs={{0,1},{1,0},{2,3},{3,2},{4,5},{5,4},{6,7},{7,6},{8,9},{9,8},{10,11... | collective-permute-start | bytes 2359304 | tf_op jit(solution)/shard_map/ppermute | solution.py:30
  184.7 2.6 collective-permute-start.16
  202.7 11.4 %collective-permute-start.18 = (f32[256,768]{1,0:T(8,128)}, f32[256,768]{1,0:T(8,128)}, u32[]{:S(2)}, u32[]{:S(2)}) collective-permute-start(f32[256,768]{1,0:T(8,128)} %convolution_add_fusion.3), channel_id=1, source_target_pairs={{0,1},{1,0},{2,3},{3,2},{4,5},{5,4},{6,7},{7,6},{8,9},{9,8},{10,11... | collective-permute-start | bytes 2359304 | tf_op jit(solution)/shard_map/ppermute | solution.py:30
  209.1 74.7 %all-to-all-start = ((bf16[16,384,384]{2,1,0:T(8,128)(2,1)}), bf16[16,384,384]{2,1,0:T(8,128)(2,1)}, u32[]{:S(2)}, u32[]{:S(2)}) async-start(bf16[16,384,384]{2,1,0:T(8,128)(2,1)} %bitcast.269), calls=%async_computation | async-start | bytes 9437184 | tf_op jit(solution)/shard_map/all_to_all | solution.py:141
  226.7 12.0 %collective-permute-start.19 = (bf16[256,768]{0,1:T(8,128)(2,1)S(1)}, bf16[256,768]{0,1:T(8,128)(2,1)S(1)}, u32[]{:S(2)}, u32[]{:S(2)}) collective-permute-start(bf16[256,768]{0,1:T(8,128)(2,1)S(1)} %get-tuple-element.163), channel_id=1, source_target_pairs={{0,2},{2,0},{4,6},{6,4},{1,3},{3,1},{5,7},{7,5},{8,10},{10,8},{12,... | collective-permute-start | bytes 1179656 | tf_op jit(solution)/shard_map/ppermute | solution.py:30
  227.0 20.9 %collective-permute-start.20 = (bf16[256,768]{0,1:T(8,128)(2,1)S(1)}, bf16[256,768]{0,1:T(8,128)(2,1)S(1)}, u32[]{:S(2)}, u32[]{:S(2)}) collective-permute-start(bf16[256,768]{0,1:T(8,128)(2,1)S(1)} %get-tuple-element.165), channel_id=1, source_target_pairs={{0,6},{2,4},{4,2},{6,0},{1,7},{3,5},{5,3},{7,1},{8,14},{10,12},{12... | collective-permute-start | bytes 1179656 | tf_op jit(solution)/shard_map/ppermute | solution.py:30
  228.9 19.0 %collective-permute-start.21 = (bf16[256,768]{0,1:T(8,128)(2,1)S(1)}, bf16[256,768]{0,1:T(8,128)(2,1)S(1)}, u32[]{:S(2)}, u32[]{:S(2)}) collective-permute-start(bf16[256,768]{0,1:T(8,128)(2,1)S(1)} %get-tuple-element.164), channel_id=1, source_target_pairs={{0,4},{2,6},{4,0},{6,2},{1,5},{3,7},{5,1},{7,3},{8,12},{10,14},{12... | collective-permute-start | bytes 1179656 | tf_op jit(solution)/shard_map/ppermute | solution.py:30
  252.6 16.5 %collective-permute-start.32 = (bf16[768,384]{1,0:T(8,128)(2,1)}, bf16[768,384]{1,0:T(8,128)(2,1)S(1)}, u32[]{:S(2)}, u32[]{:S(2)}) collective-permute-start(bf16[768,384]{1,0:T(8,128)(2,1)} %get-tuple-element.153), channel_id=1, source_target_pairs={{0,2},{2,0},{4,6},{6,4},{1,3},{3,1},{5,7},{7,5},{8,10},{10,8},{12,... | collective-permute-start | bytes 1769480 | tf_op jit(solution)/shard_map/ppermute | solution.py:30
  253.0 26.4 %collective-permute-start.33 = (bf16[768,384]{1,0:T(8,128)(2,1)}, bf16[768,384]{1,0:T(8,128)(2,1)}, u32[]{:S(2)}, u32[]{:S(2)}) collective-permute-start(bf16[768,384]{1,0:T(8,128)(2,1)} %get-tuple-element.155), channel_id=1, source_target_pairs={{0,6},{2,4},{4,2},{6,0},{1,7},{3,5},{5,3},{7,1},{8,14},{10,12},{12... | collective-permute-start | bytes 1769480 | tf_op jit(solution)/shard_map/ppermute | solution.py:30
  254.3 27.0 %collective-permute-start.34 = (bf16[768,384]{1,0:T(8,128)(2,1)S(1)}, bf16[768,384]{1,0:T(8,128)(2,1)}, u32[]{:S(2)}, u32[]{:S(2)}) collective-permute-start(bf16[768,384]{1,0:T(8,128)(2,1)S(1)} %get-tuple-element.154), channel_id=1, source_target_pairs={{0,4},{2,6},{4,0},{6,2},{1,5},{3,7},{5,1},{7,3},{8,12},{10,14},{12... | collective-permute-start | bytes 1769480 | tf_op jit(solution)/shard_map/ppermute | solution.py:30
  258.7 29.4 %collective-permute-start.22 = (f32[256,768]{1,0:T(8,128)}, f32[256,768]{1,0:T(8,128)}, u32[]{:S(2)}, u32[]{:S(2)}) collective-permute-start(f32[256,768]{1,0:T(8,128)} %convolution_add_fusion.2), channel_id=1, source_target_pairs={{0,1},{1,0},{2,3},{3,2},{4,5},{5,4},{6,7},{7,6},{8,9},{9,8},{10,11... | collective-permute-start | bytes 2359304 | tf_op jit(solution)/shard_map/ppermute | solution.py:30
  303.4 23.8 %collective-permute-start.23 = (f32[256,768]{1,0:T(8,128)S(1)}, f32[256,768]{1,0:T(8,128)}, u32[]{:S(2)}, u32[]{:S(2)}) collective-permute-start(f32[256,768]{1,0:T(8,128)S(1)} %convolution_add_fusion.1), channel_id=1, source_target_pairs={{0,1},{1,0},{2,3},{3,2},{4,5},{5,4},{6,7},{7,6},{8,9},{9,8},{10,11... | collective-permute-start | bytes 2359304 | tf_op jit(solution)/shard_map/ppermute | solution.py:30
  305.5 18.3 %collective-permute-start.27 = (bf16[96,384]{1,0:T(8,128)(2,1)}, bf16[96,384]{1,0:T(8,128)(2,1)S(1)}, u32[]{:S(2)}, u32[]{:S(2)}) collective-permute-start(bf16[96,384]{1,0:T(8,128)(2,1)} %get-tuple-element.189), channel_id=1, source_target_pairs={{0,2},{2,0},{4,6},{6,4},{1,3},{3,1},{5,7},{7,5},{8,10},{10,8},{12,... | collective-permute-start | bytes 221192 | tf_op jit(solution)/shard_map/ppermute | solution.py:30
  305.7 18.1 %collective-permute-start.28 = (bf16[96,384]{1,0:T(8,128)(2,1)}, bf16[96,384]{1,0:T(8,128)(2,1)}, u32[]{:S(2)}, u32[]{:S(2)}) collective-permute-start(bf16[96,384]{1,0:T(8,128)(2,1)} %get-tuple-element.191), channel_id=1, source_target_pairs={{0,6},{2,4},{4,2},{6,0},{1,7},{3,5},{5,3},{7,1},{8,14},{10,12},{12... | collective-permute-start | bytes 221192 | tf_op jit(solution)/shard_map/ppermute | solution.py:30
  307.8 16.0 %collective-permute-start.29 = (bf16[96,384]{1,0:T(8,128)(2,1)S(1)}, bf16[96,384]{1,0:T(8,128)(2,1)}, u32[]{:S(2)}, u32[]{:S(2)}) collective-permute-start(bf16[96,384]{1,0:T(8,128)(2,1)S(1)} %get-tuple-element.190), channel_id=1, source_target_pairs={{0,4},{2,6},{4,0},{6,2},{1,5},{3,7},{5,1},{7,3},{8,12},{10,14},{12... | collective-permute-start | bytes 221192 | tf_op jit(solution)/shard_map/ppermute | solution.py:30
  312.4 104.1 %all-to-all-start.1 = ((bf16[16,432,384]{2,1,0:T(8,128)(2,1)}), bf16[16,432,384]{2,1,0:T(8,128)(2,1)}, u32[]{:S(2)}, u32[]{:S(2)}) async-start(bf16[16,432,384]{2,1,0:T(8,128)(2,1)} %pad_maximum_fusion), calls=%async_computation.1 | async-start | bytes 10616832 | tf_op jit(solution)/shard_map/all_to_all | solution.py:141
  321.7 92.9 %all-gather.8.cloned.1.call-start = ((), (), s32[]{:S(2)}) async-start(), calls=%async_computation.5 | async-start | bytes 1253376 | tf_op jit(solution)/shard_map/all_gather | solution.py:288
  340.3 12.3 %collective-permute-start.24 = (bf16[256,768]{0,1:T(8,128)(2,1)}, bf16[256,768]{0,1:T(8,128)(2,1)}, u32[]{:S(2)}, u32[]{:S(2)}) collective-permute-start(bf16[256,768]{0,1:T(8,128)(2,1)} %get-tuple-element.160), channel_id=1, source_target_pairs={{0,2},{2,0},{4,6},{6,4},{1,3},{3,1},{5,7},{7,5},{8,10},{10,8},{12,... | collective-permute-start | bytes 1179656 | tf_op jit(solution)/shard_map/ppermute | solution.py:30
  341.7 20.1 %collective-permute-start.25 = (bf16[256,768]{0,1:T(8,128)(2,1)}, bf16[256,768]{0,1:T(8,128)(2,1)}, u32[]{:S(2)}, u32[]{:S(2)}) collective-permute-start(bf16[256,768]{0,1:T(8,128)(2,1)} %get-tuple-element.162), channel_id=1, source_target_pairs={{0,6},{2,4},{4,2},{6,0},{1,7},{3,5},{5,3},{7,1},{8,14},{10,12},{12... | collective-permute-start | bytes 1179656 | tf_op jit(solution)/shard_map/ppermute | solution.py:30
  343.0 18.8 %collective-permute-start.26 = (bf16[256,768]{0,1:T(8,128)(2,1)}, bf16[256,768]{0,1:T(8,128)(2,1)}, u32[]{:S(2)}, u32[]{:S(2)}) collective-permute-start(bf16[256,768]{0,1:T(8,128)(2,1)} %get-tuple-element.161), channel_id=1, source_target_pairs={{0,4},{2,6},{4,0},{6,2},{1,5},{3,7},{5,1},{7,3},{8,12},{10,14},{12... | collective-permute-start | bytes 1179656 | tf_op jit(solution)/shard_map/ppermute | solution.py:30
  426.1 51.2 %all-to-all-start.2 = ((bf16[64,56,384]{2,1,0:T(8,128)(2,1)}), bf16[64,56,384]{2,1,0:T(8,128)(2,1)}, u32[]{:S(2)}, u32[]{:S(2)}) async-start(bf16[64,56,384]{2,1,0:T(8,128)(2,1)} %pad_maximum_fusion.3), calls=%async_computation.2 | async-start | bytes 5505024 | tf_op jit(solution)/shard_map/all_to_all | solution.py:156
  441.6 8.8 %collective-permute-start.30 = (f32[256,768]{1,0:T(8,128)}, f32[256,768]{1,0:T(8,128)S(1)}, u32[]{:S(2)}, u32[]{:S(2)}) collective-permute-start(f32[256,768]{1,0:T(8,128)} %convolution_add_fusion), channel_id=1, source_target_pairs={{0,1},{1,0},{2,3},{3,2},{4,5},{5,4},{6,7},{7,6},{8,9},{9,8},{10,11... | collective-permute-start | bytes 2359304 | tf_op jit(solution)/shard_map/ppermute | solution.py:30
  442.6 53.2 %collective-permute-start.17 = (bf16[256,384]{1,0:T(8,128)(2,1)}, bf16[256,384]{1,0:T(8,128)(2,1)S(1)}, u32[]{:S(2)}, u32[]{:S(2)}) collective-permute-start(bf16[256,384]{1,0:T(8,128)(2,1)} %broadcast_select_fusion.13), channel_id=1, source_target_pairs={{1,4},{3,6},{4,1},{6,3},{9,12},{11,14},{12,9},{14,11},{17,20},{19,... | collective-permute-start | bytes 589832 | tf_op jit(solution)/shard_map/ppermute | solution.py:253
  443.4 27.5 %collective-permute-start.35 = (bf16[96,384]{1,0:T(8,128)(2,1)S(1)}, bf16[96,384]{1,0:T(8,128)(2,1)S(1)}, u32[]{:S(2)}, u32[]{:S(2)}) collective-permute-start(bf16[96,384]{1,0:T(8,128)(2,1)S(1)} %get-tuple-element.186), channel_id=1, source_target_pairs={{0,2},{2,0},{4,6},{6,4},{1,3},{3,1},{5,7},{7,5},{8,10},{10,8},{12,... | collective-permute-start | bytes 221192 | tf_op jit(solution)/shard_map/ppermute | solution.py:30
  445.0 31.5 %collective-permute-start.36 = (bf16[96,384]{1,0:T(8,128)(2,1)S(1)}, bf16[96,384]{1,0:T(8,128)(2,1)S(1)}, u32[]{:S(2)}, u32[]{:S(2)}) collective-permute-start(bf16[96,384]{1,0:T(8,128)(2,1)S(1)} %get-tuple-element.188), channel_id=1, source_target_pairs={{0,6},{2,4},{4,2},{6,0},{1,7},{3,5},{5,3},{7,1},{8,14},{10,12},{12... | collective-permute-start | bytes 221192 | tf_op jit(solution)/shard_map/ppermute | solution.py:30
  449.0 28.2 %collective-permute-start.37 = (bf16[96,384]{1,0:T(8,128)(2,1)S(1)}, bf16[96,384]{1,0:T(8,128)(2,1)S(1)}, u32[]{:S(2)}, u32[]{:S(2)}) collective-permute-start(bf16[96,384]{1,0:T(8,128)(2,1)S(1)} %get-tuple-element.187), channel_id=1, source_target_pairs={{0,4},{2,6},{4,0},{6,2},{1,5},{3,7},{5,1},{7,3},{8,12},{10,14},{12... | collective-permute-start | bytes 221192 | tf_op jit(solution)/shard_map/ppermute | solution.py:30
  480.9 9.8 %collective-permute-start.38 = (bf16[200,384]{1,0:T(8,128)(2,1)S(1)}, bf16[200,384]{1,0:T(8,128)(2,1)S(1)}, u32[]{:S(2)}, u32[]{:S(2)}) collective-permute-start(bf16[200,384]{1,0:T(8,128)(2,1)S(1)} %pad_maximum_fusion.43), channel_id=1, source_target_pairs={{0,24},{8,16},{16,8},{24,0},{1,25},{9,17},{17,9},{25,1},{2,26},{10... | collective-permute-start | bytes 460808 | tf_op jit(solution)/shard_map/ppermute | solution.py:30
  481.9 8.8 %collective-permute-start.39 = (bf16[200,384]{1,0:T(8,128)(2,1)S(1)}, bf16[200,384]{1,0:T(8,128)(2,1)S(1)}, u32[]{:S(2)}, u32[]{:S(2)}) collective-permute-start(bf16[200,384]{1,0:T(8,128)(2,1)S(1)} %pad_maximum_fusion.43), channel_id=1, source_target_pairs={{0,16},{8,24},{16,0},{24,8},{1,17},{9,25},{17,1},{25,9},{2,18},{10... | collective-permute-start | bytes 460808 | tf_op jit(solution)/shard_map/ppermute | solution.py:30
  483.7 7.6 %collective-permute-start.40 = (bf16[200,384]{1,0:T(8,128)(2,1)S(1)}, bf16[200,384]{1,0:T(8,128)(2,1)S(1)}, u32[]{:S(2)}, u32[]{:S(2)}) collective-permute-start(bf16[200,384]{1,0:T(8,128)(2,1)S(1)} %pad_maximum_fusion.43), channel_id=1, source_target_pairs={{0,8},{8,0},{16,24},{24,16},{1,9},{9,1},{17,25},{25,17},{2,10},{10... | collective-permute-start | bytes 460808 | tf_op jit(solution)/shard_map/ppermute | solution.py:30
  485.1 11.6 %collective-permute-start.31 = (f32[256,384]{1,0:T(8,128)S(1)}, f32[256,384]{1,0:T(8,128)S(1)}, u32[]{:S(2)}, u32[]{:S(2)}) collective-permute-start(f32[256,384]{1,0:T(8,128)S(1)} %slice_select_fusion), channel_id=1, source_target_pairs={{1,4},{3,6},{4,1},{6,3},{9,12},{11,14},{12,9},{14,11},{17,20},{19,... | collective-permute-start | bytes 1179656 | tf_op jit(solution)/shard_map/ppermute | solution.py:253
  491.6 29.0 %collective-permute-start.41 = (bf16[4,200,384]{2,1,0:T(8,128)(2,1)S(1)}, bf16[4,200,384]{2,1,0:T(8,128)(2,1)S(1)}, u32[]{:S(2)}, u32[]{:S(2)}) collective-permute-start(bf16[4,200,384]{2,1,0:T(8,128)(2,1)S(1)} %pad_maximum_fusion.11), channel_id=1, source_target_pairs={{0,96},{32,64},{64,32},{96,0},{1,97},{33,65},{65,33},{97,1},{2,98}... | collective-permute-start | bytes 1843208 | tf_op jit(solution)/shard_map/ppermute | solution.py:30
  494.5 26.2 %collective-permute-start.42 = (bf16[4,200,384]{2,1,0:T(8,128)(2,1)S(1)}, bf16[4,200,384]{2,1,0:T(8,128)(2,1)S(1)}, u32[]{:S(2)}, u32[]{:S(2)}) collective-permute-start(bf16[4,200,384]{2,1,0:T(8,128)(2,1)S(1)} %pad_maximum_fusion.11), channel_id=1, source_target_pairs={{0,64},{32,96},{64,0},{96,32},{1,65},{33,97},{65,1},{97,33},{2,66}... | collective-permute-start | bytes 1843208 | tf_op jit(solution)/shard_map/ppermute | solution.py:30
  494.6 26.7 %collective-permute-start.43 = (bf16[4,200,384]{2,1,0:T(8,128)(2,1)S(1)}, bf16[4,200,384]{2,1,0:T(8,128)(2,1)S(1)}, u32[]{:S(2)}, u32[]{:S(2)}) collective-permute-start(bf16[4,200,384]{2,1,0:T(8,128)(2,1)S(1)} %pad_maximum_fusion.11), channel_id=1, source_target_pairs={{0,32},{32,0},{64,96},{96,64},{1,33},{33,1},{65,97},{97,65},{2,34}... | collective-permute-start | bytes 1843208 | tf_op jit(solution)/shard_map/ppermute | solution.py:30
  (155 other events, 1150.8 us)
Sparse Core Ops, SparseCore 0:
  13.4 84.6 all-gather.3
  101.4 69.4 all-gather.5
  325.5 89.0 all-gather.7

commit v2 on v1

--- a/solution.py
+++ b/solution.py
@@ -15,7 +15,7 @@
 HID = 768
 PACK_A = 768
 PACK_B = 1536
-SMALL = 456
+SMALL = 19
 
 EPSILON = 1e-05
 MASKED = -1000000000.0
@@ -150,10 +150,6 @@
     for bits in (1, 3, 2):
         total = total + swapped(piece_of(pieces, place ^ bits, 0), LINE, 4, bits).astype(f32)
     return total
-
-
-def exchange(pieces):
-    return lax.all_to_all(pieces, LINE + PLANE, 0, 0, tiled=True)
 
 
 def when(value):
@@ -301,30 +297,31 @@
             grad_state = grad_state + when(one)
             one_a = line_sum(full_a.reshape(4, PACK_A, HALF), place)
         else:
+            zero_a = line_sum(full_a.reshape(4, PACK_A, HALF), place)
             zero = plane_sum(zero) + when(one)
         wide += [out_bias, down_bias, gain_one, gain_two, shift_one, shift_two]
         narrow = [narrow[z] + [qkv_bias[z], up_bias[z]] for z in range(2)]
 
     grad_in = to_output(grad_state)
 
-    wide = jnp.stack(wide) + when(zero)
+    wide = jnp.stack(wide)
     narrow = [jnp.concatenate(part) for part in narrow]
     small = jnp.stack(
         [jnp.concatenate([wide[:, (j // 2) * HALF : (j // 2 + 1) * HALF].reshape(-1), narrow[j % 2]]) for j in range(4)]
     )
-    small = split3(small.reshape(4, 16, SMALL)).transpose(1, 2, 0, 3).reshape(4, 16, 3 * SMALL)
-    small = jnp.pad(small, ((0, 0), (0, 0), (0, 8 * HALF - 3 * SMALL))).reshape(64, 8, HALF)
-    moved = exchange(jnp.concatenate([full_a, small], 1))
+    small = split3(jnp.pad(line_sum(small.reshape(4, SMALL, HALF), place), ((0, 32 - SMALL), (0, 0))))
+    small = small.reshape(3, 16, 2, HALF).transpose(1, 0, 2, 3).reshape(16, 6, HALF)
+    zero_a = (zero_a + when(zero)).astype(bf16).reshape(16, 48, HALF)
+    moved = plane_exchange(jnp.concatenate([zero_a, small, jnp.zeros((16, 2, HALF), bf16)], 1))
     zero_b = line_sum(zero[:HALF].reshape(4, 96, HALF).astype(bf16), place).astype(bf16)
-    own = jnp.sum(moved[:, 48:].reshape(64, 8 * HALF)[:, : 3 * SMALL].reshape(64 * 3, SMALL), 0, dtype=f32)
-    own = jnp.pad(split3(own).reshape(-1), (0, 8 * HALF - 3 * SMALL)).reshape(8, HALF)
-    zero = jnp.concatenate([zero_b, zero[HALF:].astype(bf16), jnp.sum(moved[:, :48], 0, dtype=f32).astype(bf16), own], 0)
+    small = split3(jnp.sum(moved[:, 48:54].reshape(48, 2, HALF), 0, dtype=f32)).reshape(6, HALF)
+    zero_a = plane_sum(moved[:, :48]).astype(bf16)
+    zero = jnp.concatenate([zero_b, zero[HALF:].astype(bf16), zero_a, small, jnp.zeros((2, HALF), bf16)], 0)
     zero = jnp.stack(in_order(near_first(gather(zero, "y")), at_y))
     zero = jnp.stack(in_order(near_first(gather(zero, "x")), at_x)).reshape(16, 200, HALF)
-    own = zero[:, 192:].reshape(16, 8 * HALF)[:, : 3 * SMALL].reshape(16, 3, SMALL).astype(f32)
-    own = jnp.sum(own, 1).reshape(-1)
+    own = jnp.sum(zero[:, 192:198].reshape(16, 3, 2, HALF), 1, dtype=f32).reshape(32 * HALF)
     wide = own[: 12 * HALF].reshape(LAYERS, 6, HALF)[::-1]
-    own = own[12 * HALF :].reshape(LAYERS, 3 * BLOCK + HID)[::-1]
+    own = own[12 * HALF : SMALL * HALF].reshape(LAYERS, 3 * BLOCK + HID)[::-1]
     grad_a = [zero[:, 144:192].reshape(PACK_A, HALF), zero[:, 96:144].reshape(PACK_A, HALF)]
     grad_b = [zero[:, :96].reshape(PACK_B, HALF), one.reshape(PACK_B, HALF)]
 

time: 555 us -> 523 us (0.942)
  the two profiles are of different devices: /device:TPU:0 before, /device:TPU:32 now
where the time goes in v2:
time: 523 us; the launch traced here: 513 us
  waiting for transfers between devices  190 us (36%)
  starting transfers between devices  85.7 us (16%)
  matrix products  85 us (16%)
  local copies, waits for them, and re-layouts  72.8 us (14%)
  other arithmetic  59.8 us (11%)
  between operations  19.9 us (4%)
    ppermute x47, waiting for transfers between devices, swapped(): return lax.ppermute(value, axes, [(i, i ^ bits) for i in range(count)])  141 us
    ppermute x47, starting transfers between devices, swapped(): return lax.ppermute(value, axes, [(i, i ^ bits) for i in range(count)])  59.5 us
    dot_general x64, matrix products, dot(): lax.dot_general(left, right, ((dims[0], dims[1]), ((), ())), preferred_el...  50.3 us
    all_gather x1, waiting for transfers between devices, on_device(): one = lax.all_gather(one, PLANE, axis=0, tiled=True)  25.7 us
    all_to_all x3, starting transfers between devices, plane_exchange(): return lax.all_to_all(pieces, PLANE, 0, 0, tiled=True)  22 us
    all_gather x1, waiting for transfers between devices, on_device(): lax.all_gather(later, LINE + PLANE, axis=0, tiled=True)  19.5 us
    unnamed x314, local copies, waits for them, and re-layouts  17.7 us
    sub x2, matrix products, attend_forward(): raised = jnp.exp(scores - peak)  11.3 us
  transfers between devices with their start and end apart: 56, of which 25 were waited for; matrix products, arithmetic and copies ran while one was open for 31% of the time, Pallas kernels for 0%

profile of v2, /device:TPU:32, one launch (start us, length us, event | category | flops | bytes accessed | tf_op | source)
XLA Modules:
  0.0 513.3 jit_solution(79390646768094843)
XLA Ops:
  24.1 21.7 %collective-permute-done.5 = bf16[2,1152]{1,0:T(2,128)(2,1)S(1)} collective-permute-done((bf16[2,1152]{1,0:T(2,128)(2,1)S(1)}, bf16[2,1152]{1,0:T(2,128)(2,1)S(1)}, u32[]{:S(2)}, u32[]{:S(2)}) %collective-permute-start.5) | collective-permute-done | bytes 4640 | tf_op jit(solution)/shard_map/ppermute | solution.py:30
  47.6 3.6 collective-permute-start.1
  58.4 9.2 %collective-permute-done.6 = bf16[256,768]{0,1:T(8,128)(2,1)S(1)} collective-permute-done((bf16[256,768]{0,1:T(8,128)(2,1)S(1)}, bf16[256,768]{0,1:T(8,128)(2,1)S(1)}, u32[]{:S(2)}, u32[]{:S(2)}) %collective-permute-start.6) | collective-permute-done | bytes 393248 | tf_op jit(solution)/shard_map/ppermute | solution.py:30
  67.6 8.2 %collective-permute-done.7 = bf16[256,768]{0,1:T(8,128)(2,1)S(1)} collective-permute-done((bf16[256,768]{0,1:T(8,128)(2,1)S(1)}, bf16[256,768]{0,1:T(8,128)(2,1)S(1)}, u32[]{:S(2)}, u32[]{:S(2)}) %collective-permute-start.7) | collective-permute-done | bytes 393248 | tf_op jit(solution)/shard_map/ppermute | solution.py:30
  75.8 3.9 collective-permute-done.8
  83.2 4.8 fusion.255
  88.1 4.4 fusion.61
  96.5 2.6 slice_bitcast_fusion.4
  99.2 3.1 multiply_convert_fusion.5
  102.9 3.1 multiply_convert_fusion.4
  115.5 8.0 %collective-permute-done.12 = bf16[256,768]{0,1:T(8,128)(2,1)S(1)} collective-permute-done((bf16[256,768]{0,1:T(8,128)(2,1)S(1)}, bf16[256,768]{0,1:T(8,128)(2,1)S(1)}, u32[]{:S(2)}, u32[]{:S(2)}) %collective-permute-start.12) | collective-permute-done | bytes 393248 | tf_op jit(solution)/shard_map/ppermute | solution.py:30
  123.5 9.9 %collective-permute-done.13 = bf16[256,768]{0,1:T(8,128)(2,1)S(1)} collective-permute-done((bf16[256,768]{0,1:T(8,128)(2,1)S(1)}, bf16[256,768]{0,1:T(8,128)(2,1)S(1)}, u32[]{:S(2)}, u32[]{:S(2)}) %collective-permute-start.13) | collective-permute-done | bytes 393248 | tf_op jit(solution)/shard_map/ppermute | solution.py:30
  133.4 2.6 pad_maximum_fusion.5
  137.3 6.4 %fusion.256 = (f32[6,256]{1,0:T(8,128)}, f32[6,256,1024]{2,1,0:T(8,128)}) fusion(pred[1024]{0:T(1024)(128)(4,1)} %copy-done.141, bf16[256,6,64]{0,2,1:T(8,128)(2,1)S(1)} %bitcast.338, bf16[1024,6,64]{0,2,1:T(8,128)(2,1)} %bitcast.320), kind=kOutput, calls=%fused_computation.601 | convolution fusion | flops 207619072 | bytes 7281664 | tf_op jit(solution)/shard_map/sub | solution.py:103
  143.7 4.1 fusion.64
  149.6 19.5 %all-gather.6.cloned.1.call-done = bf16[1536,1536]{1,0:T(8,128)(2,1)} async-done(((bf16[24,1536]{1,0:T(8,128)(2,1)}), bf16[1536,1536]{1,0:T(8,128)(2,1)}) %all-gather.6.cloned.1.call-update) | async-done | bytes 4718608 | tf_op jit(solution)/shard_map/all_gather | solution.py:174
  169.2 2.6 slice_bitcast_fusion
  175.2 3.2 multiply_convert_fusion.3
  179.0 3.1 multiply_convert_fusion.2
  191.5 3.0 convert_reduce_fusion.5
  196.5 3.0 convert_reduce_fusion.3
  204.3 2.9 copy.93
  207.2 4.9 all-to-all-start
  218.8 3.8 multiply_reduce_fusion.1
  231.2 6.7 %collective-permute-done.19 = bf16[256,768]{0,1:T(8,128)(2,1)S(1)} collective-permute-done((bf16[256,768]{0,1:T(8,128)(2,1)S(1)}, bf16[256,768]{0,1:T(8,128)(2,1)S(1)}, u32[]{:S(2)}, u32[]{:S(2)}) %collective-permute-start.19) | collective-permute-done | bytes 393248 | tf_op jit(solution)/shard_map/ppermute | solution.py:30
  237.9 9.5 %collective-permute-done.20 = bf16[256,768]{0,1:T(8,128)(2,1)S(1)} collective-permute-done((bf16[256,768]{0,1:T(8,128)(2,1)S(1)}, bf16[256,768]{0,1:T(8,128)(2,1)S(1)}, u32[]{:S(2)}, u32[]{:S(2)}) %collective-permute-start.20) | collective-permute-done | bytes 393248 | tf_op jit(solution)/shard_map/ppermute | solution.py:30
  261.5 5.6 %collective-permute-done.32 = bf16[768,384]{1,0:T(8,128)(2,1)S(1)} collective-permute-done((bf16[768,384]{1,0:T(8,128)(2,1)S(1)}, bf16[768,384]{1,0:T(8,128)(2,1)S(1)}, u32[]{:S(2)}, u32[]{:S(2)}) %collective-permute-start.32) | collective-permute-done | bytes 589856 | tf_op jit(solution)/shard_map/ppermute | solution.py:30
  267.1 14.0 %collective-permute-done.33 = bf16[768,384]{1,0:T(8,128)(2,1)S(1)} collective-permute-done((bf16[768,384]{1,0:T(8,128)(2,1)S(1)}, bf16[768,384]{1,0:T(8,128)(2,1)S(1)}, u32[]{:S(2)}, u32[]{:S(2)}) %collective-permute-start.33) | collective-permute-done | bytes 589856 | tf_op jit(solution)/shard_map/ppermute | solution.py:30
  282.3 3.1 convert_reduce_fusion.1
  290.8 3.0 convert_reduce_fusion.4
  295.8 3.0 convert_reduce_fusion.2
  300.0 3.0 collective-permute-start.28
  308.5 2.8 pad_maximum_fusion
  311.4 8.6 %all-to-all-start.1 = ((bf16[16,432,384]{2,1,0:T(8,128)(2,1)}), bf16[16,432,384]{2,1,0:T(8,128)(2,1)}, u32[]{:S(2)}, u32[]{:S(2)}) async-start(bf16[16,432,384]{2,1,0:T(8,128)(2,1)} %pad_maximum_fusion), calls=%async_computation.1 | async-start | bytes 10616832 | tf_op jit(solution)/shard_map/all_to_all | solution.py:141
  328.6 3.7 multiply_reduce_fusion
  343.6 2.7 stack.196
  346.3 2.9 fusion.60
  350.2 8.1 %collective-permute-done.25 = bf16[256,768]{0,1:T(8,128)(2,1)} collective-permute-done((bf16[256,768]{0,1:T(8,128)(2,1)}, bf16[256,768]{0,1:T(8,128)(2,1)}, u32[]{:S(2)}, u32[]{:S(2)}) %collective-permute-start.25) | collective-permute-done | bytes 393248 | tf_op jit(solution)/shard_map/ppermute | solution.py:30
  380.8 3.0 collective-permute-done.41
  384.4 3.2 collective-permute-start.40
  388.1 25.7 %all-gather.8.cloned.1.call-done = bf16[1536,384]{1,0:T(8,128)(2,1)} async-done(((bf16[96,384]{1,0:T(8,128)(2,1)}), bf16[1536,384]{1,0:T(8,128)(2,1)}) %all-gather.8.cloned.1.call-update) | async-done | bytes 1179664 | tf_op jit(solution)/shard_map/all_gather | solution.py:284
  415.7 3.4 convert_reduce_fusion
  424.2 8.5 %all-to-all-start.2 = ((bf16[16,56,384]{2,1,0:T(8,128)(2,1)}), bf16[16,56,384]{2,1,0:T(8,128)(2,1)S(1)}, u32[]{:S(2)}, u32[]{:S(2)}) async-start(bf16[16,56,384]{2,1,0:T(8,128)(2,1)} %maximum_maximum_fusion), calls=%async_computation.2 | async-start | bytes 1376256 | tf_op jit(solution)/shard_map/all_to_all | solution.py:141
  432.9 3.4 collective-permute-start.36
  439.4 2.7 collective-permute-done.37
  442.2 2.9 all-to-all-done.2
  450.4 3.2 collective-permute-done.44
  461.6 23.3 %collective-permute-done.47 = bf16[4,200,384]{2,1,0:T(8,128)(2,1)S(1)} collective-permute-done((bf16[4,200,384]{2,1,0:T(8,128)(2,1)S(1)}, bf16[4,200,384]{2,1,0:T(8,128)(2,1)S(1)}, u32[]{:S(2)}, u32[]{:S(2)}) %collective-permute-start.47) | collective-permute-done | bytes 614432 | tf_op jit(solution)/shard_map/ppermute | solution.py:30
  (660 shorter events, 195.6 us)
Async XLA Ops:
  7.2 89.3 %all-gather.4.cloned.1.call-start = ((), (), s32[]{:S(2)}) async-start(), calls=%async_computation.3 | async-start | bytes 7188480 | tf_op jit(solution)/shard_map/all_gather | solution.py:173
  13.3 155.8 %all-gather.6.cloned.1.call-start = ((), (), s32[]{:S(2)}) async-start(), calls=%async_computation.4 | async-start | bytes 4792320 | tf_op jit(solution)/shard_map/all_gather | solution.py:174
  13.5 37.7 %collective-permute-start.2 = (bf16[384,768]{0,1:T(8,128)(2,1)S(1)}, bf16[384,768]{0,1:T(8,128)(2,1)S(1)}, u32[]{:S(2)}, u32[]{:S(2)}) collective-permute-start(bf16[384,768]{0,1:T(8,128)(2,1)S(1)} %pad_maximum_fusion.11), channel_id=1, source_target_pairs={{0,6},{2,4},{4,2},{6,0},{1,7},{3,5},{5,3},{7,1},{8,14},{10,12},{12... | collective-permute-start | bytes 1769480 | tf_op jit(solution)/shard_map/ppermute | solution.py:30
  15.5 35.7 %collective-permute-start.3 = (bf16[384,768]{0,1:T(8,128)(2,1)S(1)}, bf16[384,768]{0,1:T(8,128)(2,1)S(1)}, u32[]{:S(2)}, u32[]{:S(2)}) collective-permute-start(bf16[384,768]{0,1:T(8,128)(2,1)S(1)} %pad_maximum_fusion.11), channel_id=1, source_target_pairs={{0,4},{2,6},{4,0},{6,2},{1,5},{3,7},{5,1},{7,3},{8,12},{10,14},{12... | collective-permute-start | bytes 1769480 | tf_op jit(solution)/shard_map/ppermute | solution.py:30
  16.7 34.6 %collective-permute-start.4 = (bf16[384,768]{0,1:T(8,128)(2,1)S(1)}, bf16[384,768]{0,1:T(8,128)(2,1)S(1)}, u32[]{:S(2)}, u32[]{:S(2)}) collective-permute-start(bf16[384,768]{0,1:T(8,128)(2,1)S(1)} %pad_maximum_fusion.11), channel_id=1, source_target_pairs={{0,2},{2,0},{4,6},{6,4},{1,3},{3,1},{5,7},{7,5},{8,10},{10,8},{12,... | collective-permute-start | bytes 1769480 | tf_op jit(solution)/shard_map/ppermute | solution.py:30
  17.9 28.0 %collective-permute-start.5 = (bf16[2,1152]{1,0:T(2,128)(2,1)S(1)}, bf16[2,1152]{1,0:T(2,128)(2,1)S(1)}, u32[]{:S(2)}, u32[]{:S(2)}) collective-permute-start(bf16[2,1152]{1,0:T(2,128)(2,1)S(1)} %constant_dynamic-update-slice_fusion.2), channel_id=1, source_target_pairs={{0,2},{2,0},{1,3},{3,1},{4,6},{6,4},{5,7},{7,5},{8,10},{10,8},{9,1... | collective-permute-start | bytes 13832 | tf_op jit(solution)/shard_map/ppermute | solution.py:30
  19.9 27.7 %collective-permute-start = (bf16[512,384]{1,0:T(8,128)(2,1)S(1)}, bf16[512,384]{1,0:T(8,128)(2,1)}, u32[]{:S(2)}, u32[]{:S(2)}) collective-permute-start(bf16[512,384]{1,0:T(8,128)(2,1)S(1)} %constant_dynamic-update-slice_fusion), channel_id=1, source_target_pairs={{1,4},{3,6},{4,1},{6,3},{9,12},{11,14},{12,9},{14,11},{17,20},{19,... | collective-permute-start | bytes 1179656 | tf_op jit(solution)/shard_map/ppermute | solution.py:201
  45.9 48.3 %collective-permute-start.10 = (bf16[2,6,384]{2,1,0:T(8,128)(2,1)S(1)}, bf16[2,6,384]{2,1,0:T(8,128)(2,1)S(1)}, u32[]{:S(2)}, u32[]{:S(2)}) collective-permute-start(bf16[2,6,384]{2,1,0:T(8,128)(2,1)S(1)} %get-tuple-element.241), channel_id=1, source_target_pairs={{0,4},{4,0},{1,5},{5,1},{2,6},{6,2},{3,7},{7,3},{8,12},{12,8},{9,1... | collective-permute-start | bytes 27656 | tf_op jit(solution)/shard_map/ppermute | solution.py:30
  53.7 13.9 %collective-permute-start.6 = (bf16[256,768]{0,1:T(8,128)(2,1)S(1)}, bf16[256,768]{0,1:T(8,128)(2,1)S(1)}, u32[]{:S(2)}, u32[]{:S(2)}) collective-permute-start(bf16[256,768]{0,1:T(8,128)(2,1)S(1)} %pad_maximum_fusion.14), channel_id=1, source_target_pairs={{0,2},{2,0},{4,6},{6,4},{1,3},{3,1},{5,7},{7,5},{8,10},{10,8},{12,... | collective-permute-start | bytes 1179656 | tf_op jit(solution)/shard_map/ppermute | solution.py:30
  56.0 19.7 %collective-permute-start.7 = (bf16[256,768]{0,1:T(8,128)(2,1)S(1)}, bf16[256,768]{0,1:T(8,128)(2,1)S(1)}, u32[]{:S(2)}, u32[]{:S(2)}) collective-permute-start(bf16[256,768]{0,1:T(8,128)(2,1)S(1)} %pad_maximum_fusion.14), channel_id=1, source_target_pairs={{0,6},{2,4},{4,2},{6,0},{1,7},{3,5},{5,3},{7,1},{8,14},{10,12},{12... | collective-permute-start | bytes 1179656 | tf_op jit(solution)/shard_map/ppermute | solution.py:30
  56.2 23.5 %collective-permute-start.8 = (bf16[256,768]{0,1:T(8,128)(2,1)S(1)}, bf16[256,768]{0,1:T(8,128)(2,1)S(1)}, u32[]{:S(2)}, u32[]{:S(2)}) collective-permute-start(bf16[256,768]{0,1:T(8,128)(2,1)S(1)} %pad_maximum_fusion.14), channel_id=1, source_target_pairs={{0,4},{2,6},{4,0},{6,2},{1,5},{3,7},{5,1},{7,3},{8,12},{10,14},{12... | collective-permute-start | bytes 1179656 | tf_op jit(solution)/shard_map/ppermute | solution.py:30
  111.0 12.6 %collective-permute-start.12 = (bf16[256,768]{0,1:T(8,128)(2,1)S(1)}, bf16[256,768]{0,1:T(8,128)(2,1)S(1)}, u32[]{:S(2)}, u32[]{:S(2)}) collective-permute-start(bf16[256,768]{0,1:T(8,128)(2,1)S(1)} %pad_maximum_fusion.15), channel_id=1, source_target_pairs={{0,2},{2,0},{4,6},{6,4},{1,3},{3,1},{5,7},{7,5},{8,10},{10,8},{12,... | collective-permute-start | bytes 1179656 | tf_op jit(solution)/shard_map/ppermute | solution.py:30
  112.7 20.8 %collective-permute-start.13 = (bf16[256,768]{0,1:T(8,128)(2,1)S(1)}, bf16[256,768]{0,1:T(8,128)(2,1)S(1)}, u32[]{:S(2)}, u32[]{:S(2)}) collective-permute-start(bf16[256,768]{0,1:T(8,128)(2,1)S(1)} %pad_maximum_fusion.15), channel_id=1, source_target_pairs={{0,6},{2,4},{4,2},{6,0},{1,7},{3,5},{5,3},{7,1},{8,14},{10,12},{12... | collective-permute-start | bytes 1179656 | tf_op jit(solution)/shard_map/ppermute | solution.py:30
  114.9 18.6 %collective-permute-start.14 = (bf16[256,768]{0,1:T(8,128)(2,1)S(1)}, bf16[256,768]{0,1:T(8,128)(2,1)S(1)}, u32[]{:S(2)}, u32[]{:S(2)}) collective-permute-start(bf16[256,768]{0,1:T(8,128)(2,1)S(1)} %pad_maximum_fusion.15), channel_id=1, source_target_pairs={{0,4},{2,6},{4,0},{6,2},{1,5},{3,7},{5,1},{7,3},{8,12},{10,14},{12... | collective-permute-start | bytes 1179656 | tf_op jit(solution)/shard_map/ppermute | solution.py:30
  148.9 23.0 %collective-permute-start.15 = (f32[256,768]{1,0:T(8,128)S(1)}, f32[256,768]{1,0:T(8,128)S(1)}, u32[]{:S(2)}, u32[]{:S(2)}) collective-permute-start(f32[256,768]{1,0:T(8,128)S(1)} %convolution_add_fusion.7), channel_id=1, source_target_pairs={{0,1},{1,0},{2,3},{3,2},{4,5},{5,4},{6,7},{7,6},{8,9},{9,8},{10,11... | collective-permute-start | bytes 2359304 | tf_op jit(solution)/shard_map/ppermute | solution.py:30
  200.9 13.1 %collective-permute-start.18 = (f32[256,768]{1,0:T(8,128)}, f32[256,768]{1,0:T(8,128)}, u32[]{:S(2)}, u32[]{:S(2)}) collective-permute-start(f32[256,768]{1,0:T(8,128)} %convolution_add_fusion.3), channel_id=1, source_target_pairs={{0,1},{1,0},{2,3},{3,2},{4,5},{5,4},{6,7},{7,6},{8,9},{9,8},{10,11... | collective-permute-start | bytes 2359304 | tf_op jit(solution)/shard_map/ppermute | solution.py:30
  207.2 75.1 %all-to-all-start = ((bf16[16,384,384]{2,1,0:T(8,128)(2,1)}), bf16[16,384,384]{2,1,0:T(8,128)(2,1)}, u32[]{:S(2)}, u32[]{:S(2)}) async-start(bf16[16,384,384]{2,1,0:T(8,128)(2,1)} %bitcast.293), calls=%async_computation | async-start | bytes 9437184 | tf_op jit(solution)/shard_map/all_to_all | solution.py:141
  225.9 12.0 %collective-permute-start.19 = (bf16[256,768]{0,1:T(8,128)(2,1)S(1)}, bf16[256,768]{0,1:T(8,128)(2,1)S(1)}, u32[]{:S(2)}, u32[]{:S(2)}) collective-permute-start(bf16[256,768]{0,1:T(8,128)(2,1)S(1)} %get-tuple-element.178), channel_id=1, source_target_pairs={{0,2},{2,0},{4,6},{6,4},{1,3},{3,1},{5,7},{7,5},{8,10},{10,8},{12,... | collective-permute-start | bytes 1179656 | tf_op jit(solution)/shard_map/ppermute | solution.py:30
  227.8 19.5 %collective-permute-start.20 = (bf16[256,768]{0,1:T(8,128)(2,1)S(1)}, bf16[256,768]{0,1:T(8,128)(2,1)S(1)}, u32[]{:S(2)}, u32[]{:S(2)}) collective-permute-start(bf16[256,768]{0,1:T(8,128)(2,1)S(1)} %get-tuple-element.180), channel_id=1, source_target_pairs={{0,6},{2,4},{4,2},{6,0},{1,7},{3,5},{5,3},{7,1},{8,14},{10,12},{12... | collective-permute-start | bytes 1179656 | tf_op jit(solution)/shard_map/ppermute | solution.py:30
  228.6 18.7 %collective-permute-start.21 = (bf16[256,768]{0,1:T(8,128)(2,1)S(1)}, bf16[256,768]{0,1:T(8,128)(2,1)S(1)}, u32[]{:S(2)}, u32[]{:S(2)}) collective-permute-start(bf16[256,768]{0,1:T(8,128)(2,1)S(1)} %get-tuple-element.179), channel_id=1, source_target_pairs={{0,4},{2,6},{4,0},{6,2},{1,5},{3,7},{5,1},{7,3},{8,12},{10,14},{12... | collective-permute-start | bytes 1179656 | tf_op jit(solution)/shard_map/ppermute | solution.py:30
  250.8 16.3 %collective-permute-start.32 = (bf16[768,384]{1,0:T(8,128)(2,1)S(1)}, bf16[768,384]{1,0:T(8,128)(2,1)S(1)}, u32[]{:S(2)}, u32[]{:S(2)}) collective-permute-start(bf16[768,384]{1,0:T(8,128)(2,1)S(1)} %get-tuple-element.168), channel_id=1, source_target_pairs={{0,2},{2,0},{4,6},{6,4},{1,3},{3,1},{5,7},{7,5},{8,10},{10,8},{12,... | collective-permute-start | bytes 1769480 | tf_op jit(solution)/shard_map/ppermute | solution.py:30
  252.5 28.7 %collective-permute-start.33 = (bf16[768,384]{1,0:T(8,128)(2,1)S(1)}, bf16[768,384]{1,0:T(8,128)(2,1)S(1)}, u32[]{:S(2)}, u32[]{:S(2)}) collective-permute-start(bf16[768,384]{1,0:T(8,128)(2,1)S(1)} %get-tuple-element.170), channel_id=1, source_target_pairs={{0,6},{2,4},{4,2},{6,0},{1,7},{3,5},{5,3},{7,1},{8,14},{10,12},{12... | collective-permute-start | bytes 1769480 | tf_op jit(solution)/shard_map/ppermute | solution.py:30
  253.5 27.7 %collective-permute-start.34 = (bf16[768,384]{1,0:T(8,128)(2,1)S(1)}, bf16[768,384]{1,0:T(8,128)(2,1)S(1)}, u32[]{:S(2)}, u32[]{:S(2)}) collective-permute-start(bf16[768,384]{1,0:T(8,128)(2,1)S(1)} %get-tuple-element.169), channel_id=1, source_target_pairs={{0,4},{2,6},{4,0},{6,2},{1,5},{3,7},{5,1},{7,3},{8,12},{10,14},{12... | collective-permute-start | bytes 1769480 | tf_op jit(solution)/shard_map/ppermute | solution.py:30
  256.9 29.7 %collective-permute-start.22 = (f32[256,768]{1,0:T(8,128)}, f32[256,768]{1,0:T(8,128)}, u32[]{:S(2)}, u32[]{:S(2)}) collective-permute-start(f32[256,768]{1,0:T(8,128)} %convolution_add_fusion.2), channel_id=1, source_target_pairs={{0,1},{1,0},{2,3},{3,2},{4,5},{5,4},{6,7},{7,6},{8,9},{9,8},{10,11... | collective-permute-start | bytes 2359304 | tf_op jit(solution)/shard_map/ppermute | solution.py:30
  259.4 199.5 %collective-permute-start.17 = (bf16[256,384]{1,0:T(8,128)(2,1)}, bf16[256,384]{1,0:T(8,128)(2,1)}, u32[]{:S(2)}, u32[]{:S(2)}) collective-permute-start(bf16[256,384]{1,0:T(8,128)(2,1)} %broadcast_select_fusion.13), channel_id=1, source_target_pairs={{1,4},{3,6},{4,1},{6,3},{9,12},{11,14},{12,9},{14,11},{17,20},{19,... | collective-permute-start | bytes 589832 | tf_op jit(solution)/shard_map/ppermute | solution.py:249
  299.2 25.0 %collective-permute-start.23 = (f32[256,768]{1,0:T(8,128)S(1)}, f32[256,768]{1,0:T(8,128)}, u32[]{:S(2)}, u32[]{:S(2)}) collective-permute-start(f32[256,768]{1,0:T(8,128)S(1)} %convolution_add_fusion.1), channel_id=1, source_target_pairs={{0,1},{1,0},{2,3},{3,2},{4,5},{5,4},{6,7},{7,6},{8,9},{9,8},{10,11... | collective-permute-start | bytes 2359304 | tf_op jit(solution)/shard_map/ppermute | solution.py:30
  300.0 21.9 %collective-permute-start.27 = (bf16[96,384]{1,0:T(8,128)(2,1)}, bf16[96,384]{1,0:T(8,128)(2,1)S(1)}, u32[]{:S(2)}, u32[]{:S(2)}) collective-permute-start(bf16[96,384]{1,0:T(8,128)(2,1)} %get-tuple-element.205), channel_id=1, source_target_pairs={{0,2},{2,0},{4,6},{6,4},{1,3},{3,1},{5,7},{7,5},{8,10},{10,8},{12,... | collective-permute-start | bytes 221192 | tf_op jit(solution)/shard_map/ppermute | solution.py:30
  300.0 21.9 %collective-permute-start.28 = (bf16[96,384]{1,0:T(8,128)(2,1)}, bf16[96,384]{1,0:T(8,128)(2,1)}, u32[]{:S(2)}, u32[]{:S(2)}) collective-permute-start(bf16[96,384]{1,0:T(8,128)(2,1)} %get-tuple-element.207), channel_id=1, source_target_pairs={{0,6},{2,4},{4,2},{6,0},{1,7},{3,5},{5,3},{7,1},{8,14},{10,12},{12... | collective-permute-start | bytes 221192 | tf_op jit(solution)/shard_map/ppermute | solution.py:30
  303.1 18.9 %collective-permute-start.29 = (bf16[96,384]{1,0:T(8,128)(2,1)S(1)}, bf16[96,384]{1,0:T(8,128)(2,1)}, u32[]{:S(2)}, u32[]{:S(2)}) collective-permute-start(bf16[96,384]{1,0:T(8,128)(2,1)S(1)} %get-tuple-element.206), channel_id=1, source_target_pairs={{0,4},{2,6},{4,0},{6,2},{1,5},{3,7},{5,1},{7,3},{8,12},{10,14},{12... | collective-permute-start | bytes 221192 | tf_op jit(solution)/shard_map/ppermute | solution.py:30
  311.4 104.3 %all-to-all-start.1 = ((bf16[16,432,384]{2,1,0:T(8,128)(2,1)}), bf16[16,432,384]{2,1,0:T(8,128)(2,1)}, u32[]{:S(2)}, u32[]{:S(2)}) async-start(bf16[16,432,384]{2,1,0:T(8,128)(2,1)} %pad_maximum_fusion), calls=%async_computation.1 | async-start | bytes 10616832 | tf_op jit(solution)/shard_map/all_to_all | solution.py:141
  319.9 93.9 %all-gather.8.cloned.1.call-start = ((), (), s32[]{:S(2)}) async-start(), calls=%async_computation.5 | async-start | bytes 1253376 | tf_op jit(solution)/shard_map/all_gather | solution.py:284
  337.8 12.4 %collective-permute-start.24 = (bf16[256,768]{0,1:T(8,128)(2,1)}, bf16[256,768]{0,1:T(8,128)(2,1)}, u32[]{:S(2)}, u32[]{:S(2)}) collective-permute-start(bf16[256,768]{0,1:T(8,128)(2,1)} %get-tuple-element.175), channel_id=1, source_target_pairs={{0,2},{2,0},{4,6},{6,4},{1,3},{3,1},{5,7},{7,5},{8,10},{10,8},{12,... | collective-permute-start | bytes 1179656 | tf_op jit(solution)/shard_map/ppermute | solution.py:30
  339.1 19.1 %collective-permute-start.25 = (bf16[256,768]{0,1:T(8,128)(2,1)}, bf16[256,768]{0,1:T(8,128)(2,1)}, u32[]{:S(2)}, u32[]{:S(2)}) collective-permute-start(bf16[256,768]{0,1:T(8,128)(2,1)} %get-tuple-element.177), channel_id=1, source_target_pairs={{0,6},{2,4},{4,2},{6,0},{1,7},{3,5},{5,3},{7,1},{8,14},{10,12},{12... | collective-permute-start | bytes 1179656 | tf_op jit(solution)/shard_map/ppermute | solution.py:30
  341.2 17.1 %collective-permute-start.26 = (bf16[256,768]{0,1:T(8,128)(2,1)}, bf16[256,768]{0,1:T(8,128)(2,1)}, u32[]{:S(2)}, u32[]{:S(2)}) collective-permute-start(bf16[256,768]{0,1:T(8,128)(2,1)} %get-tuple-element.176), channel_id=1, source_target_pairs={{0,4},{2,6},{4,0},{6,2},{1,5},{3,7},{5,1},{7,3},{8,12},{10,14},{12... | collective-permute-start | bytes 1179656 | tf_op jit(solution)/shard_map/ppermute | solution.py:30
  368.4 51.9 %collective-permute-start.38 = (bf16[768,384]{1,0:T(8,128)(2,1)}, bf16[768,384]{1,0:T(8,128)(2,1)}, u32[]{:S(2)}, u32[]{:S(2)}) collective-permute-start(bf16[768,384]{1,0:T(8,128)(2,1)} %get-tuple-element.165), channel_id=1, source_target_pairs={{0,2},{2,0},{4,6},{6,4},{1,3},{3,1},{5,7},{7,5},{8,10},{10,8},{12,... | collective-permute-start | bytes 1769480 | tf_op jit(solution)/shard_map/ppermute | solution.py:30
  374.7 9.1 %collective-permute-start.41 = (f32[19,384]{1,0:T(8,128)S(1)}, f32[19,384]{1,0:T(8,128)S(1)}, u32[]{:S(2)}, u32[]{:S(2)}) collective-permute-start(f32[19,384]{1,0:T(8,128)S(1)} %get-tuple-element.224), channel_id=1, source_target_pairs={{0,2},{2,0},{4,6},{6,4},{1,3},{3,1},{5,7},{7,5},{8,10},{10,8},{12,... | collective-permute-start | bytes 87560 | tf_op jit(solution)/shard_map/ppermute | solution.py:30
  374.8 9.6 %collective-permute-start.42 = (f32[19,384]{1,0:T(8,128)S(1)}, f32[19,384]{1,0:T(8,128)S(1)}, u32[]{:S(2)}, u32[]{:S(2)}) collective-permute-start(f32[19,384]{1,0:T(8,128)S(1)} %get-tuple-element.226), channel_id=1, source_target_pairs={{0,6},{2,4},{4,2},{6,0},{1,7},{3,5},{5,3},{7,1},{8,14},{10,12},{12... | collective-permute-start | bytes 87560 | tf_op jit(solution)/shard_map/ppermute | solution.py:30
  376.5 11.1 %collective-permute-start.43 = (f32[19,384]{1,0:T(8,128)S(1)}, f32[19,384]{1,0:T(8,128)S(1)}, u32[]{:S(2)}, u32[]{:S(2)}) collective-permute-start(f32[19,384]{1,0:T(8,128)S(1)} %get-tuple-element.225), channel_id=1, source_target_pairs={{0,4},{2,6},{4,0},{6,2},{1,5},{3,7},{5,1},{7,3},{8,12},{10,14},{12... | collective-permute-start | bytes 87560 | tf_op jit(solution)/shard_map/ppermute | solution.py:30
  383.8 36.5 %collective-permute-start.39 = (bf16[768,384]{1,0:T(8,128)(2,1)}, bf16[768,384]{1,0:T(8,128)(2,1)S(1)}, u32[]{:S(2)}, u32[]{:S(2)}) collective-permute-start(bf16[768,384]{1,0:T(8,128)(2,1)} %get-tuple-element.167), channel_id=1, source_target_pairs={{0,6},{2,4},{4,2},{6,0},{1,7},{3,5},{5,3},{7,1},{8,14},{10,12},{12... | collective-permute-start | bytes 1769480 | tf_op jit(solution)/shard_map/ppermute | solution.py:30
  384.4 35.9 %collective-permute-start.40 = (bf16[768,384]{1,0:T(8,128)(2,1)}, bf16[768,384]{1,0:T(8,128)(2,1)}, u32[]{:S(2)}, u32[]{:S(2)}) collective-permute-start(bf16[768,384]{1,0:T(8,128)(2,1)} %get-tuple-element.166), channel_id=1, source_target_pairs={{0,4},{2,6},{4,0},{6,2},{1,5},{3,7},{5,1},{7,3},{8,12},{10,14},{12... | collective-permute-start | bytes 1769480 | tf_op jit(solution)/shard_map/ppermute | solution.py:30
  387.6 49.4 %collective-permute-start.30 = (f32[256,768]{1,0:T(8,128)}, f32[256,768]{1,0:T(8,128)S(1)}, u32[]{:S(2)}, u32[]{:S(2)}) collective-permute-start(f32[256,768]{1,0:T(8,128)} %convolution_add_fusion), channel_id=1, source_target_pairs={{0,1},{1,0},{2,3},{3,2},{4,5},{5,4},{6,7},{7,6},{8,9},{9,8},{10,11... | collective-permute-start | bytes 2359304 | tf_op jit(solution)/shard_map/ppermute | solution.py:30
  424.2 20.9 %all-to-all-start.2 = ((bf16[16,56,384]{2,1,0:T(8,128)(2,1)}), bf16[16,56,384]{2,1,0:T(8,128)(2,1)S(1)}, u32[]{:S(2)}, u32[]{:S(2)}) async-start(bf16[16,56,384]{2,1,0:T(8,128)(2,1)} %maximum_maximum_fusion), calls=%async_computation.2 | async-start | bytes 1376256 | tf_op jit(solution)/shard_map/all_to_all | solution.py:141
  445.5 8.1 %collective-permute-start.44 = (bf16[200,384]{1,0:T(8,128)(2,1)S(1)}, bf16[200,384]{1,0:T(8,128)(2,1)S(1)}, u32[]{:S(2)}, u32[]{:S(2)}) collective-permute-start(bf16[200,384]{1,0:T(8,128)(2,1)S(1)} %concatenate.232), channel_id=1, source_target_pairs={{0,24},{8,16},{16,8},{24,0},{1,25},{9,17},{17,9},{25,1},{2,26},{10... | collective-permute-start | bytes 460808 | tf_op jit(solution)/shard_map/ppermute | solution.py:30
  446.2 7.5 %collective-permute-start.45 = (bf16[200,384]{1,0:T(8,128)(2,1)S(1)}, bf16[200,384]{1,0:T(8,128)(2,1)S(1)}, u32[]{:S(2)}, u32[]{:S(2)}) collective-permute-start(bf16[200,384]{1,0:T(8,128)(2,1)S(1)} %concatenate.232), channel_id=1, source_target_pairs={{0,16},{8,24},{16,0},{24,8},{1,17},{9,25},{17,1},{25,9},{2,18},{10... | collective-permute-start | bytes 460808 | tf_op jit(solution)/shard_map/ppermute | solution.py:30
  449.7 11.0 %collective-permute-start.31 = (f32[256,384]{1,0:T(8,128)S(1)}, f32[256,384]{1,0:T(8,128)S(1)}, u32[]{:S(2)}, u32[]{:S(2)}) collective-permute-start(f32[256,384]{1,0:T(8,128)S(1)} %slice_select_fusion), channel_id=1, source_target_pairs={{1,4},{3,6},{4,1},{6,3},{9,12},{11,14},{12,9},{14,11},{17,20},{19,... | collective-permute-start | bytes 1179656 | tf_op jit(solution)/shard_map/ppermute | solution.py:249
  454.7 30.1 %collective-permute-start.47 = (bf16[4,200,384]{2,1,0:T(8,128)(2,1)S(1)}, bf16[4,200,384]{2,1,0:T(8,128)(2,1)S(1)}, u32[]{:S(2)}, u32[]{:S(2)}) collective-permute-start(bf16[4,200,384]{2,1,0:T(8,128)(2,1)S(1)} %pad_maximum_fusion.10), channel_id=1, source_target_pairs={{0,96},{32,64},{64,32},{96,0},{1,97},{33,65},{65,33},{97,1},{2,98}... | collective-permute-start | bytes 1843208 | tf_op jit(solution)/shard_map/ppermute | solution.py:30
  455.8 29.0 %collective-permute-start.48 = (bf16[4,200,384]{2,1,0:T(8,128)(2,1)S(1)}, bf16[4,200,384]{2,1,0:T(8,128)(2,1)S(1)}, u32[]{:S(2)}, u32[]{:S(2)}) collective-permute-start(bf16[4,200,384]{2,1,0:T(8,128)(2,1)S(1)} %pad_maximum_fusion.10), channel_id=1, source_target_pairs={{0,64},{32,96},{64,0},{96,32},{1,65},{33,97},{65,1},{97,33},{2,66}... | collective-permute-start | bytes 1843208 | tf_op jit(solution)/shard_map/ppermute | solution.py:30
  456.7 28.8 %collective-permute-start.49 = (bf16[4,200,384]{2,1,0:T(8,128)(2,1)S(1)}, bf16[4,200,384]{2,1,0:T(8,128)(2,1)S(1)}, u32[]{:S(2)}, u32[]{:S(2)}) collective-permute-start(bf16[4,200,384]{2,1,0:T(8,128)(2,1)S(1)} %pad_maximum_fusion.10), channel_id=1, source_target_pairs={{0,32},{32,0},{64,96},{96,64},{1,33},{33,1},{65,97},{97,65},{2,34}... | collective-permute-start | bytes 1843208 | tf_op jit(solution)/shard_map/ppermute | solution.py:30
  (159 other events, 1113.7 us)
Sparse Core Ops, SparseCore 0:
  13.4 83.0 all-gather.3
  99.9 69.2 all-gather.5
  323.7 90.0 all-gather.7

commit v3 on v2

--- a/solution.py
+++ b/solution.py
@@ -125,12 +125,14 @@
     return jax.nn.gelu(value, approximate=False)
 
 
-def weight_grad(pairs):
+def weight_grad(pairs, extra=None):
     blocks = []
     for row in range(2):
         for z in range(2):
             blocks += [tm(right[z], left[:, row * HALF : (row + 1) * HALF]).astype(bf16) for left, right in pairs]
-    return jnp.concatenate(blocks, 0).reshape(64, -1, HALF)
+            if extra is not None:
+                blocks.append(extra[2 * row + z])
+    return jnp.concatenate(blocks, 0)
 
 
 def plane_pieces(pieces):
@@ -270,7 +272,8 @@
             one = plane_exchange(pieces)
         else:
             one = line_sum(one.reshape(4, 96, HALF).astype(bf16), place).astype(bf16)
-            zero = plane_exchange(jnp.concatenate([pieces, one_a.astype(bf16).reshape(16, 48, HALF)], 1))
+            one = jnp.concatenate([one, plane_sum(one_a).astype(bf16)], 0)
+            zero = plane_exchange(pieces)
         resid_one, gain_one, shift_one = norm_backward(normed_grad, unit_one, inverse_one, gain[0])
         attn_low = resid_one.astype(bf16)
         out_bias = jnp.sum(attn_low, 0, dtype=f32)
@@ -291,39 +294,44 @@
             )
         qkv_bias = [jnp.sum(qkv_grad[z], 0, dtype=f32) for z in range(2)]
         grad_state = resid_one + core_sum(sum(mt(qkv_grad[z], wa[z][:, : 3 * BLOCK]) for z in range(2)))
-        full_a = weight_grad([(low, qkv_grad), (attn_low, mix_parts)])
+        wide = [out_bias, down_bias, gain_one, gain_two, shift_one, shift_two] + wide
+        narrow = [[qkv_bias[z], up_bias[z]] + narrow[z] for z in range(2)]
+        pairs_a = [(low, qkv_grad), (attn_low, mix_parts)]
         if l == 1:
             one = plane_sum(one)
             grad_state = grad_state + when(one)
-            one_a = line_sum(full_a.reshape(4, PACK_A, HALF), place)
+            one_a = (line_sum(weight_grad(pairs_a).reshape(4, PACK_A, HALF), place) + when(one)).astype(bf16)
+            one_a = plane_exchange(one_a.reshape(16, 48, HALF))
         else:
-            zero_a = line_sum(full_a.reshape(4, PACK_A, HALF), place)
+            wide = jnp.stack(wide)
+            small = [
+                jnp.concatenate([wide[:, (j // 2) * HALF : (j // 2 + 1) * HALF].reshape(-1)] + narrow[j % 2])
+                for j in range(4)
+            ]
+            small = split3(jnp.stack(small).reshape(4, SMALL, HALF)).transpose(1, 0, 2, 3).reshape(4, 3 * SMALL, HALF)
+            small = jnp.pad(small, ((0, 0), (0, 64 - 3 * SMALL), (0, 0)))
+            zero_a = line_sum(weight_grad(pairs_a, small).reshape(4, PACK_A + 64, HALF), place)
             zero = plane_sum(zero) + when(one)
-        wide += [out_bias, down_bias, gain_one, gain_two, shift_one, shift_two]
-        narrow = [narrow[z] + [qkv_bias[z], up_bias[z]] for z in range(2)]
 
     grad_in = to_output(grad_state)
 
-    wide = jnp.stack(wide)
-    narrow = [jnp.concatenate(part) for part in narrow]
-    small = jnp.stack(
-        [jnp.concatenate([wide[:, (j // 2) * HALF : (j // 2 + 1) * HALF].reshape(-1), narrow[j % 2]]) for j in range(4)]
-    )
-    small = split3(jnp.pad(line_sum(small.reshape(4, SMALL, HALF), place), ((0, 32 - SMALL), (0, 0))))
+    small = jnp.sum(zero_a[PACK_A : PACK_A + 3 * SMALL].reshape(3, SMALL, HALF), 0)
+    small = split3(jnp.pad(small, ((0, 32 - SMALL), (0, 0))))
     small = small.reshape(3, 16, 2, HALF).transpose(1, 0, 2, 3).reshape(16, 6, HALF)
-    zero_a = (zero_a + when(zero)).astype(bf16).reshape(16, 48, HALF)
+    zero_a = (zero_a[:PACK_A] + when(zero)).astype(bf16).reshape(16, 48, HALF)
     moved = plane_exchange(jnp.concatenate([zero_a, small, jnp.zeros((16, 2, HALF), bf16)], 1))
-    zero_b = line_sum(zero[:HALF].reshape(4, 96, HALF).astype(bf16), place).astype(bf16)
+    zero_b = line_sum(zero.reshape(4, 96, HALF).astype(bf16), place).astype(bf16)
     small = split3(jnp.sum(moved[:, 48:54].reshape(48, 2, HALF), 0, dtype=f32)).reshape(6, HALF)
     zero_a = plane_sum(moved[:, :48]).astype(bf16)
-    zero = jnp.concatenate([zero_b, zero[HALF:].astype(bf16), zero_a, small, jnp.zeros((2, HALF), bf16)], 0)
+    zero = jnp.concatenate([zero_b, zero_a, small, jnp.zeros((2, HALF), bf16)], 0)
     zero = jnp.stack(in_order(near_first(gather(zero, "y")), at_y))
-    zero = jnp.stack(in_order(near_first(gather(zero, "x")), at_x)).reshape(16, 200, HALF)
-    own = jnp.sum(zero[:, 192:198].reshape(16, 3, 2, HALF), 1, dtype=f32).reshape(32 * HALF)
-    wide = own[: 12 * HALF].reshape(LAYERS, 6, HALF)[::-1]
-    own = own[12 * HALF : SMALL * HALF].reshape(LAYERS, 3 * BLOCK + HID)[::-1]
-    grad_a = [zero[:, 144:192].reshape(PACK_A, HALF), zero[:, 96:144].reshape(PACK_A, HALF)]
-    grad_b = [zero[:, :96].reshape(PACK_B, HALF), one.reshape(PACK_B, HALF)]
+    zero = jnp.stack(in_order(near_first(gather(zero, "x")), at_x)).reshape(16, 152, HALF)
+    own = jnp.sum(zero[:, 144:150].reshape(16, 3, 2, HALF), 1, dtype=f32).reshape(32 * HALF)
+    wide = own[: 12 * HALF].reshape(LAYERS, 6, HALF)
+    own = own[12 * HALF : SMALL * HALF].reshape(LAYERS, 3 * BLOCK + HID)
+    one = one.reshape(16, 144, HALF)
+    grad_a = [zero[:, 96:144].reshape(PACK_A, HALF), one[:, 96:].reshape(PACK_A, HALF)]
+    grad_b = [zero[:, :96].reshape(PACK_B, HALF), one[:, :96].reshape(PACK_B, HALF)]
 
     def both(parts, turn):
         return jnp.stack([part.T if turn else part for part in parts]).astype(f32)

time: 523 us -> 518 us (level)
  the two profiles are of different devices: /device:TPU:32 before, /device:TPU:0 now
where the time goes in v3:
time: 518 us; the launch traced here: 508 us
  waiting for transfers between devices  183 us (35%)
  starting transfers between devices  94.3 us (18%)
  matrix products  91 us (18%)
  other arithmetic  60.4 us (12%)
  local copies, waits for them, and re-layouts  59.3 us (11%)
  between operations  20.3 us (4%)
    ppermute x44, waiting for transfers between devices, swapped(): return lax.ppermute(value, axes, [(i, i ^ bits) for i in range(count)])  141 us
    ppermute x44, starting transfers between devices, swapped(): return lax.ppermute(value, axes, [(i, i ^ bits) for i in range(count)])  59.2 us
    dot_general x64, matrix products, dot(): lax.dot_general(left, right, ((dims[0], dims[1]), ((), ())), preferred_el...  58.4 us
    all_to_all x4, starting transfers between devices, plane_exchange(): return lax.all_to_all(pieces, PLANE, 0, 0, tiled=True)  32.2 us
    all_gather x1, waiting for transfers between devices, on_device(): lax.all_gather(later, LINE + PLANE, axis=0, tiled=True)  17 us
    unnamed x371, local copies, waits for them, and re-layouts  16.9 us
    all_to_all x4, waiting for transfers between devices, plane_exchange(): return lax.all_to_all(pieces, PLANE, 0, 0, tiled=True)  15 us
    sub x2, matrix products, attend_forward(): raised = jnp.exp(scores - peak)  10.6 us
  transfers between devices with their start and end apart: 54, of which 26 were waited for; matrix products, arithmetic and copies ran while one was open for 31% of the time, Pallas kernels for 0%

profile of v3, /device:TPU:0, one launch (start us, length us, event | category | flops | bytes accessed | tf_op | source)
XLA Modules:
  0.0 508.1 jit_solution(5414186644513995384)
XLA Ops:
  14.4 4.1 collective-permute-start.2
  22.9 24.8 %collective-permute-done.5 = bf16[2,1152]{1,0:T(2,128)(2,1)S(1)} collective-permute-done((bf16[2,1152]{1,0:T(2,128)(2,1)S(1)}, bf16[2,1152]{1,0:T(2,128)(2,1)S(1)}, u32[]{:S(2)}, u32[]{:S(2)}) %collective-permute-start.5) | collective-permute-done | bytes 4640 | tf_op jit(solution)/shard_map/ppermute | solution.py:30
  49.7 3.6 collective-permute-start.1
  58.9 3.2 collective-permute-start.8
  62.2 8.6 %collective-permute-done.6 = bf16[256,768]{0,1:T(8,128)(2,1)S(1)} collective-permute-done((bf16[256,768]{0,1:T(8,128)(2,1)S(1)}, bf16[256,768]{0,1:T(8,128)(2,1)S(1)}, u32[]{:S(2)}, u32[]{:S(2)}) %collective-permute-start.6) | collective-permute-done | bytes 393248 | tf_op jit(solution)/shard_map/ppermute | solution.py:30
  70.8 8.8 %collective-permute-done.7 = bf16[256,768]{0,1:T(8,128)(2,1)S(1)} collective-permute-done((bf16[256,768]{0,1:T(8,128)(2,1)S(1)}, bf16[256,768]{0,1:T(8,128)(2,1)S(1)}, u32[]{:S(2)}, u32[]{:S(2)}) %collective-permute-start.7) | collective-permute-done | bytes 393248 | tf_op jit(solution)/shard_map/ppermute | solution.py:30
  79.7 3.2 collective-permute-done.8
  86.5 4.8 fusion.256
  91.9 4.4 fusion.61
  101.3 2.8 slice_bitcast_fusion.4
  104.1 3.1 multiply_convert_fusion.5
  108.1 3.1 multiply_convert_fusion.4
  116.8 3.1 collective-permute-start.13
  121.6 7.1 %collective-permute-done.12 = bf16[256,768]{0,1:T(8,128)(2,1)S(1)} collective-permute-done((bf16[256,768]{0,1:T(8,128)(2,1)S(1)}, bf16[256,768]{0,1:T(8,128)(2,1)S(1)}, u32[]{:S(2)}, u32[]{:S(2)}) %collective-permute-start.12) | collective-permute-done | bytes 393248 | tf_op jit(solution)/shard_map/ppermute | solution.py:30
  128.7 9.8 %collective-permute-done.13 = bf16[256,768]{0,1:T(8,128)(2,1)S(1)} collective-permute-done((bf16[256,768]{0,1:T(8,128)(2,1)S(1)}, bf16[256,768]{0,1:T(8,128)(2,1)S(1)}, u32[]{:S(2)}, u32[]{:S(2)}) %collective-permute-start.13) | collective-permute-done | bytes 393248 | tf_op jit(solution)/shard_map/ppermute | solution.py:30
  144.2 5.8 %fusion.257 = (f32[6,256]{1,0:T(8,128)S(1)}, f32[6,256,1024]{2,1,0:T(8,128)}) fusion(pred[1024]{0:T(1024)(128)(4,1)S(1)} %copy-done.169, bf16[256,6,64]{0,2,1:T(8,128)(2,1)S(1)} %bitcast.352, bf16[1024,6,64]{0,2,1:T(8,128)(2,1)} %bitcast.329), kind=kOutput, calls=%fused_computation.613 | convolution fusion | flops 207619072 | bytes 7281664 | tf_op jit(solution)/shard_map/sub | solution.py:103
  150.0 4.3 fusion.64
  156.8 17.0 %all-gather.6.cloned.1.call-done = bf16[1536,1536]{1,0:T(8,128)(2,1)} async-done(((bf16[24,1536]{1,0:T(8,128)(2,1)}), bf16[1536,1536]{1,0:T(8,128)(2,1)}) %all-gather.6.cloned.1.call-update) | async-done | bytes 4718608 | tf_op jit(solution)/shard_map/all_gather | solution.py:176
  179.3 3.1 multiply_convert_fusion.3
  183.1 3.2 multiply_convert_fusion.2
  195.6 3.0 convert_reduce_fusion.4
  200.6 3.0 convert_reduce_fusion.2
  208.4 2.9 copy.103
  211.3 4.8 all-to-all-start
  218.0 3.0 multiply_reduce_fusion.3
  223.4 3.9 multiply_reduce_fusion.1
  238.4 4.9 collective-permute-done.19
  243.3 9.2 %collective-permute-done.20 = bf16[256,768]{0,1:T(8,128)(2,1)S(1)} collective-permute-done((bf16[256,768]{0,1:T(8,128)(2,1)S(1)}, bf16[256,768]{0,1:T(8,128)(2,1)S(1)}, u32[]{:S(2)}, u32[]{:S(2)}) %collective-permute-start.20) | collective-permute-done | bytes 393248 | tf_op jit(solution)/shard_map/ppermute | solution.py:30
  264.2 14.5 %all-to-all-done = bf16[16,384,384]{2,1,0:T(8,128)(2,1)} async-done(((bf16[16,384,384]{2,1,0:T(8,128)(2,1)}), bf16[16,384,384]{2,1,0:T(8,128)(2,1)}, u32[]{:S(2)}, u32[]{:S(2)}) %all-to-all-start) | async-done | bytes 4718624 | tf_op jit(solution)/shard_map/all_to_all | solution.py:143
  278.7 3.1 convert_reduce_fusion.1
  286.9 3.0 convert_reduce_fusion.5
  293.4 3.0 convert_reduce_fusion.3
  306.3 15.1 %all-to-all-start.2 = ((bf16[16,48,384]{2,1,0:T(8,128)(2,1)}), bf16[16,48,384]{2,1,0:T(8,128)(2,1)S(1)}, u32[]{:S(2)}, u32[]{:S(2)}) async-start(bf16[16,48,384]{2,1,0:T(8,128)(2,1)} %bitcast.340), calls=%async_computation.2 | async-start | bytes 1179648 | tf_op jit(solution)/shard_map/all_to_all | solution.py:143
  328.3 5.4 %copy.104 = bf16[4,16,96,384]{3,2,0,1:T(8,128)(2,1)} copy(bf16[4,16,96,384]{3,2,1,0:T(8,128)(2,1)} %bitcast.84) | data formatting | bytes 9437184 | tf_op jit(solution)/shard_map/reshape | solution.py:139
  336.6 7.3 %all-to-all-start.1 = ((bf16[16,384,384]{2,1,0:T(8,128)(2,1)}), bf16[16,384,384]{2,1,0:T(8,128)(2,1)}, u32[]{:S(2)}, u32[]{:S(2)}) async-start(bf16[16,384,384]{2,1,0:T(8,128)(2,1)} %bitcast.303), calls=%async_computation.1 | async-start | bytes 9437184 | tf_op jit(solution)/shard_map/all_to_all | solution.py:143
  348.6 3.7 multiply_reduce_fusion
  362.5 7.9 %collective-permute-done.24 = bf16[256,768]{0,1:T(8,128)(2,1)S(1)} collective-permute-done((bf16[256,768]{0,1:T(8,128)(2,1)}, bf16[256,768]{0,1:T(8,128)(2,1)S(1)}, u32[]{:S(2)}, u32[]{:S(2)}) %collective-permute-start.24) | collective-permute-done | bytes 393248 | tf_op jit(solution)/shard_map/ppermute | solution.py:30
  370.4 6.6 %collective-permute-done.25 = bf16[256,768]{0,1:T(8,128)(2,1)} collective-permute-done((bf16[256,768]{0,1:T(8,128)(2,1)}, bf16[256,768]{0,1:T(8,128)(2,1)}, u32[]{:S(2)}, u32[]{:S(2)}) %collective-permute-start.25) | collective-permute-done | bytes 393248 | tf_op jit(solution)/shard_map/ppermute | solution.py:30
  399.0 5.7 %collective-permute-done.38 = bf16[832,384]{1,0:T(8,128)(2,1)S(1)} collective-permute-done((bf16[832,384]{1,0:T(8,128)(2,1)}, bf16[832,384]{1,0:T(8,128)(2,1)S(1)}, u32[]{:S(2)}, u32[]{:S(2)}) %collective-permute-start.38) | collective-permute-done | bytes 639008 | tf_op jit(solution)/shard_map/ppermute | solution.py:30
  404.7 14.1 %collective-permute-done.39 = bf16[832,384]{1,0:T(8,128)(2,1)} collective-permute-done((bf16[832,384]{1,0:T(8,128)(2,1)}, bf16[832,384]{1,0:T(8,128)(2,1)}, u32[]{:S(2)}, u32[]{:S(2)}) %collective-permute-start.39) | collective-permute-done | bytes 639008 | tf_op jit(solution)/shard_map/ppermute | solution.py:30
  420.8 9.9 %all-gather.8.cloned.1.call-done = bf16[2304,384]{1,0:T(8,128)(2,1)} async-done(((bf16[144,384]{1,0:T(8,128)(2,1)}), bf16[2304,384]{1,0:T(8,128)(2,1)}) %all-gather.8.cloned.1.call-update) | async-done | bytes 1769488 | tf_op jit(solution)/shard_map/all_gather | solution.py:287
  432.6 3.0 convert_reduce_fusion
  438.0 5.0 all-to-all-start.3
  455.4 2.8 collective-permute-start.41
  460.3 2.8 collective-permute-done.41
  465.8 2.8 collective-permute-start.44
  473.3 13.8 %collective-permute-done.44 = bf16[4,152,384]{2,1,0:T(8,128)(2,1)S(1)} collective-permute-done((bf16[4,152,384]{2,1,0:T(8,128)(2,1)S(1)}, bf16[4,152,384]{2,1,0:T(8,128)(2,1)S(1)}, u32[]{:S(2)}, u32[]{:S(2)}) %collective-permute-start.44) | collective-permute-done | bytes 466976 | tf_op jit(solution)/shard_map/ppermute | solution.py:30
  496.3 2.9 maximum_convert_fusion.1
  (714 shorter events, 192.9 us)
Async XLA Ops:
  7.2 94.1 %all-gather.4.cloned.1.call-start = ((), (), s32[]{:S(2)}) async-start(), calls=%async_computation.4 | async-start | bytes 7188480 | tf_op jit(solution)/shard_map/all_gather | solution.py:175
  13.4 160.3 %all-gather.6.cloned.1.call-start = ((), (), s32[]{:S(2)}) async-start(), calls=%async_computation.5 | async-start | bytes 4792320 | tf_op jit(solution)/shard_map/all_gather | solution.py:176
  14.4 39.6 %collective-permute-start.2 = (bf16[384,768]{0,1:T(8,128)(2,1)}, bf16[384,768]{0,1:T(8,128)(2,1)S(1)}, u32[]{:S(2)}, u32[]{:S(2)}) collective-permute-start(bf16[384,768]{0,1:T(8,128)(2,1)} %pad_maximum_fusion.9), channel_id=1, source_target_pairs={{0,6},{2,4},{4,2},{6,0},{1,7},{3,5},{5,3},{7,1},{8,14},{10,12},{12... | collective-permute-start | bytes 1769480 | tf_op jit(solution)/shard_map/ppermute | solution.py:30
  18.5 35.4 %collective-permute-start.3 = (bf16[384,768]{0,1:T(8,128)(2,1)}, bf16[384,768]{0,1:T(8,128)(2,1)S(1)}, u32[]{:S(2)}, u32[]{:S(2)}) collective-permute-start(bf16[384,768]{0,1:T(8,128)(2,1)} %pad_maximum_fusion.9), channel_id=1, source_target_pairs={{0,4},{2,6},{4,0},{6,2},{1,5},{3,7},{5,1},{7,3},{8,12},{10,14},{12... | collective-permute-start | bytes 1769480 | tf_op jit(solution)/shard_map/ppermute | solution.py:30
  18.5 36.3 %collective-permute-start.4 = (bf16[384,768]{0,1:T(8,128)(2,1)}, bf16[384,768]{0,1:T(8,128)(2,1)}, u32[]{:S(2)}, u32[]{:S(2)}) collective-permute-start(bf16[384,768]{0,1:T(8,128)(2,1)} %pad_maximum_fusion.9), channel_id=1, source_target_pairs={{0,2},{2,0},{4,6},{6,4},{1,3},{3,1},{5,7},{7,5},{8,10},{10,8},{12,... | collective-permute-start | bytes 1769480 | tf_op jit(solution)/shard_map/ppermute | solution.py:30
  19.5 28.2 %collective-permute-start.5 = (bf16[2,1152]{1,0:T(2,128)(2,1)S(1)}, bf16[2,1152]{1,0:T(2,128)(2,1)S(1)}, u32[]{:S(2)}, u32[]{:S(2)}) collective-permute-start(bf16[2,1152]{1,0:T(2,128)(2,1)S(1)} %constant_dynamic-update-slice_fusion.2), channel_id=1, source_target_pairs={{0,2},{2,0},{1,3},{3,1},{4,6},{6,4},{5,7},{7,5},{8,10},{10,8},{9,1... | collective-permute-start | bytes 13832 | tf_op jit(solution)/shard_map/ppermute | solution.py:30
  20.8 28.8 %collective-permute-start = (bf16[512,384]{1,0:T(8,128)(2,1)S(1)}, bf16[512,384]{1,0:T(8,128)(2,1)S(1)}, u32[]{:S(2)}, u32[]{:S(2)}) collective-permute-start(bf16[512,384]{1,0:T(8,128)(2,1)S(1)} %constant_dynamic-update-slice_fusion), channel_id=1, source_target_pairs={{1,4},{3,6},{4,1},{6,3},{9,12},{11,14},{12,9},{14,11},{17,20},{19,... | collective-permute-start | bytes 1179656 | tf_op jit(solution)/shard_map/ppermute | solution.py:203
  47.7 50.9 %collective-permute-start.10 = (bf16[2,6,384]{2,1,0:T(8,128)(2,1)}, bf16[2,6,384]{2,1,0:T(8,128)(2,1)}, u32[]{:S(2)}, u32[]{:S(2)}) collective-permute-start(bf16[2,6,384]{2,1,0:T(8,128)(2,1)} %get-tuple-element.237), channel_id=1, source_target_pairs={{0,4},{4,0},{1,5},{5,1},{2,6},{6,2},{3,7},{7,3},{8,12},{12,8},{9,1... | collective-permute-start | bytes 27656 | tf_op jit(solution)/shard_map/ppermute | solution.py:30
  49.7 7.0 %collective-permute-start.1 = (bf16[512,384]{1,0:T(8,128)(2,1)S(1)}, bf16[512,384]{1,0:T(8,128)(2,1)S(1)}, u32[]{:S(2)}, u32[]{:S(2)}) collective-permute-start(bf16[512,384]{1,0:T(8,128)(2,1)S(1)} %broadcast_select_fusion.12), channel_id=1, source_target_pairs={{0,1},{1,0},{2,3},{3,2},{4,5},{5,4},{6,7},{7,6},{8,9},{9,8},{10,11... | collective-permute-start | bytes 1179656 | tf_op jit(solution)/shard_map/ppermute | solution.py:30
  57.9 13.0 %collective-permute-start.6 = (bf16[256,768]{0,1:T(8,128)(2,1)S(1)}, bf16[256,768]{0,1:T(8,128)(2,1)S(1)}, u32[]{:S(2)}, u32[]{:S(2)}) collective-permute-start(bf16[256,768]{0,1:T(8,128)(2,1)S(1)} %pad_maximum_fusion.13), channel_id=1, source_target_pairs={{0,2},{2,0},{4,6},{6,4},{1,3},{3,1},{5,7},{7,5},{8,10},{10,8},{12,... | collective-permute-start | bytes 1179656 | tf_op jit(solution)/shard_map/ppermute | solution.py:30
  58.0 21.7 %collective-permute-start.7 = (bf16[256,768]{0,1:T(8,128)(2,1)S(1)}, bf16[256,768]{0,1:T(8,128)(2,1)S(1)}, u32[]{:S(2)}, u32[]{:S(2)}) collective-permute-start(bf16[256,768]{0,1:T(8,128)(2,1)S(1)} %pad_maximum_fusion.13), channel_id=1, source_target_pairs={{0,6},{2,4},{4,2},{6,0},{1,7},{3,5},{5,3},{7,1},{8,14},{10,12},{12... | collective-permute-start | bytes 1179656 | tf_op jit(solution)/shard_map/ppermute | solution.py:30
  58.9 24.0 %collective-permute-start.8 = (bf16[256,768]{0,1:T(8,128)(2,1)S(1)}, bf16[256,768]{0,1:T(8,128)(2,1)S(1)}, u32[]{:S(2)}, u32[]{:S(2)}) collective-permute-start(bf16[256,768]{0,1:T(8,128)(2,1)S(1)} %pad_maximum_fusion.13), channel_id=1, source_target_pairs={{0,4},{2,6},{4,0},{6,2},{1,5},{3,7},{5,1},{7,3},{8,12},{10,14},{12... | collective-permute-start | bytes 1179656 | tf_op jit(solution)/shard_map/ppermute | solution.py:30
  116.3 12.4 %collective-permute-start.12 = (bf16[256,768]{0,1:T(8,128)(2,1)S(1)}, bf16[256,768]{0,1:T(8,128)(2,1)S(1)}, u32[]{:S(2)}, u32[]{:S(2)}) collective-permute-start(bf16[256,768]{0,1:T(8,128)(2,1)S(1)} %pad_maximum_fusion.14), channel_id=1, source_target_pairs={{0,2},{2,0},{4,6},{6,4},{1,3},{3,1},{5,7},{7,5},{8,10},{10,8},{12,... | collective-permute-start | bytes 1179656 | tf_op jit(solution)/shard_map/ppermute | solution.py:30
  116.8 21.7 %collective-permute-start.13 = (bf16[256,768]{0,1:T(8,128)(2,1)S(1)}, bf16[256,768]{0,1:T(8,128)(2,1)S(1)}, u32[]{:S(2)}, u32[]{:S(2)}) collective-permute-start(bf16[256,768]{0,1:T(8,128)(2,1)S(1)} %pad_maximum_fusion.14), channel_id=1, source_target_pairs={{0,6},{2,4},{4,2},{6,0},{1,7},{3,5},{5,3},{7,1},{8,14},{10,12},{12... | collective-permute-start | bytes 1179656 | tf_op jit(solution)/shard_map/ppermute | solution.py:30
  119.9 20.4 %collective-permute-start.14 = (bf16[256,768]{0,1:T(8,128)(2,1)S(1)}, bf16[256,768]{0,1:T(8,128)(2,1)S(1)}, u32[]{:S(2)}, u32[]{:S(2)}) collective-permute-start(bf16[256,768]{0,1:T(8,128)(2,1)S(1)} %pad_maximum_fusion.14), channel_id=1, source_target_pairs={{0,4},{2,6},{4,0},{6,2},{1,5},{3,7},{5,1},{7,3},{8,12},{10,14},{12... | collective-permute-start | bytes 1179656 | tf_op jit(solution)/shard_map/ppermute | solution.py:30
  156.1 20.3 %collective-permute-start.15 = (f32[256,768]{1,0:T(8,128)}, f32[256,768]{1,0:T(8,128)S(1)}, u32[]{:S(2)}, u32[]{:S(2)}) collective-permute-start(f32[256,768]{1,0:T(8,128)} %convolution_add_fusion.7), channel_id=1, source_target_pairs={{0,1},{1,0},{2,3},{3,2},{4,5},{5,4},{6,7},{7,6},{8,9},{9,8},{10,11... | collective-permute-start | bytes 2359304 | tf_op jit(solution)/shard_map/ppermute | solution.py:30
  205.0 13.0 %collective-permute-start.18 = (f32[256,768]{1,0:T(8,128)}, f32[256,768]{1,0:T(8,128)}, u32[]{:S(2)}, u32[]{:S(2)}) collective-permute-start(f32[256,768]{1,0:T(8,128)} %convolution_add_fusion.3), channel_id=1, source_target_pairs={{0,1},{1,0},{2,3},{3,2},{4,5},{5,4},{6,7},{7,6},{8,9},{9,8},{10,11... | collective-permute-start | bytes 2359304 | tf_op jit(solution)/shard_map/ppermute | solution.py:30
  211.3 67.3 %all-to-all-start = ((bf16[16,384,384]{2,1,0:T(8,128)(2,1)}), bf16[16,384,384]{2,1,0:T(8,128)(2,1)}, u32[]{:S(2)}, u32[]{:S(2)}) async-start(bf16[16,384,384]{2,1,0:T(8,128)(2,1)} %bitcast.304), calls=%async_computation | async-start | bytes 9437184 | tf_op jit(solution)/shard_map/all_to_all | solution.py:143
  231.3 12.0 %collective-permute-start.19 = (bf16[256,768]{0,1:T(8,128)(2,1)S(1)}, bf16[256,768]{0,1:T(8,128)(2,1)S(1)}, u32[]{:S(2)}, u32[]{:S(2)}) collective-permute-start(bf16[256,768]{0,1:T(8,128)(2,1)S(1)} %get-tuple-element.176), channel_id=1, source_target_pairs={{0,2},{2,0},{4,6},{6,4},{1,3},{3,1},{5,7},{7,5},{8,10},{10,8},{12,... | collective-permute-start | bytes 1179656 | tf_op jit(solution)/shard_map/ppermute | solution.py:30
  231.5 21.0 %collective-permute-start.20 = (bf16[256,768]{0,1:T(8,128)(2,1)S(1)}, bf16[256,768]{0,1:T(8,128)(2,1)S(1)}, u32[]{:S(2)}, u32[]{:S(2)}) collective-permute-start(bf16[256,768]{0,1:T(8,128)(2,1)S(1)} %get-tuple-element.178), channel_id=1, source_target_pairs={{0,6},{2,4},{4,2},{6,0},{1,7},{3,5},{5,3},{7,1},{8,14},{10,12},{12... | collective-permute-start | bytes 1179656 | tf_op jit(solution)/shard_map/ppermute | solution.py:30
  233.5 19.0 %collective-permute-start.21 = (bf16[256,768]{0,1:T(8,128)(2,1)S(1)}, bf16[256,768]{0,1:T(8,128)(2,1)S(1)}, u32[]{:S(2)}, u32[]{:S(2)}) collective-permute-start(bf16[256,768]{0,1:T(8,128)(2,1)S(1)} %get-tuple-element.177), channel_id=1, source_target_pairs={{0,4},{2,6},{4,0},{6,2},{1,5},{3,7},{5,1},{7,3},{8,12},{10,14},{12... | collective-permute-start | bytes 1179656 | tf_op jit(solution)/shard_map/ppermute | solution.py:30
  253.8 29.2 %collective-permute-start.22 = (f32[256,768]{1,0:T(8,128)S(1)}, f32[256,768]{1,0:T(8,128)}, u32[]{:S(2)}, u32[]{:S(2)}) collective-permute-start(f32[256,768]{1,0:T(8,128)S(1)} %convolution_add_fusion.2), channel_id=1, source_target_pairs={{0,1},{1,0},{2,3},{3,2},{4,5},{5,4},{6,7},{7,6},{8,9},{9,8},{10,11... | collective-permute-start | bytes 2359304 | tf_op jit(solution)/shard_map/ppermute | solution.py:30
  259.3 43.0 %collective-permute-start.32 = (bf16[768,384]{1,0:T(8,128)(2,1)}, bf16[768,384]{1,0:T(8,128)(2,1)}, u32[]{:S(2)}, u32[]{:S(2)}) collective-permute-start(bf16[768,384]{1,0:T(8,128)(2,1)} %get-tuple-element.159), channel_id=1, source_target_pairs={{0,2},{2,0},{4,6},{6,4},{1,3},{3,1},{5,7},{7,5},{8,10},{10,8},{12,... | collective-permute-start | bytes 1769480 | tf_op jit(solution)/shard_map/ppermute | solution.py:30
  259.8 42.5 %collective-permute-start.33 = (bf16[768,384]{1,0:T(8,128)(2,1)}, bf16[768,384]{1,0:T(8,128)(2,1)}, u32[]{:S(2)}, u32[]{:S(2)}) collective-permute-start(bf16[768,384]{1,0:T(8,128)(2,1)} %get-tuple-element.161), channel_id=1, source_target_pairs={{0,6},{2,4},{4,2},{6,0},{1,7},{3,5},{5,3},{7,1},{8,14},{10,12},{12... | collective-permute-start | bytes 1769480 | tf_op jit(solution)/shard_map/ppermute | solution.py:30
  261.0 41.2 %collective-permute-start.34 = (bf16[768,384]{1,0:T(8,128)(2,1)}, bf16[768,384]{1,0:T(8,128)(2,1)}, u32[]{:S(2)}, u32[]{:S(2)}) collective-permute-start(bf16[768,384]{1,0:T(8,128)(2,1)} %get-tuple-element.160), channel_id=1, source_target_pairs={{0,4},{2,6},{4,0},{6,2},{1,5},{3,7},{5,1},{7,3},{8,12},{10,14},{12... | collective-permute-start | bytes 1769480 | tf_op jit(solution)/shard_map/ppermute | solution.py:30
  299.8 45.1 %collective-permute-start.23 = (f32[256,768]{1,0:T(8,128)S(1)}, f32[256,768]{1,0:T(8,128)}, u32[]{:S(2)}, u32[]{:S(2)}) collective-permute-start(f32[256,768]{1,0:T(8,128)S(1)} %convolution_add_fusion.1), channel_id=1, source_target_pairs={{0,1},{1,0},{2,3},{3,2},{4,5},{5,4},{6,7},{7,6},{8,9},{9,8},{10,11... | collective-permute-start | bytes 2359304 | tf_op jit(solution)/shard_map/ppermute | solution.py:30
  306.3 30.3 %all-to-all-start.2 = ((bf16[16,48,384]{2,1,0:T(8,128)(2,1)}), bf16[16,48,384]{2,1,0:T(8,128)(2,1)S(1)}, u32[]{:S(2)}, u32[]{:S(2)}) async-start(bf16[16,48,384]{2,1,0:T(8,128)(2,1)} %bitcast.340), calls=%async_computation.2 | async-start | bytes 1179648 | tf_op jit(solution)/shard_map/all_to_all | solution.py:143
  321.5 13.9 %collective-permute-start.27 = (bf16[96,384]{1,0:T(8,128)(2,1)S(1)}, bf16[96,384]{1,0:T(8,128)(2,1)S(1)}, u32[]{:S(2)}, u32[]{:S(2)}) collective-permute-start(bf16[96,384]{1,0:T(8,128)(2,1)S(1)} %get-tuple-element.201), channel_id=1, source_target_pairs={{0,2},{2,0},{4,6},{6,4},{1,3},{3,1},{5,7},{7,5},{8,10},{10,8},{12,... | collective-permute-start | bytes 221192 | tf_op jit(solution)/shard_map/ppermute | solution.py:30
  322.0 13.4 %collective-permute-start.28 = (bf16[96,384]{1,0:T(8,128)(2,1)S(1)}, bf16[96,384]{1,0:T(8,128)(2,1)S(1)}, u32[]{:S(2)}, u32[]{:S(2)}) collective-permute-start(bf16[96,384]{1,0:T(8,128)(2,1)S(1)} %get-tuple-element.203), channel_id=1, source_target_pairs={{0,6},{2,4},{4,2},{6,0},{1,7},{3,5},{5,3},{7,1},{8,14},{10,12},{12... | collective-permute-start | bytes 221192 | tf_op jit(solution)/shard_map/ppermute | solution.py:30
  324.7 10.7 %collective-permute-start.29 = (bf16[96,384]{1,0:T(8,128)(2,1)S(1)}, bf16[96,384]{1,0:T(8,128)(2,1)S(1)}, u32[]{:S(2)}, u32[]{:S(2)}) collective-permute-start(bf16[96,384]{1,0:T(8,128)(2,1)S(1)} %get-tuple-element.202), channel_id=1, source_target_pairs={{0,4},{2,6},{4,0},{6,2},{1,5},{3,7},{5,1},{7,3},{8,12},{10,14},{12... | collective-permute-start | bytes 221192 | tf_op jit(solution)/shard_map/ppermute | solution.py:30
  336.6 95.9 %all-to-all-start.1 = ((bf16[16,384,384]{2,1,0:T(8,128)(2,1)}), bf16[16,384,384]{2,1,0:T(8,128)(2,1)}, u32[]{:S(2)}, u32[]{:S(2)}) async-start(bf16[16,384,384]{2,1,0:T(8,128)(2,1)} %bitcast.303), calls=%async_computation.1 | async-start | bytes 9437184 | tf_op jit(solution)/shard_map/all_to_all | solution.py:143
  343.9 86.8 %all-gather.8.cloned.1.call-start = ((), (), s32[]{:S(2)}) async-start(), calls=%async_computation.6 | async-start | bytes 1880064 | tf_op jit(solution)/shard_map/all_gather | solution.py:287
  358.2 12.3 %collective-permute-start.24 = (bf16[256,768]{0,1:T(8,128)(2,1)}, bf16[256,768]{0,1:T(8,128)(2,1)S(1)}, u32[]{:S(2)}, u32[]{:S(2)}) collective-permute-start(bf16[256,768]{0,1:T(8,128)(2,1)} %get-tuple-element.173), channel_id=1, source_target_pairs={{0,2},{2,0},{4,6},{6,4},{1,3},{3,1},{5,7},{7,5},{8,10},{10,8},{12,... | collective-permute-start | bytes 1179656 | tf_op jit(solution)/shard_map/ppermute | solution.py:30
  358.3 18.8 %collective-permute-start.25 = (bf16[256,768]{0,1:T(8,128)(2,1)}, bf16[256,768]{0,1:T(8,128)(2,1)}, u32[]{:S(2)}, u32[]{:S(2)}) collective-permute-start(bf16[256,768]{0,1:T(8,128)(2,1)} %get-tuple-element.175), channel_id=1, source_target_pairs={{0,6},{2,4},{4,2},{6,0},{1,7},{3,5},{5,3},{7,1},{8,14},{10,12},{12... | collective-permute-start | bytes 1179656 | tf_op jit(solution)/shard_map/ppermute | solution.py:30
  360.9 17.9 %collective-permute-start.26 = (bf16[256,768]{0,1:T(8,128)(2,1)S(1)}, bf16[256,768]{0,1:T(8,128)(2,1)}, u32[]{:S(2)}, u32[]{:S(2)}) collective-permute-start(bf16[256,768]{0,1:T(8,128)(2,1)S(1)} %get-tuple-element.174), channel_id=1, source_target_pairs={{0,4},{2,6},{4,0},{6,2},{1,5},{3,7},{5,1},{7,3},{8,12},{10,14},{12... | collective-permute-start | bytes 1179656 | tf_op jit(solution)/shard_map/ppermute | solution.py:30
  387.1 17.5 %collective-permute-start.38 = (bf16[832,384]{1,0:T(8,128)(2,1)}, bf16[832,384]{1,0:T(8,128)(2,1)S(1)}, u32[]{:S(2)}, u32[]{:S(2)}) collective-permute-start(bf16[832,384]{1,0:T(8,128)(2,1)} %get-tuple-element.156), channel_id=1, source_target_pairs={{0,2},{2,0},{4,6},{6,4},{1,3},{3,1},{5,7},{7,5},{8,10},{10,8},{12,... | collective-permute-start | bytes 1916936 | tf_op jit(solution)/shard_map/ppermute | solution.py:30
  387.1 31.6 %collective-permute-start.39 = (bf16[832,384]{1,0:T(8,128)(2,1)}, bf16[832,384]{1,0:T(8,128)(2,1)}, u32[]{:S(2)}, u32[]{:S(2)}) collective-permute-start(bf16[832,384]{1,0:T(8,128)(2,1)} %get-tuple-element.158), channel_id=1, source_target_pairs={{0,6},{2,4},{4,2},{6,0},{1,7},{3,5},{5,3},{7,1},{8,14},{10,12},{12... | collective-permute-start | bytes 1916936 | tf_op jit(solution)/shard_map/ppermute | solution.py:30
  389.4 29.3 %collective-permute-start.40 = (bf16[832,384]{1,0:T(8,128)(2,1)}, bf16[832,384]{1,0:T(8,128)(2,1)}, u32[]{:S(2)}, u32[]{:S(2)}) collective-permute-start(bf16[832,384]{1,0:T(8,128)(2,1)} %get-tuple-element.157), channel_id=1, source_target_pairs={{0,4},{2,6},{4,0},{6,2},{1,5},{3,7},{5,1},{7,3},{8,12},{10,14},{12... | collective-permute-start | bytes 1916936 | tf_op jit(solution)/shard_map/ppermute | solution.py:30
  392.1 67.5 %collective-permute-start.17 = (bf16[256,384]{1,0:T(8,128)(2,1)}, bf16[256,384]{1,0:T(8,128)(2,1)}, u32[]{:S(2)}, u32[]{:S(2)}) collective-permute-start(bf16[256,384]{1,0:T(8,128)(2,1)} %broadcast_select_fusion.13), channel_id=1, source_target_pairs={{1,4},{3,6},{4,1},{6,3},{9,12},{11,14},{12,9},{14,11},{17,20},{19,... | collective-permute-start | bytes 589832 | tf_op jit(solution)/shard_map/ppermute | solution.py:251
  396.4 46.6 %collective-permute-start.30 = (f32[256,768]{1,0:T(8,128)}, f32[256,768]{1,0:T(8,128)}, u32[]{:S(2)}, u32[]{:S(2)}) collective-permute-start(f32[256,768]{1,0:T(8,128)} %convolution_add_fusion), channel_id=1, source_target_pairs={{0,1},{1,0},{2,3},{3,2},{4,5},{5,4},{6,7},{7,6},{8,9},{9,8},{10,11... | collective-permute-start | bytes 2359304 | tf_op jit(solution)/shard_map/ppermute | solution.py:30
  438.0 16.9 %all-to-all-start.3 = ((bf16[16,56,384]{2,1,0:T(8,128)(2,1)}), bf16[16,56,384]{2,1,0:T(8,128)(2,1)S(1)}, u32[]{:S(2)}, u32[]{:S(2)}) async-start(bf16[16,56,384]{2,1,0:T(8,128)(2,1)} %maximum_maximum_fusion), calls=%async_computation.3 | async-start | bytes 1376256 | tf_op jit(solution)/shard_map/all_to_all | solution.py:143
  449.3 20.6 %collective-permute-start.31 = (f32[256,384]{1,0:T(8,128)S(1)}, f32[256,384]{1,0:T(8,128)S(1)}, u32[]{:S(2)}, u32[]{:S(2)}) collective-permute-start(f32[256,384]{1,0:T(8,128)S(1)} %slice_select_fusion), channel_id=1, source_target_pairs={{1,4},{3,6},{4,1},{6,3},{9,12},{11,14},{12,9},{14,11},{17,20},{19,... | collective-permute-start | bytes 1179656 | tf_op jit(solution)/shard_map/ppermute | solution.py:251
  455.4 7.7 %collective-permute-start.41 = (bf16[152,384]{1,0:T(8,128)(2,1)S(1)}, bf16[152,384]{1,0:T(8,128)(2,1)S(1)}, u32[]{:S(2)}, u32[]{:S(2)}) collective-permute-start(bf16[152,384]{1,0:T(8,128)(2,1)S(1)} %maximum_maximum_fusion.1), channel_id=1, source_target_pairs={{0,24},{8,16},{16,8},{24,0},{1,25},{9,17},{17,9},{25,1},{2,26},{10... | collective-permute-start | bytes 350216 | tf_op jit(solution)/shard_map/ppermute | solution.py:30
  458.2 7.4 %collective-permute-start.42 = (bf16[152,384]{1,0:T(8,128)(2,1)S(1)}, bf16[152,384]{1,0:T(8,128)(2,1)S(1)}, u32[]{:S(2)}, u32[]{:S(2)}) collective-permute-start(bf16[152,384]{1,0:T(8,128)(2,1)S(1)} %maximum_maximum_fusion.1), channel_id=1, source_target_pairs={{0,16},{8,24},{16,0},{24,8},{1,17},{9,25},{17,1},{25,9},{2,18},{10... | collective-permute-start | bytes 350216 | tf_op jit(solution)/shard_map/ppermute | solution.py:30
  459.0 6.5 %collective-permute-start.43 = (bf16[152,384]{1,0:T(8,128)(2,1)S(1)}, bf16[152,384]{1,0:T(8,128)(2,1)S(1)}, u32[]{:S(2)}, u32[]{:S(2)}) collective-permute-start(bf16[152,384]{1,0:T(8,128)(2,1)S(1)} %maximum_maximum_fusion.1), channel_id=1, source_target_pairs={{0,8},{8,0},{16,24},{24,16},{1,9},{9,1},{17,25},{25,17},{2,10},{10... | collective-permute-start | bytes 350216 | tf_op jit(solution)/shard_map/ppermute | solution.py:30
  465.8 21.3 %collective-permute-start.44 = (bf16[4,152,384]{2,1,0:T(8,128)(2,1)S(1)}, bf16[4,152,384]{2,1,0:T(8,128)(2,1)S(1)}, u32[]{:S(2)}, u32[]{:S(2)}) collective-permute-start(bf16[4,152,384]{2,1,0:T(8,128)(2,1)S(1)} %pad_maximum_fusion.10), channel_id=1, source_target_pairs={{0,96},{32,64},{64,32},{96,0},{1,97},{33,65},{65,33},{97,1},{2,98}... | collective-permute-start | bytes 1400840 | tf_op jit(solution)/shard_map/ppermute | solution.py:30
  468.5 18.5 %collective-permute-start.45 = (bf16[4,152,384]{2,1,0:T(8,128)(2,1)S(1)}, bf16[4,152,384]{2,1,0:T(8,128)(2,1)S(1)}, u32[]{:S(2)}, u32[]{:S(2)}) collective-permute-start(bf16[4,152,384]{2,1,0:T(8,128)(2,1)S(1)} %pad_maximum_fusion.10), channel_id=1, source_target_pairs={{0,64},{32,96},{64,0},{96,32},{1,65},{33,97},{65,1},{97,33},{2,66}... | collective-permute-start | bytes 1400840 | tf_op jit(solution)/shard_map/ppermute | solution.py:30
  469.4 18.3 %collective-permute-start.46 = (bf16[4,152,384]{2,1,0:T(8,128)(2,1)S(1)}, bf16[4,152,384]{2,1,0:T(8,128)(2,1)S(1)}, u32[]{:S(2)}, u32[]{:S(2)}) collective-permute-start(bf16[4,152,384]{2,1,0:T(8,128)(2,1)S(1)} %pad_maximum_fusion.10), channel_id=1, source_target_pairs={{0,32},{32,0},{64,96},{96,64},{1,33},{33,1},{65,97},{97,65},{2,34}... | collective-permute-start | bytes 1400840 | tf_op jit(solution)/shard_map/ppermute | solution.py:30
  (184 other events, 1180.5 us)
Sparse Core Ops, SparseCore 0:
  13.5 86.1 all-gather.3
  103.1 70.6 all-gather.5
  346.9 83.7 all-gather.7

commit v4 on v3

--- a/solution.py
+++ b/solution.py
@@ -272,8 +272,7 @@
             one = plane_exchange(pieces)
         else:
             one = line_sum(one.reshape(4, 96, HALF).astype(bf16), place).astype(bf16)
-            one = jnp.concatenate([one, plane_sum(one_a).astype(bf16)], 0)
-            zero = plane_exchange(pieces)
+            zero = plane_exchange(jnp.concatenate([pieces, one_a.reshape(16, 48, HALF)], 1))
         resid_one, gain_one, shift_one = norm_backward(normed_grad, unit_one, inverse_one, gain[0])
         attn_low = resid_one.astype(bf16)
         out_bias = jnp.sum(attn_low, 0, dtype=f32)
@@ -300,8 +299,7 @@
         if l == 1:
             one = plane_sum(one)
             grad_state = grad_state + when(one)
-            one_a = (line_sum(weight_grad(pairs_a).reshape(4, PACK_A, HALF), place) + when(one)).astype(bf16)
-            one_a = plane_exchange(one_a.reshape(16, 48, HALF))
+            one_a = line_sum(weight_grad(pairs_a).reshape(4, PACK_A, HALF), place).astype(bf16)
         else:
             wide = jnp.stack(wide)
             small = [
@@ -320,18 +318,17 @@
     small = small.reshape(3, 16, 2, HALF).transpose(1, 0, 2, 3).reshape(16, 6, HALF)
     zero_a = (zero_a[:PACK_A] + when(zero)).astype(bf16).reshape(16, 48, HALF)
     moved = plane_exchange(jnp.concatenate([zero_a, small, jnp.zeros((16, 2, HALF), bf16)], 1))
-    zero_b = line_sum(zero.reshape(4, 96, HALF).astype(bf16), place).astype(bf16)
+    zero_b = line_sum(zero[:HALF].reshape(4, 96, HALF).astype(bf16), place).astype(bf16)
     small = split3(jnp.sum(moved[:, 48:54].reshape(48, 2, HALF), 0, dtype=f32)).reshape(6, HALF)
     zero_a = plane_sum(moved[:, :48]).astype(bf16)
-    zero = jnp.concatenate([zero_b, zero_a, small, jnp.zeros((2, HALF), bf16)], 0)
+    zero = jnp.concatenate([zero_b, zero[HALF:].astype(bf16), zero_a, small, jnp.zeros((2, HALF), bf16)], 0)
     zero = jnp.stack(in_order(near_first(gather(zero, "y")), at_y))
-    zero = jnp.stack(in_order(near_first(gather(zero, "x")), at_x)).reshape(16, 152, HALF)
-    own = jnp.sum(zero[:, 144:150].reshape(16, 3, 2, HALF), 1, dtype=f32).reshape(32 * HALF)
+    zero = jnp.stack(in_order(near_first(gather(zero, "x")), at_x)).reshape(16, 200, HALF)
+    own = jnp.sum(zero[:, 192:198].reshape(16, 3, 2, HALF), 1, dtype=f32).reshape(32 * HALF)
     wide = own[: 12 * HALF].reshape(LAYERS, 6, HALF)
     own = own[12 * HALF : SMALL * HALF].reshape(LAYERS, 3 * BLOCK + HID)
-    one = one.reshape(16, 144, HALF)
-    grad_a = [zero[:, 96:144].reshape(PACK_A, HALF), one[:, 96:].reshape(PACK_A, HALF)]
-    grad_b = [zero[:, :96].reshape(PACK_B, HALF), one[:, :96].reshape(PACK_B, HALF)]
+    grad_a = [zero[:, 144:192].reshape(PACK_A, HALF), zero[:, 96:144].reshape(PACK_A, HALF)]
+    grad_b = [zero[:, :96].reshape(PACK_B, HALF), one.reshape(PACK_B, HALF)]
 
     def both(parts, turn):
         return jnp.stack([part.T if turn else part for part in parts]).astype(f32)

time: 518 us -> 516 us (level)
  waiting for transfers between devices: 183 us -> 198 us
  starting transfers between devices: 94.3 us -> 84.6 us
  matrix products: 91 us -> 84.7 us
  local copies, waits for them, and re-layouts: 59.3 us -> 54.1 us
    ppermute x44, waiting for transfers between devices: 141 us -> 162 us  [swapped(): return lax.ppermute(value, axes, [(i, i ^ bits) for i in range(count)])]
    all_to_all x4 -> x3, waiting for transfers between devices: 15 us -> 5.35 us  [plane_exchange(): return lax.all_to_all(pieces, PLANE, 0, 0, tiled=True)]
    all_to_all x4 -> x3, starting transfers between devices: 32.2 us -> 23.3 us  [plane_exchange(): return lax.all_to_all(pieces, PLANE, 0, 0, tiled=True)]
    dot_general x64, matrix products: 58.4 us -> 52.1 us  [dot(): lax.dot_general(left, right, ((dims[0], dims[1]), ((), ())), preferred_el...]
    unnamed x371 -> x381, local copies, waits for them, and re-layouts: 16.9 us -> 16.6 us
  transfers between devices with their start and end apart: 54 -> 53, of which waited for: 26 -> 27; matrix products, arithmetic and copies ran while one was open for 31% -> 27% of each run, Pallas kernels for 0% -> 0%
where the time goes in v4:
time: 516 us; the launch traced here: 506 us
  waiting for transfers between devices  198 us (38%)
  matrix products  84.7 us (16%)
  starting transfers between devices  84.6 us (16%)
  other arithmetic  63.8 us (12%)
  local copies, waits for them, and re-layouts  54.1 us (10%)
  between operations  20.5 us (4%)
    ppermute x44, waiting for transfers between devices, swapped(): return lax.ppermute(value, axes, [(i, i ^ bits) for i in range(count)])  162 us
    ppermute x44, starting transfers between devices, swapped(): return lax.ppermute(value, axes, [(i, i ^ bits) for i in range(count)])  58.3 us
    dot_general x64, matrix products, dot(): lax.dot_general(left, right, ((dims[0], dims[1]), ((), ())), preferred_el...  52.1 us
    all_to_all x3, starting transfers between devices, plane_exchange(): return lax.all_to_all(pieces, PLANE, 0, 0, tiled=True)  23.3 us
    all_gather x1, waiting for transfers between devices, on_device(): lax.all_gather(later, LINE + PLANE, axis=0, tiled=True)  16.9 us
    unnamed x381, local copies, waits for them, and re-layouts  16.6 us
    all_gather x1, waiting for transfers between devices, on_device(): one = lax.all_gather(one, PLANE, axis=0, tiled=True)  13.6 us
    sub x2, matrix products, attend_forward(): raised = jnp.exp(scores - peak)  10.6 us
  transfers between devices with their start and end apart: 53, of which 27 were waited for; matrix products, arithmetic and copies ran while one was open for 27% of the time, Pallas kernels for 0%

profile of v4, /device:TPU:0, one launch (start us, length us, event | category | flops | bytes accessed | tf_op | source)
XLA Modules:
  0.0 506.2 jit_solution(10336225411549205857)
XLA Ops:
  14.4 4.1 collective-permute-start.2
  22.9 24.8 %collective-permute-done.5 = bf16[2,1152]{1,0:T(2,128)(2,1)S(1)} collective-permute-done((bf16[2,1152]{1,0:T(2,128)(2,1)S(1)}, bf16[2,1152]{1,0:T(2,128)(2,1)S(1)}, u32[]{:S(2)}, u32[]{:S(2)}) %collective-permute-start.5) | collective-permute-done | bytes 4640 | tf_op jit(solution)/shard_map/ppermute | solution.py:30
  49.7 3.6 collective-permute-start.1
  58.9 3.2 collective-permute-start.8
  62.2 8.6 %collective-permute-done.6 = bf16[256,768]{0,1:T(8,128)(2,1)S(1)} collective-permute-done((bf16[256,768]{0,1:T(8,128)(2,1)S(1)}, bf16[256,768]{0,1:T(8,128)(2,1)S(1)}, u32[]{:S(2)}, u32[]{:S(2)}) %collective-permute-start.6) | collective-permute-done | bytes 393248 | tf_op jit(solution)/shard_map/ppermute | solution.py:30
  70.8 8.8 %collective-permute-done.7 = bf16[256,768]{0,1:T(8,128)(2,1)S(1)} collective-permute-done((bf16[256,768]{0,1:T(8,128)(2,1)S(1)}, bf16[256,768]{0,1:T(8,128)(2,1)S(1)}, u32[]{:S(2)}, u32[]{:S(2)}) %collective-permute-start.7) | collective-permute-done | bytes 393248 | tf_op jit(solution)/shard_map/ppermute | solution.py:30
  79.7 3.2 collective-permute-done.8
  86.5 4.8 fusion.256
  91.9 4.4 fusion.60
  101.3 2.8 slice_bitcast_fusion.4
  104.1 3.1 multiply_convert_fusion.5
  108.0 3.1 multiply_convert_fusion.4
  117.1 3.1 collective-permute-start.13
  122.0 7.1 %collective-permute-done.12 = bf16[256,768]{0,1:T(8,128)(2,1)S(1)} collective-permute-done((bf16[256,768]{0,1:T(8,128)(2,1)S(1)}, bf16[256,768]{0,1:T(8,128)(2,1)S(1)}, u32[]{:S(2)}, u32[]{:S(2)}) %collective-permute-start.12) | collective-permute-done | bytes 393248 | tf_op jit(solution)/shard_map/ppermute | solution.py:30
  129.1 10.0 %collective-permute-done.13 = bf16[256,768]{0,1:T(8,128)(2,1)S(1)} collective-permute-done((bf16[256,768]{0,1:T(8,128)(2,1)S(1)}, bf16[256,768]{0,1:T(8,128)(2,1)S(1)}, u32[]{:S(2)}, u32[]{:S(2)}) %collective-permute-start.13) | collective-permute-done | bytes 393248 | tf_op jit(solution)/shard_map/ppermute | solution.py:30
  144.4 5.8 %fusion.257 = (f32[6,256]{1,0:T(8,128)S(1)}, f32[6,256,1024]{2,1,0:T(8,128)}) fusion(pred[1024]{0:T(1024)(128)(4,1)S(1)} %copy-done.174, bf16[256,6,64]{0,2,1:T(8,128)(2,1)S(1)} %bitcast.347, bf16[1024,6,64]{0,2,1:T(8,128)(2,1)} %bitcast.329), kind=kOutput, calls=%fused_computation.614 | convolution fusion | flops 207619072 | bytes 7281664 | tf_op jit(solution)/shard_map/sub | solution.py:103
  150.2 4.3 fusion.63
  157.0 16.9 %all-gather.6.cloned.1.call-done = bf16[1536,1536]{1,0:T(8,128)(2,1)} async-done(((bf16[24,1536]{1,0:T(8,128)(2,1)}), bf16[1536,1536]{1,0:T(8,128)(2,1)}) %all-gather.6.cloned.1.call-update) | async-done | bytes 4718608 | tf_op jit(solution)/shard_map/all_gather | solution.py:176
  179.5 3.2 multiply_convert_fusion.3
  183.3 3.1 multiply_convert_fusion.2
  195.8 3.0 convert_reduce_fusion.4
  200.8 2.9 convert_reduce_fusion.2
  208.6 2.8 copy.101
  211.5 4.8 all-to-all-start
  216.4 3.6 multiply_reduce_fusion.3
  222.3 3.9 multiply_reduce_fusion.1
  234.8 6.7 %collective-permute-done.19 = bf16[256,768]{0,1:T(8,128)(2,1)S(1)} collective-permute-done((bf16[256,768]{0,1:T(8,128)(2,1)S(1)}, bf16[256,768]{0,1:T(8,128)(2,1)S(1)}, u32[]{:S(2)}, u32[]{:S(2)}) %collective-permute-start.19) | collective-permute-done | bytes 393248 | tf_op jit(solution)/shard_map/ppermute | solution.py:30
  241.5 9.2 %collective-permute-done.20 = bf16[256,768]{0,1:T(8,128)(2,1)S(1)} collective-permute-done((bf16[256,768]{0,1:T(8,128)(2,1)S(1)}, bf16[256,768]{0,1:T(8,128)(2,1)S(1)}, u32[]{:S(2)}, u32[]{:S(2)}) %collective-permute-start.20) | collective-permute-done | bytes 393248 | tf_op jit(solution)/shard_map/ppermute | solution.py:30
  266.9 5.0 collective-permute-done.32
  271.9 10.3 %collective-permute-done.33 = bf16[768,384]{1,0:T(8,128)(2,1)} collective-permute-done((bf16[768,384]{1,0:T(8,128)(2,1)}, bf16[768,384]{1,0:T(8,128)(2,1)}, u32[]{:S(2)}, u32[]{:S(2)}) %collective-permute-start.33) | collective-permute-done | bytes 589856 | tf_op jit(solution)/shard_map/ppermute | solution.py:30
  286.7 3.0 convert_reduce_fusion.1
  294.5 3.0 convert_reduce_fusion.5
  299.4 3.0 convert_reduce_fusion.3
  312.2 2.8 pad_maximum_fusion
  316.8 7.9 %all-to-all-start.1 = ((bf16[16,432,384]{2,1,0:T(8,128)(2,1)}), bf16[16,432,384]{2,1,0:T(8,128)(2,1)}, u32[]{:S(2)}, u32[]{:S(2)}) async-start(bf16[16,432,384]{2,1,0:T(8,128)(2,1)} %pad_maximum_fusion), calls=%async_computation.1 | async-start | bytes 10616832 | tf_op jit(solution)/shard_map/all_to_all | solution.py:143
  330.9 3.7 multiply_reduce_fusion
  344.8 7.9 %collective-permute-done.24 = bf16[256,768]{0,1:T(8,128)(2,1)S(1)} collective-permute-done((bf16[256,768]{0,1:T(8,128)(2,1)}, bf16[256,768]{0,1:T(8,128)(2,1)S(1)}, u32[]{:S(2)}, u32[]{:S(2)}) %collective-permute-start.24) | collective-permute-done | bytes 393248 | tf_op jit(solution)/shard_map/ppermute | solution.py:30
  352.7 7.1 %collective-permute-done.25 = bf16[256,768]{0,1:T(8,128)(2,1)} collective-permute-done((bf16[256,768]{0,1:T(8,128)(2,1)}, bf16[256,768]{0,1:T(8,128)(2,1)}, u32[]{:S(2)}, u32[]{:S(2)}) %collective-permute-start.25) | collective-permute-done | bytes 393248 | tf_op jit(solution)/shard_map/ppermute | solution.py:30
  381.6 5.7 %collective-permute-done.38 = bf16[832,384]{1,0:T(8,128)(2,1)S(1)} collective-permute-done((bf16[832,384]{1,0:T(8,128)(2,1)}, bf16[832,384]{1,0:T(8,128)(2,1)S(1)}, u32[]{:S(2)}, u32[]{:S(2)}) %collective-permute-start.38) | collective-permute-done | bytes 639008 | tf_op jit(solution)/shard_map/ppermute | solution.py:30
  387.4 14.6 %collective-permute-done.39 = bf16[832,384]{1,0:T(8,128)(2,1)} collective-permute-done((bf16[832,384]{1,0:T(8,128)(2,1)}, bf16[832,384]{1,0:T(8,128)(2,1)}, u32[]{:S(2)}, u32[]{:S(2)}) %collective-permute-start.39) | collective-permute-done | bytes 639008 | tf_op jit(solution)/shard_map/ppermute | solution.py:30
  404.0 13.6 %all-gather.8.cloned.1.call-done = bf16[1536,384]{1,0:T(8,128)(2,1)} async-done(((bf16[96,384]{1,0:T(8,128)(2,1)}), bf16[1536,384]{1,0:T(8,128)(2,1)}) %all-gather.8.cloned.1.call-update) | async-done | bytes 1179664 | tf_op jit(solution)/shard_map/all_gather | solution.py:286
  419.5 3.4 convert_reduce_fusion
  425.3 10.6 %all-to-all-start.2 = ((bf16[16,56,384]{2,1,0:T(8,128)(2,1)}), bf16[16,56,384]{2,1,0:T(8,128)(2,1)S(1)}, u32[]{:S(2)}, u32[]{:S(2)}) async-start(bf16[16,56,384]{2,1,0:T(8,128)(2,1)} %maximum_maximum_fusion), calls=%async_computation.2 | async-start | bytes 1376256 | tf_op jit(solution)/shard_map/all_to_all | solution.py:143
  437.2 3.0 collective-permute-start.37
  443.1 5.3 %all-to-all-done.2 = bf16[16,56,384]{2,1,0:T(8,128)(2,1)S(1)} async-done(((bf16[16,56,384]{2,1,0:T(8,128)(2,1)}), bf16[16,56,384]{2,1,0:T(8,128)(2,1)S(1)}, u32[]{:S(2)}, u32[]{:S(2)}) %all-to-all-start.2) | async-done | bytes 688160 | tf_op jit(solution)/shard_map/all_to_all | solution.py:143
  453.8 3.2 collective-permute-done.41
  464.9 19.7 %collective-permute-done.44 = bf16[4,200,384]{2,1,0:T(8,128)(2,1)S(1)} collective-permute-done((bf16[4,200,384]{2,1,0:T(8,128)(2,1)S(1)}, bf16[4,200,384]{2,1,0:T(8,128)(2,1)S(1)}, u32[]{:S(2)}, u32[]{:S(2)}) %collective-permute-start.44) | collective-permute-done | bytes 614432 | tf_op jit(solution)/shard_map/ppermute | solution.py:30
  494.3 2.9 maximum_convert_fusion.1
  (721 shorter events, 184.8 us)
Async XLA Ops:
  7.2 94.1 %all-gather.4.cloned.1.call-start = ((), (), s32[]{:S(2)}) async-start(), calls=%async_computation.3 | async-start | bytes 7188480 | tf_op jit(solution)/shard_map/all_gather | solution.py:175
  13.4 160.5 %all-gather.6.cloned.1.call-start = ((), (), s32[]{:S(2)}) async-start(), calls=%async_computation.4 | async-start | bytes 4792320 | tf_op jit(solution)/shard_map/all_gather | solution.py:176
  14.4 39.6 %collective-permute-start.2 = (bf16[384,768]{0,1:T(8,128)(2,1)}, bf16[384,768]{0,1:T(8,128)(2,1)S(1)}, u32[]{:S(2)}, u32[]{:S(2)}) collective-permute-start(bf16[384,768]{0,1:T(8,128)(2,1)} %pad_maximum_fusion.11), channel_id=1, source_target_pairs={{0,6},{2,4},{4,2},{6,0},{1,7},{3,5},{5,3},{7,1},{8,14},{10,12},{12... | collective-permute-start | bytes 1769480 | tf_op jit(solution)/shard_map/ppermute | solution.py:30
  18.5 35.4 %collective-permute-start.3 = (bf16[384,768]{0,1:T(8,128)(2,1)}, bf16[384,768]{0,1:T(8,128)(2,1)S(1)}, u32[]{:S(2)}, u32[]{:S(2)}) collective-permute-start(bf16[384,768]{0,1:T(8,128)(2,1)} %pad_maximum_fusion.11), channel_id=1, source_target_pairs={{0,4},{2,6},{4,0},{6,2},{1,5},{3,7},{5,1},{7,3},{8,12},{10,14},{12... | collective-permute-start | bytes 1769480 | tf_op jit(solution)/shard_map/ppermute | solution.py:30
  18.5 36.3 %collective-permute-start.4 = (bf16[384,768]{0,1:T(8,128)(2,1)}, bf16[384,768]{0,1:T(8,128)(2,1)}, u32[]{:S(2)}, u32[]{:S(2)}) collective-permute-start(bf16[384,768]{0,1:T(8,128)(2,1)} %pad_maximum_fusion.11), channel_id=1, source_target_pairs={{0,2},{2,0},{4,6},{6,4},{1,3},{3,1},{5,7},{7,5},{8,10},{10,8},{12,... | collective-permute-start | bytes 1769480 | tf_op jit(solution)/shard_map/ppermute | solution.py:30
  19.5 28.2 %collective-permute-start.5 = (bf16[2,1152]{1,0:T(2,128)(2,1)S(1)}, bf16[2,1152]{1,0:T(2,128)(2,1)S(1)}, u32[]{:S(2)}, u32[]{:S(2)}) collective-permute-start(bf16[2,1152]{1,0:T(2,128)(2,1)S(1)} %constant_dynamic-update-slice_fusion.2), channel_id=1, source_target_pairs={{0,2},{2,0},{1,3},{3,1},{4,6},{6,4},{5,7},{7,5},{8,10},{10,8},{9,1... | collective-permute-start | bytes 13832 | tf_op jit(solution)/shard_map/ppermute | solution.py:30
  20.8 28.8 %collective-permute-start = (bf16[512,384]{1,0:T(8,128)(2,1)S(1)}, bf16[512,384]{1,0:T(8,128)(2,1)S(1)}, u32[]{:S(2)}, u32[]{:S(2)}) collective-permute-start(bf16[512,384]{1,0:T(8,128)(2,1)S(1)} %constant_dynamic-update-slice_fusion), channel_id=1, source_target_pairs={{1,4},{3,6},{4,1},{6,3},{9,12},{11,14},{12,9},{14,11},{17,20},{19,... | collective-permute-start | bytes 1179656 | tf_op jit(solution)/shard_map/ppermute | solution.py:203
  47.7 50.9 %collective-permute-start.10 = (bf16[2,6,384]{2,1,0:T(8,128)(2,1)}, bf16[2,6,384]{2,1,0:T(8,128)(2,1)}, u32[]{:S(2)}, u32[]{:S(2)}) collective-permute-start(bf16[2,6,384]{2,1,0:T(8,128)(2,1)} %get-tuple-element.241), channel_id=1, source_target_pairs={{0,4},{4,0},{1,5},{5,1},{2,6},{6,2},{3,7},{7,3},{8,12},{12,8},{9,1... | collective-permute-start | bytes 27656 | tf_op jit(solution)/shard_map/ppermute | solution.py:30
  49.7 7.0 %collective-permute-start.1 = (bf16[512,384]{1,0:T(8,128)(2,1)S(1)}, bf16[512,384]{1,0:T(8,128)(2,1)S(1)}, u32[]{:S(2)}, u32[]{:S(2)}) collective-permute-start(bf16[512,384]{1,0:T(8,128)(2,1)S(1)} %broadcast_select_fusion.12), channel_id=1, source_target_pairs={{0,1},{1,0},{2,3},{3,2},{4,5},{5,4},{6,7},{7,6},{8,9},{9,8},{10,11... | collective-permute-start | bytes 1179656 | tf_op jit(solution)/shard_map/ppermute | solution.py:30
  57.9 13.0 %collective-permute-start.6 = (bf16[256,768]{0,1:T(8,128)(2,1)S(1)}, bf16[256,768]{0,1:T(8,128)(2,1)S(1)}, u32[]{:S(2)}, u32[]{:S(2)}) collective-permute-start(bf16[256,768]{0,1:T(8,128)(2,1)S(1)} %pad_maximum_fusion.14), channel_id=1, source_target_pairs={{0,2},{2,0},{4,6},{6,4},{1,3},{3,1},{5,7},{7,5},{8,10},{10,8},{12,... | collective-permute-start | bytes 1179656 | tf_op jit(solution)/shard_map/ppermute | solution.py:30
  58.0 21.7 %collective-permute-start.7 = (bf16[256,768]{0,1:T(8,128)(2,1)S(1)}, bf16[256,768]{0,1:T(8,128)(2,1)S(1)}, u32[]{:S(2)}, u32[]{:S(2)}) collective-permute-start(bf16[256,768]{0,1:T(8,128)(2,1)S(1)} %pad_maximum_fusion.14), channel_id=1, source_target_pairs={{0,6},{2,4},{4,2},{6,0},{1,7},{3,5},{5,3},{7,1},{8,14},{10,12},{12... | collective-permute-start | bytes 1179656 | tf_op jit(solution)/shard_map/ppermute | solution.py:30
  58.9 24.0 %collective-permute-start.8 = (bf16[256,768]{0,1:T(8,128)(2,1)S(1)}, bf16[256,768]{0,1:T(8,128)(2,1)S(1)}, u32[]{:S(2)}, u32[]{:S(2)}) collective-permute-start(bf16[256,768]{0,1:T(8,128)(2,1)S(1)} %pad_maximum_fusion.14), channel_id=1, source_target_pairs={{0,4},{2,6},{4,0},{6,2},{1,5},{3,7},{5,1},{7,3},{8,12},{10,14},{12... | collective-permute-start | bytes 1179656 | tf_op jit(solution)/shard_map/ppermute | solution.py:30
  116.7 12.4 %collective-permute-start.12 = (bf16[256,768]{0,1:T(8,128)(2,1)S(1)}, bf16[256,768]{0,1:T(8,128)(2,1)S(1)}, u32[]{:S(2)}, u32[]{:S(2)}) collective-permute-start(bf16[256,768]{0,1:T(8,128)(2,1)S(1)} %pad_maximum_fusion.15), channel_id=1, source_target_pairs={{0,2},{2,0},{4,6},{6,4},{1,3},{3,1},{5,7},{7,5},{8,10},{10,8},{12,... | collective-permute-start | bytes 1179656 | tf_op jit(solution)/shard_map/ppermute | solution.py:30
  117.1 21.9 %collective-permute-start.13 = (bf16[256,768]{0,1:T(8,128)(2,1)S(1)}, bf16[256,768]{0,1:T(8,128)(2,1)S(1)}, u32[]{:S(2)}, u32[]{:S(2)}) collective-permute-start(bf16[256,768]{0,1:T(8,128)(2,1)S(1)} %pad_maximum_fusion.15), channel_id=1, source_target_pairs={{0,6},{2,4},{4,2},{6,0},{1,7},{3,5},{5,3},{7,1},{8,14},{10,12},{12... | collective-permute-start | bytes 1179656 | tf_op jit(solution)/shard_map/ppermute | solution.py:30
  120.3 20.3 %collective-permute-start.14 = (bf16[256,768]{0,1:T(8,128)(2,1)S(1)}, bf16[256,768]{0,1:T(8,128)(2,1)S(1)}, u32[]{:S(2)}, u32[]{:S(2)}) collective-permute-start(bf16[256,768]{0,1:T(8,128)(2,1)S(1)} %pad_maximum_fusion.15), channel_id=1, source_target_pairs={{0,4},{2,6},{4,0},{6,2},{1,5},{3,7},{5,1},{7,3},{8,12},{10,14},{12... | collective-permute-start | bytes 1179656 | tf_op jit(solution)/shard_map/ppermute | solution.py:30
  156.4 20.3 %collective-permute-start.15 = (f32[256,768]{1,0:T(8,128)}, f32[256,768]{1,0:T(8,128)S(1)}, u32[]{:S(2)}, u32[]{:S(2)}) collective-permute-start(f32[256,768]{1,0:T(8,128)} %convolution_add_fusion.7), channel_id=1, source_target_pairs={{0,1},{1,0},{2,3},{3,2},{4,5},{5,4},{6,7},{7,6},{8,9},{9,8},{10,11... | collective-permute-start | bytes 2359304 | tf_op jit(solution)/shard_map/ppermute | solution.py:30
  205.1 11.1 %collective-permute-start.18 = (f32[256,768]{1,0:T(8,128)}, f32[256,768]{1,0:T(8,128)}, u32[]{:S(2)}, u32[]{:S(2)}) collective-permute-start(f32[256,768]{1,0:T(8,128)} %convolution_add_fusion.3), channel_id=1, source_target_pairs={{0,1},{1,0},{2,3},{3,2},{4,5},{5,4},{6,7},{7,6},{8,9},{9,8},{10,11... | collective-permute-start | bytes 2359304 | tf_op jit(solution)/shard_map/ppermute | solution.py:30
  211.5 75.2 %all-to-all-start = ((bf16[16,384,384]{2,1,0:T(8,128)(2,1)}), bf16[16,384,384]{2,1,0:T(8,128)(2,1)}, u32[]{:S(2)}, u32[]{:S(2)}) async-start(bf16[16,384,384]{2,1,0:T(8,128)(2,1)} %bitcast.302), calls=%async_computation | async-start | bytes 9437184 | tf_op jit(solution)/shard_map/all_to_all | solution.py:143
  229.5 12.0 %collective-permute-start.19 = (bf16[256,768]{0,1:T(8,128)(2,1)S(1)}, bf16[256,768]{0,1:T(8,128)(2,1)S(1)}, u32[]{:S(2)}, u32[]{:S(2)}) collective-permute-start(bf16[256,768]{0,1:T(8,128)(2,1)S(1)} %get-tuple-element.178), channel_id=1, source_target_pairs={{0,2},{2,0},{4,6},{6,4},{1,3},{3,1},{5,7},{7,5},{8,10},{10,8},{12,... | collective-permute-start | bytes 1179656 | tf_op jit(solution)/shard_map/ppermute | solution.py:30
  229.7 21.0 %collective-permute-start.20 = (bf16[256,768]{0,1:T(8,128)(2,1)S(1)}, bf16[256,768]{0,1:T(8,128)(2,1)S(1)}, u32[]{:S(2)}, u32[]{:S(2)}) collective-permute-start(bf16[256,768]{0,1:T(8,128)(2,1)S(1)} %get-tuple-element.180), channel_id=1, source_target_pairs={{0,6},{2,4},{4,2},{6,0},{1,7},{3,5},{5,3},{7,1},{8,14},{10,12},{12... | collective-permute-start | bytes 1179656 | tf_op jit(solution)/shard_map/ppermute | solution.py:30
  231.7 19.0 %collective-permute-start.21 = (bf16[256,768]{0,1:T(8,128)(2,1)S(1)}, bf16[256,768]{0,1:T(8,128)(2,1)S(1)}, u32[]{:S(2)}, u32[]{:S(2)}) collective-permute-start(bf16[256,768]{0,1:T(8,128)(2,1)S(1)} %get-tuple-element.179), channel_id=1, source_target_pairs={{0,4},{2,6},{4,0},{6,2},{1,5},{3,7},{5,1},{7,3},{8,12},{10,14},{12... | collective-permute-start | bytes 1179656 | tf_op jit(solution)/shard_map/ppermute | solution.py:30
  255.4 16.5 %collective-permute-start.32 = (bf16[768,384]{1,0:T(8,128)(2,1)}, bf16[768,384]{1,0:T(8,128)(2,1)S(1)}, u32[]{:S(2)}, u32[]{:S(2)}) collective-permute-start(bf16[768,384]{1,0:T(8,128)(2,1)} %get-tuple-element.168), channel_id=1, source_target_pairs={{0,2},{2,0},{4,6},{6,4},{1,3},{3,1},{5,7},{7,5},{8,10},{10,8},{12,... | collective-permute-start | bytes 1769480 | tf_op jit(solution)/shard_map/ppermute | solution.py:30
  255.9 26.4 %collective-permute-start.33 = (bf16[768,384]{1,0:T(8,128)(2,1)}, bf16[768,384]{1,0:T(8,128)(2,1)}, u32[]{:S(2)}, u32[]{:S(2)}) collective-permute-start(bf16[768,384]{1,0:T(8,128)(2,1)} %get-tuple-element.170), channel_id=1, source_target_pairs={{0,6},{2,4},{4,2},{6,0},{1,7},{3,5},{5,3},{7,1},{8,14},{10,12},{12... | collective-permute-start | bytes 1769480 | tf_op jit(solution)/shard_map/ppermute | solution.py:30
  257.2 27.0 %collective-permute-start.34 = (bf16[768,384]{1,0:T(8,128)(2,1)}, bf16[768,384]{1,0:T(8,128)(2,1)}, u32[]{:S(2)}, u32[]{:S(2)}) collective-permute-start(bf16[768,384]{1,0:T(8,128)(2,1)} %get-tuple-element.169), channel_id=1, source_target_pairs={{0,4},{2,6},{4,0},{6,2},{1,5},{3,7},{5,1},{7,3},{8,12},{10,14},{12... | collective-permute-start | bytes 1769480 | tf_op jit(solution)/shard_map/ppermute | solution.py:30
  261.6 29.3 %collective-permute-start.22 = (f32[256,768]{1,0:T(8,128)}, f32[256,768]{1,0:T(8,128)}, u32[]{:S(2)}, u32[]{:S(2)}) collective-permute-start(f32[256,768]{1,0:T(8,128)} %convolution_add_fusion.2), channel_id=1, source_target_pairs={{0,1},{1,0},{2,3},{3,2},{4,5},{5,4},{6,7},{7,6},{8,9},{9,8},{10,11... | collective-permute-start | bytes 2359304 | tf_op jit(solution)/shard_map/ppermute | solution.py:30
  302.9 24.3 %collective-permute-start.23 = (f32[256,768]{1,0:T(8,128)S(1)}, f32[256,768]{1,0:T(8,128)}, u32[]{:S(2)}, u32[]{:S(2)}) collective-permute-start(f32[256,768]{1,0:T(8,128)S(1)} %convolution_add_fusion.1), channel_id=1, source_target_pairs={{0,1},{1,0},{2,3},{3,2},{4,5},{5,4},{6,7},{7,6},{8,9},{9,8},{10,11... | collective-permute-start | bytes 2359304 | tf_op jit(solution)/shard_map/ppermute | solution.py:30
  303.7 21.2 %collective-permute-start.27 = (bf16[96,384]{1,0:T(8,128)(2,1)}, bf16[96,384]{1,0:T(8,128)(2,1)S(1)}, u32[]{:S(2)}, u32[]{:S(2)}) collective-permute-start(bf16[96,384]{1,0:T(8,128)(2,1)} %get-tuple-element.205), channel_id=1, source_target_pairs={{0,2},{2,0},{4,6},{6,4},{1,3},{3,1},{5,7},{7,5},{8,10},{10,8},{12,... | collective-permute-start | bytes 221192 | tf_op jit(solution)/shard_map/ppermute | solution.py:30
  304.0 21.0 %collective-permute-start.28 = (bf16[96,384]{1,0:T(8,128)(2,1)}, bf16[96,384]{1,0:T(8,128)(2,1)S(1)}, u32[]{:S(2)}, u32[]{:S(2)}) collective-permute-start(bf16[96,384]{1,0:T(8,128)(2,1)} %get-tuple-element.207), channel_id=1, source_target_pairs={{0,6},{2,4},{4,2},{6,0},{1,7},{3,5},{5,3},{7,1},{8,14},{10,12},{12... | collective-permute-start | bytes 221192 | tf_op jit(solution)/shard_map/ppermute | solution.py:30
  306.0 18.9 %collective-permute-start.29 = (bf16[96,384]{1,0:T(8,128)(2,1)S(1)}, bf16[96,384]{1,0:T(8,128)(2,1)}, u32[]{:S(2)}, u32[]{:S(2)}) collective-permute-start(bf16[96,384]{1,0:T(8,128)(2,1)S(1)} %get-tuple-element.206), channel_id=1, source_target_pairs={{0,4},{2,6},{4,0},{6,2},{1,5},{3,7},{5,1},{7,3},{8,12},{10,14},{12... | collective-permute-start | bytes 221192 | tf_op jit(solution)/shard_map/ppermute | solution.py:30
  316.8 102.7 %all-to-all-start.1 = ((bf16[16,432,384]{2,1,0:T(8,128)(2,1)}), bf16[16,432,384]{2,1,0:T(8,128)(2,1)}, u32[]{:S(2)}, u32[]{:S(2)}) async-start(bf16[16,432,384]{2,1,0:T(8,128)(2,1)} %pad_maximum_fusion), calls=%async_computation.1 | async-start | bytes 10616832 | tf_op jit(solution)/shard_map/all_to_all | solution.py:143
  324.7 93.0 %all-gather.8.cloned.1.call-start = ((), (), s32[]{:S(2)}) async-start(), calls=%async_computation.5 | async-start | bytes 1253376 | tf_op jit(solution)/shard_map/all_gather | solution.py:286
  340.5 12.2 %collective-permute-start.24 = (bf16[256,768]{0,1:T(8,128)(2,1)}, bf16[256,768]{0,1:T(8,128)(2,1)S(1)}, u32[]{:S(2)}, u32[]{:S(2)}) collective-permute-start(bf16[256,768]{0,1:T(8,128)(2,1)} %get-tuple-element.175), channel_id=1, source_target_pairs={{0,2},{2,0},{4,6},{6,4},{1,3},{3,1},{5,7},{7,5},{8,10},{10,8},{12,... | collective-permute-start | bytes 1179656 | tf_op jit(solution)/shard_map/ppermute | solution.py:30
  341.1 18.7 %collective-permute-start.25 = (bf16[256,768]{0,1:T(8,128)(2,1)}, bf16[256,768]{0,1:T(8,128)(2,1)}, u32[]{:S(2)}, u32[]{:S(2)}) collective-permute-start(bf16[256,768]{0,1:T(8,128)(2,1)} %get-tuple-element.177), channel_id=1, source_target_pairs={{0,6},{2,4},{4,2},{6,0},{1,7},{3,5},{5,3},{7,1},{8,14},{10,12},{12... | collective-permute-start | bytes 1179656 | tf_op jit(solution)/shard_map/ppermute | solution.py:30
  343.1 18.6 %collective-permute-start.26 = (bf16[256,768]{0,1:T(8,128)(2,1)S(1)}, bf16[256,768]{0,1:T(8,128)(2,1)}, u32[]{:S(2)}, u32[]{:S(2)}) collective-permute-start(bf16[256,768]{0,1:T(8,128)(2,1)S(1)} %get-tuple-element.176), channel_id=1, source_target_pairs={{0,4},{2,6},{4,0},{6,2},{1,5},{3,7},{5,1},{7,3},{8,12},{10,14},{12... | collective-permute-start | bytes 1179656 | tf_op jit(solution)/shard_map/ppermute | solution.py:30
  369.8 17.5 %collective-permute-start.38 = (bf16[832,384]{1,0:T(8,128)(2,1)}, bf16[832,384]{1,0:T(8,128)(2,1)S(1)}, u32[]{:S(2)}, u32[]{:S(2)}) collective-permute-start(bf16[832,384]{1,0:T(8,128)(2,1)} %get-tuple-element.156), channel_id=1, source_target_pairs={{0,2},{2,0},{4,6},{6,4},{1,3},{3,1},{5,7},{7,5},{8,10},{10,8},{12,... | collective-permute-start | bytes 1916936 | tf_op jit(solution)/shard_map/ppermute | solution.py:30
  369.8 32.1 %collective-permute-start.39 = (bf16[832,384]{1,0:T(8,128)(2,1)}, bf16[832,384]{1,0:T(8,128)(2,1)}, u32[]{:S(2)}, u32[]{:S(2)}) collective-permute-start(bf16[832,384]{1,0:T(8,128)(2,1)} %get-tuple-element.158), channel_id=1, source_target_pairs={{0,6},{2,4},{4,2},{6,0},{1,7},{3,5},{5,3},{7,1},{8,14},{10,12},{12... | collective-permute-start | bytes 1916936 | tf_op jit(solution)/shard_map/ppermute | solution.py:30
  372.1 29.8 %collective-permute-start.40 = (bf16[832,384]{1,0:T(8,128)(2,1)}, bf16[832,384]{1,0:T(8,128)(2,1)}, u32[]{:S(2)}, u32[]{:S(2)}) collective-permute-start(bf16[832,384]{1,0:T(8,128)(2,1)} %get-tuple-element.157), channel_id=1, source_target_pairs={{0,4},{2,6},{4,0},{6,2},{1,5},{3,7},{5,1},{7,3},{8,12},{10,14},{12... | collective-permute-start | bytes 1916936 | tf_op jit(solution)/shard_map/ppermute | solution.py:30
  374.7 87.5 %collective-permute-start.17 = (bf16[256,384]{1,0:T(8,128)(2,1)}, bf16[256,384]{1,0:T(8,128)(2,1)}, u32[]{:S(2)}, u32[]{:S(2)}) collective-permute-start(bf16[256,384]{1,0:T(8,128)(2,1)} %broadcast_select_fusion.13), channel_id=1, source_target_pairs={{1,4},{3,6},{4,1},{6,3},{9,12},{11,14},{12,9},{14,11},{17,20},{19,... | collective-permute-start | bytes 589832 | tf_op jit(solution)/shard_map/ppermute | solution.py:251
  379.0 61.2 %collective-permute-start.30 = (f32[256,768]{1,0:T(8,128)}, f32[256,768]{1,0:T(8,128)}, u32[]{:S(2)}, u32[]{:S(2)}) collective-permute-start(f32[256,768]{1,0:T(8,128)} %convolution_add_fusion), channel_id=1, source_target_pairs={{0,1},{1,0},{2,3},{3,2},{4,5},{5,4},{6,7},{7,6},{8,9},{9,8},{10,11... | collective-permute-start | bytes 2359304 | tf_op jit(solution)/shard_map/ppermute | solution.py:30
  425.3 23.1 %all-to-all-start.2 = ((bf16[16,56,384]{2,1,0:T(8,128)(2,1)}), bf16[16,56,384]{2,1,0:T(8,128)(2,1)S(1)}, u32[]{:S(2)}, u32[]{:S(2)}) async-start(bf16[16,56,384]{2,1,0:T(8,128)(2,1)} %maximum_maximum_fusion), calls=%async_computation.2 | async-start | bytes 1376256 | tf_op jit(solution)/shard_map/all_to_all | solution.py:143
  437.2 5.9 %collective-permute-start.37 = (bf16[96,384]{1,0:T(8,128)(2,1)S(1)}, bf16[96,384]{1,0:T(8,128)(2,1)S(1)}, u32[]{:S(2)}, u32[]{:S(2)}) collective-permute-start(bf16[96,384]{1,0:T(8,128)(2,1)S(1)} %get-tuple-element.203), channel_id=1, source_target_pairs={{0,4},{2,6},{4,0},{6,2},{1,5},{3,7},{5,1},{7,3},{8,12},{10,14},{12... | collective-permute-start | bytes 221192 | tf_op jit(solution)/shard_map/ppermute | solution.py:30
  448.9 8.1 %collective-permute-start.41 = (bf16[200,384]{1,0:T(8,128)(2,1)S(1)}, bf16[200,384]{1,0:T(8,128)(2,1)S(1)}, u32[]{:S(2)}, u32[]{:S(2)}) collective-permute-start(bf16[200,384]{1,0:T(8,128)(2,1)S(1)} %concatenate.250), channel_id=1, source_target_pairs={{0,24},{8,16},{16,8},{24,0},{1,25},{9,17},{17,9},{25,1},{2,26},{10... | collective-permute-start | bytes 460808 | tf_op jit(solution)/shard_map/ppermute | solution.py:30
  449.5 7.5 %collective-permute-start.42 = (bf16[200,384]{1,0:T(8,128)(2,1)S(1)}, bf16[200,384]{1,0:T(8,128)(2,1)S(1)}, u32[]{:S(2)}, u32[]{:S(2)}) collective-permute-start(bf16[200,384]{1,0:T(8,128)(2,1)S(1)} %concatenate.250), channel_id=1, source_target_pairs={{0,16},{8,24},{16,0},{24,8},{1,17},{9,25},{17,1},{25,9},{2,18},{10... | collective-permute-start | bytes 460808 | tf_op jit(solution)/shard_map/ppermute | solution.py:30
  451.6 6.3 %collective-permute-start.43 = (bf16[200,384]{1,0:T(8,128)(2,1)S(1)}, bf16[200,384]{1,0:T(8,128)(2,1)S(1)}, u32[]{:S(2)}, u32[]{:S(2)}) collective-permute-start(bf16[200,384]{1,0:T(8,128)(2,1)S(1)} %concatenate.250), channel_id=1, source_target_pairs={{0,8},{8,0},{16,24},{24,16},{1,9},{9,1},{17,25},{25,17},{2,10},{10... | collective-permute-start | bytes 460808 | tf_op jit(solution)/shard_map/ppermute | solution.py:30
  453.1 11.0 %collective-permute-start.31 = (f32[256,384]{1,0:T(8,128)S(1)}, f32[256,384]{1,0:T(8,128)S(1)}, u32[]{:S(2)}, u32[]{:S(2)}) collective-permute-start(f32[256,384]{1,0:T(8,128)S(1)} %slice_select_fusion), channel_id=1, source_target_pairs={{1,4},{3,6},{4,1},{6,3},{9,12},{11,14},{12,9},{14,11},{17,20},{19,... | collective-permute-start | bytes 1179656 | tf_op jit(solution)/shard_map/ppermute | solution.py:251
  458.0 26.6 %collective-permute-start.44 = (bf16[4,200,384]{2,1,0:T(8,128)(2,1)S(1)}, bf16[4,200,384]{2,1,0:T(8,128)(2,1)S(1)}, u32[]{:S(2)}, u32[]{:S(2)}) collective-permute-start(bf16[4,200,384]{2,1,0:T(8,128)(2,1)S(1)} %pad_maximum_fusion.10), channel_id=1, source_target_pairs={{0,96},{32,64},{64,32},{96,0},{1,97},{33,65},{65,33},{97,1},{2,98}... | collective-permute-start | bytes 1843208 | tf_op jit(solution)/shard_map/ppermute | solution.py:30
  459.1 25.5 %collective-permute-start.45 = (bf16[4,200,384]{2,1,0:T(8,128)(2,1)S(1)}, bf16[4,200,384]{2,1,0:T(8,128)(2,1)S(1)}, u32[]{:S(2)}, u32[]{:S(2)}) collective-permute-start(bf16[4,200,384]{2,1,0:T(8,128)(2,1)S(1)} %pad_maximum_fusion.10), channel_id=1, source_target_pairs={{0,64},{32,96},{64,0},{96,32},{1,65},{33,97},{65,1},{97,33},{2,66}... | collective-permute-start | bytes 1843208 | tf_op jit(solution)/shard_map/ppermute | solution.py:30
  460.0 25.3 %collective-permute-start.46 = (bf16[4,200,384]{2,1,0:T(8,128)(2,1)S(1)}, bf16[4,200,384]{2,1,0:T(8,128)(2,1)S(1)}, u32[]{:S(2)}, u32[]{:S(2)}) collective-permute-start(bf16[4,200,384]{2,1,0:T(8,128)(2,1)S(1)} %pad_maximum_fusion.10), channel_id=1, source_target_pairs={{0,32},{32,0},{64,96},{96,64},{1,33},{33,1},{65,97},{97,65},{2,34}... | collective-permute-start | bytes 1843208 | tf_op jit(solution)/shard_map/ppermute | solution.py:30
  (188 other events, 1220.5 us)
Sparse Core Ops, SparseCore 0:
  13.5 86.1 all-gather.3
  103.1 70.7 all-gather.5
  327.7 89.8 all-gather.7
